TPU v7x, 512 devices: a whole 4x8x8 slice. The times are simulated.
512 devices in a mesh: dp: 64 (over x, y, core), tensor: 8 (over z).
Axes of the slice: x: 4, y: 8, z: 8, core: 2. Of those that a mesh axis runs over, the one named last changes fastest.
Arguments:
- queries: bfloat16 [8192, 8192], P('dp', 'tensor'), may hold values from -52 to 52
- keys_in: bfloat16 [8192, 16, 1024], P('dp', 'tensor'), may hold values from -6.5 to 6.5
- values_in: bfloat16 [8192, 16, 1024], P('dp', 'tensor'), may hold values from -4 to 4
- dout: bfloat16 [8192, 8192], P('dp', 'tensor'), may hold values from -4 to 4
- req_tiles: int32 [8192], P('dp'), may hold values from 0 to 8191, as said below
- tile_docs: int32 [8192], P('dp'), may hold values from 0 to 7, as said below
- tile_rows: int32 [8192], P('dp'), may hold values from 0 to 127, as said below
- doc_ends: int32 [512], P('dp'), may hold values from 1 to 128, as said below
Outputs:
- grad_queries: bfloat16 [8192, 8192], P('dp', 'tensor')
- grad_keys: bfloat16 [8192, 16, 1024], P('dp', 'tensor')
- grad_values: bfloat16 [8192, 16, 1024], P('dp', 'tensor')
Inputs may be any that keep to these rules, and one draw needn't show every extreme that they name: `req_tiles`: every tile id appears exactly once over all lists; tile g is held at index g // 128 of dp; one index of dp lists at most 3 tiles of one holder, and each index lists exactly 3 from some holder. `tile_docs`: never falls along one index's list; every document reads 4 or more tiles. `tile_rows`: lies within the rows of the tile's document; the first listed tile of each document is visible from the document's first row. `doc_ends`: rising along one index; the last of each index is 128; document j begins where document j - 1 ends, the first at row 0.
All inputs are finite; a program needn't handle non-finite values.
Results may differ from a plain program's by a relative error of at most 0.013.
Values may be sent and summed in bfloat16 or wider, within the bound.
No kernel may reach another device: no remote copies, remote signals or barrier semaphores. Data moves between devices by JAX's collectives and lax.ppermute only.
A program may use at most 64 MiB of HBM per device.

v0:
```python
import math

import jax
import jax.numpy as jnp
from jax import lax
from jax.sharding import PartitionSpec as P

HD = 128


def group_backward(query_group, key_rows, value_rows, dout_group, visible):
    scale = 1.0 / math.sqrt(HD)
    tok_rows, group, width = query_group.shape
    step_rows = math.gcd(tok_rows, max(1, 512 // group))
    steps = tok_rows // step_rows
    key_count = key_rows.shape[0]

    def one_step(carry, pieces):
        acc_keys, acc_values = carry
        query_part, dout_part, seen_part = pieces
        scores = (
            jnp.einsum("rgd,kd->rgk", query_part, key_rows, preferred_element_type=jnp.float32)
            * scale
        )
        scores = jnp.where(seen_part[:, None, :], scores, -1e30)
        top = jnp.max(scores, axis=-1, keepdims=True)
        expo = jnp.exp(scores - top)
        probs = expo / jnp.sum(expo, axis=-1, keepdims=True)
        probs_low = probs.astype(jnp.bfloat16)
        output = jnp.einsum(
            "rgk,kd->rgd", probs_low, value_rows, preferred_element_type=jnp.float32
        )
        delta = jnp.sum(dout_part.astype(jnp.float32) * output, axis=-1, keepdims=True)
        dprobs = jnp.einsum(
            "rgd,kd->rgk", dout_part, value_rows, preferred_element_type=jnp.float32
        )
        dscores = (probs * (dprobs - delta)).astype(jnp.bfloat16)
        grad_q = (
            jnp.einsum("rgk,kd->rgd", dscores, key_rows, preferred_element_type=jnp.float32) * scale
        )
        acc_keys = (
            acc_keys
            + jnp.einsum("rgk,rgd->kd", dscores, query_part, preferred_element_type=jnp.float32)
            * scale
        )
        acc_values = acc_values + jnp.einsum(
            "rgk,rgd->kd", probs_low, dout_part, preferred_element_type=jnp.float32
        )
        return ((acc_keys, acc_values), grad_q.astype(jnp.bfloat16))

    start = (jnp.zeros((key_count, width), jnp.float32), jnp.zeros((key_count, width), jnp.float32))
    pieces = (
        query_group.reshape(steps, step_rows, group, width),
        dout_group.reshape(steps, step_rows, group, width),
        visible.reshape(steps, step_rows, key_count),
    )
    (acc_keys, acc_values), grad_q = lax.scan(one_step, start, pieces)
    return (grad_q.reshape(tok_rows, group * width), acc_keys, acc_values)


def per_device(queries, keys_in, values_in, dout, req_tiles, tile_docs, tile_rows, doc_ends):
    dp_count = lax.axis_size("dp")
    slots = req_tiles.shape[0]
    capacity = slots // dp_count + 1
    tile_len = keys_in.shape[1] * lax.axis_size("tensor")
    my_index = lax.axis_index("dp")
    every_list = lax.all_gather(req_tiles, "dp", axis=0, tiled=True).reshape(dp_count, slots)
    holder = every_list // slots
    local_tile = every_list % slots
    mine = holder == my_index
    mine_count = mine.astype(jnp.int32)
    earlier = jnp.cumsum(mine_count, axis=1) - mine_count
    picked = mine[:, None, :] & (
        earlier[:, None, :] == jnp.arange(capacity, dtype=jnp.int32)[None, :, None]
    )
    local_for = jnp.sum(jnp.where(picked, local_tile[:, None, :], 0), axis=-1)
    filled = jnp.any(picked, axis=-1)
    send_keys = jnp.where(filled[:, :, None, None], keys_in[local_for], jnp.zeros((), jnp.bfloat16))
    send_values = jnp.where(
        filled[:, :, None, None], values_in[local_for], jnp.zeros((), jnp.bfloat16)
    )
    recv_keys, recv_values = (
        lax.all_to_all(
            lax.all_to_all(send_keys, "tensor", split_axis=3, concat_axis=2, tiled=True),
            "dp",
            split_axis=0,
            concat_axis=0,
            tiled=True,
        ),
        lax.all_to_all(
            lax.all_to_all(send_values, "tensor", split_axis=3, concat_axis=2, tiled=True),
            "dp",
            split_axis=0,
            concat_axis=0,
            tiled=True,
        ),
    )
    kv_width = recv_keys.shape[-1]
    own_holder = req_tiles // slots
    slot_index = jnp.arange(slots, dtype=jnp.int32)
    same_before = (own_holder[:, None] == own_holder[None, :]) & (
        slot_index[None, :] < slot_index[:, None]
    )
    own_rank = jnp.sum(same_before.astype(jnp.int32), axis=1)
    place = own_holder * capacity + own_rank
    key_rows = recv_keys.reshape(dp_count * capacity, tile_len, kv_width)[place].reshape(
        slots * tile_len, kv_width
    )
    value_rows = recv_values.reshape(dp_count * capacity, tile_len, kv_width)[place].reshape(
        slots * tile_len, kv_width
    )
    doc_count = doc_ends.shape[0]
    slot_ends = jnp.sum(
        jnp.where(
            tile_docs[:, None] == jnp.arange(doc_count, dtype=jnp.int32)[None, :],
            doc_ends[None, :],
            0,
        ),
        axis=1,
    )
    tok_rows = queries.shape[0]
    text_row = jnp.arange(tok_rows, dtype=jnp.int32)[:, None]
    seen = (text_row >= tile_rows[None, :]) & (text_row < slot_ends[None, :])
    visible = jnp.broadcast_to(seen[:, :, None], (tok_rows, slots, tile_len)).reshape(
        tok_rows, slots * tile_len
    )
    kv_local = kv_width // HD
    group = queries.shape[1] // HD // kv_local
    grads_q, grads_k, grads_v = ([], [], [])
    grad_q, grad_k, grad_v = group_backward(
        queries.reshape(tok_rows, group, HD),
        key_rows,
        value_rows,
        dout.reshape(tok_rows, group, HD),
        visible,
    )
    grads_q.append(grad_q)
    grads_k.append(grad_k.astype(jnp.bfloat16))
    grads_v.append(grad_v.astype(jnp.bfloat16))
    grad_queries = grads_q[0]
    tile_grad_keys = grads_k[0].reshape(slots, tile_len, kv_width)
    tile_grad_values = grads_v[0].reshape(slots, tile_len, kv_width)
    back_keys = (
        jnp.zeros((dp_count * capacity, tile_len, kv_width), jnp.bfloat16)
        .at[place]
        .set(tile_grad_keys)
    )
    back_values = (
        jnp.zeros((dp_count * capacity, tile_len, kv_width), jnp.bfloat16)
        .at[place]
        .set(tile_grad_values)
    )
    back_keys = back_keys.reshape(dp_count, capacity, tile_len, kv_width)
    back_values = back_values.reshape(dp_count, capacity, tile_len, kv_width)
    home_keys, home_values = (
        lax.all_to_all(
            lax.all_to_all(back_keys, "dp", split_axis=0, concat_axis=0, tiled=True),
            "tensor",
            split_axis=2,
            concat_axis=3,
            tiled=True,
        ),
        lax.all_to_all(
            lax.all_to_all(back_values, "dp", split_axis=0, concat_axis=0, tiled=True),
            "tensor",
            split_axis=2,
            concat_axis=3,
            tiled=True,
        ),
    )
    target = jnp.where(filled, local_for, slots).reshape(-1)
    row_part = home_keys.shape[2]
    full_width = home_keys.shape[3]
    grad_keys = (
        jnp.zeros(keys_in.shape, jnp.bfloat16)
        .at[target]
        .set(home_keys.reshape(dp_count * capacity, row_part, full_width), mode="drop")
    )
    grad_values = (
        jnp.zeros(values_in.shape, jnp.bfloat16)
        .at[target]
        .set(home_values.reshape(dp_count * capacity, row_part, full_width), mode="drop")
    )
    return (grad_queries, grad_keys, grad_values)


def solution(mesh):
    return jax.shard_map(
        per_device,
        mesh=mesh,
        in_specs=(
            P("dp", "tensor"),
            P("dp", "tensor", None),
            P("dp", "tensor", None),
            P("dp", "tensor"),
            P("dp"),
            P("dp"),
            P("dp"),
            P("dp"),
        ),
        out_specs=(P("dp", "tensor"), P("dp", "tensor", None), P("dp", "tensor", None)),
        check_vma=False,
    )
```

profile of v0, /device:TPU:1, one launch (start us, length us, event | category | flops | bytes accessed | tf_op | source)
XLA Modules:
  0.0 366.1 jit_solution(5389444882111337532)
XLA Ops:
  0.6 39.8 %all-gather = s32[64,1,128]{2,1,0:T(1,128)S(1)} all-gather(s32[1,1,128]{2,1,0:T(1,128)} %bitcast.164), channel_id=1, replica_groups=mesh['dp'=64,'tensor'=8] {'dp'}, dimensions={0}, use_global_device_ids=true | all-gather | bytes 33280 | tf_op jit(solution)/shard_map/all_gather | solution.py:67
  44.2 3.2 gather_fusion
  54.1 8.0 %all-to-all-start.2 = ((bf16[8,2,24576]{2,1,0:T(2,128)(2,1)}), bf16[8,2,24576]{2,1,0:T(2,128)(2,1)S(1)}, u32[]{:S(2)}, u32[]{:S(2)}) async-start(bf16[8,2,24576]{2,1,0:T(2,128)(2,1)} %reshape.324), calls=%async_computation.2 | async-start | bytes 1572864 | tf_op jit(solution)/shard_map/all_to_all | solution.py:91
  62.1 4.3 %copy.89 = bf16[64,3,2,1024]{0,2,1,3:T(2,128)(2,1)S(1)} copy(bf16[64,3,2,1024]{3,2,1,0:T(2,128)(2,1)} %get-tuple-element.162) | data formatting | bytes 1572864 | tf_op jit(solution)/shard_map/jit(_where)/select_n | solution.py:78
  68.4 17.4 %all-to-all-done.2 = bf16[8,2,24576]{2,1,0:T(2,128)(2,1)S(1)} async-done(((bf16[8,2,24576]{2,1,0:T(2,128)(2,1)}), bf16[8,2,24576]{2,1,0:T(2,128)(2,1)S(1)}, u32[]{:S(2)}, u32[]{:S(2)}) %all-to-all-start.2) | async-done | bytes 786464 | tf_op jit(solution)/shard_map/all_to_all | solution.py:91
  86.7 3.5 all-to-all-start
  92.4 3.2 copy.110
  98.2 15.6 %all-to-all-done = bf16[8,2,24576]{2,1,0:T(2,128)(2,1)S(1)} async-done(((bf16[8,2,24576]{2,1,0:T(2,128)(2,1)}), bf16[8,2,24576]{2,1,0:T(2,128)(2,1)S(1)}, u32[]{:S(2)}, u32[]{:S(2)}) %all-to-all-start) | async-done | bytes 786464 | tf_op jit(solution)/shard_map/all_to_all | solution.py:84
  113.8 7.2 %all-to-all-start.3 = ((bf16[64,3,16,128]{3,2,1,0:T(8,128)(2,1)}), bf16[64,3,16,128]{3,2,1,0:T(8,128)(2,1)}, u32[]{:S(2)}, u32[]{:S(2)}) async-start(bf16[64,3,16,128]{3,2,1,0:T(8,128)(2,1)} %copy.96), calls=%async_computation.3 | async-start | bytes 1572864 | tf_op jit(solution)/shard_map/all_to_all | solution.py:90
  125.5 18.4 %all-to-all-done.3 = bf16[64,3,16,128]{3,2,1,0:T(8,128)(2,1)} async-done(((bf16[64,3,16,128]{3,2,1,0:T(8,128)(2,1)}), bf16[64,3,16,128]{3,2,1,0:T(8,128)(2,1)}, u32[]{:S(2)}, u32[]{:S(2)}) %all-to-all-start.3) | async-done | bytes 786464 | tf_op jit(solution)/shard_map/all_to_all | solution.py:90
  143.9 6.2 %all-to-all-start.1 = ((bf16[64,3,16,128]{3,2,1,0:T(8,128)(2,1)}), bf16[64,3,16,128]{3,2,1,0:T(8,128)(2,1)S(1)}, u32[]{:S(2)}, u32[]{:S(2)}) async-start(bf16[64,3,16,128]{3,2,1,0:T(8,128)(2,1)} %copy.92), calls=%async_computation.1 | async-start | bytes 1572864 | tf_op jit(solution)/shard_map/all_to_all | solution.py:83
  156.2 16.9 %all-to-all-done.1 = bf16[64,3,16,128]{3,2,1,0:T(8,128)(2,1)S(1)} async-done(((bf16[64,3,16,128]{3,2,1,0:T(8,128)(2,1)}), bf16[64,3,16,128]{3,2,1,0:T(8,128)(2,1)S(1)}, u32[]{:S(2)}, u32[]{:S(2)}) %all-to-all-start.1) | async-done | bytes 786464 | tf_op jit(solution)/shard_map/all_to_all | solution.py:83
  174.5 40.6 %while.15 = (s32[]{:T(128)}, f32[2048,128]{1,0:T(8,128)}, f32[2048,128]{1,0:T(8,128)}, bf16[2,64,8,128]{3,2,1,0:T(8,128)(2,1)}, pred[2,64,2048]{2,1,0:T(8,128)(4...) while((s32[]{:T(128)}, f32[2048,128]{1,0:T(8,128)}, ...), condition=%wide.region_9.10_spmd.clone, body=%wide.region_5.9_spmd.clone.sunk | while | flops 1622738432 | bytes 59972856 | solution.py:57
  175.5 4.7 %fusion.92 = (f32[64,8]{1,0:T(8,128)S(1)}, f32[64,8,2048]{2,1,0:T(8,128)}) fusion(pred[64,2048]{1,0:T(8,128)(4,1)S(1)} %dynamic-slice_bitcast_fusion.2, bf16[2048,128]{1,0:T(8,128)(2,1)} %get-tuple-element.252, bf16[2,64,8,128]{3,2,1,0:T(8,128)(2,1)} %get-tuple-element.251, s32[]{:T(128)} %get-tuple-element.235), kind=kOutput, calls=%fused_computation.90.clone.1 | convolution fusion | flops 272631808 | bytes 4983296 | tf_op jit(solution)/shard_map/while/body/eval_jaxpr/sub | solution.py:27
  180.2 2.9 fusion.93
  186.0 3.6 fusion.95
  195.0 4.7 %fusion.92 = (f32[64,8]{1,0:T(8,128)S(1)}, f32[64,8,2048]{2,1,0:T(8,128)}) fusion(pred[64,2048]{1,0:T(8,128)(4,1)S(1)} %dynamic-slice_bitcast_fusion.2, bf16[2048,128]{1,0:T(8,128)(2,1)} %get-tuple-element.252, bf16[2,64,8,128]{3,2,1,0:T(8,128)(2,1)} %get-tuple-element.251, s32[]{:T(128)} %get-tuple-element.235), kind=kOutput, calls=%fused_computation.90.clone.1 | convolution fusion | flops 272631808 | bytes 4983296 | tf_op jit(solution)/shard_map/while/body/eval_jaxpr/sub | solution.py:27
  199.7 2.9 fusion.93
  205.5 3.9 %fusion.95 = f32[2048,128]{1,0:T(8,128)} fusion(bf16[64,8,2048]{2,1,0:T(8,128)(2,1)} %multiply_convert_fusion.2, f32[2048,128]{1,0:T(8,128)} %get-tuple-element.236, pred[]{:T(512)S(6)} %compare.24, bf16[2,64,8,128]{3,2,1,0:T(8,128)(2,1)} %get-tuple-element.251, s32[]{:T(128)} %get-tuple-element.235), kind=kOutput, calls=%fused_computation.16.clone.1 | convolution fusion | flops 269221888 | bytes 4325889 | tf_op jit(solution)/shard_map/while/body/eval_jaxpr/rgk,rgd->kd/dot_general | solution.py:43
  212.0 3.2 fusion.96
  217.5 12.4 %scatter_fusion.2 = bf16[192,16,128]{2,1,0:T(8,128)(2,1)} fusion(bf16[192,16,128]{2,1,0:T(8,128)(2,1)} %broadcast.228.clone.1, s32[128]{0:T(128)S(1)} %compare_select_fusion.2, bf16[128,16,128]{2,1,0:T(8,128)(2,1)S(1)} %bitcast.155), kind=kCustom, calls=%fused_computation.6 | custom fusion | bytes 1573376 | tf_op jit(solution)/shard_map/scatter | solution.py:151
  229.9 6.2 %all-to-all-start.6 = ((bf16[64,3,16,128]{3,2,1,0:T(8,128)(2,1)}), bf16[64,3,16,128]{3,2,1,0:T(8,128)(2,1)S(1)}, u32[]{:S(2)}, u32[]{:S(2)}) async-start(bf16[64,3,16,128]{3,2,1,0:T(8,128)(2,1)} %bitcast.24), calls=%async_computation.6 | async-start | bytes 1572864 | tf_op jit(solution)/shard_map/all_to_all | solution.py:164
  237.2 12.4 %scatter_fusion = bf16[192,16,128]{2,1,0:T(8,128)(2,1)} fusion(bf16[192,16,128]{2,1,0:T(8,128)(2,1)} %broadcast.228.clone, s32[128]{0:T(128)S(1)} %compare_select_fusion.2, bf16[128,16,128]{2,1,0:T(8,128)(2,1)S(1)} %bitcast.154), kind=kCustom, calls=%fused_computation.4 | custom fusion | bytes 1573376 | tf_op jit(solution)/shard_map/scatter | solution.py:146
  249.6 9.6 %all-to-all-done.6 = bf16[64,3,16,128]{3,2,1,0:T(8,128)(2,1)S(1)} async-done(((bf16[64,3,16,128]{3,2,1,0:T(8,128)(2,1)}), bf16[64,3,16,128]{3,2,1,0:T(8,128)(2,1)S(1)}, u32[]{:S(2)}, u32[]{:S(2)}) %all-to-all-start.6) | async-done | bytes 786464 | tf_op jit(solution)/shard_map/all_to_all | solution.py:164
  259.1 6.2 %all-to-all-start.4 = ((bf16[64,3,16,128]{3,2,1,0:T(8,128)(2,1)}), bf16[64,3,16,128]{3,2,1,0:T(8,128)(2,1)S(1)}, u32[]{:S(2)}, u32[]{:S(2)}) async-start(bf16[64,3,16,128]{3,2,1,0:T(8,128)(2,1)} %bitcast.19), calls=%async_computation.4 | async-start | bytes 1572864 | tf_op jit(solution)/shard_map/all_to_all | solution.py:157
  266.5 21.9 %all-to-all-done.4 = bf16[64,3,16,128]{3,2,1,0:T(8,128)(2,1)S(1)} async-done(((bf16[64,3,16,128]{3,2,1,0:T(8,128)(2,1)}), bf16[64,3,16,128]{3,2,1,0:T(8,128)(2,1)S(1)}, u32[]{:S(2)}, u32[]{:S(2)}) %all-to-all-start.4) | async-done | bytes 786464 | tf_op jit(solution)/shard_map/all_to_all | solution.py:157
  288.3 3.5 all-to-all-start.7
  292.9 22.5 %all-to-all-done.7 = bf16[64,3,16,128]{3,0,1,2:T(8,128)(2,1)S(1)} async-done(((bf16[64,3,16,128]{3,0,1,2:T(8,128)(2,1)}), bf16[64,3,16,128]{3,0,1,2:T(8,128)(2,1)S(1)}, u32[]{:S(2)}, u32[]{:S(2)}) %all-to-all-start.7) | async-done | bytes 786464 | tf_op jit(solution)/shard_map/all_to_all | solution.py:163
  315.4 3.8 %all-to-all-start.5 = ((bf16[64,3,16,128]{3,0,1,2:T(8,128)(2,1)}), bf16[64,3,16,128]{3,0,1,2:T(8,128)(2,1)S(1)}, u32[]{:S(2)}, u32[]{:S(2)}) async-start(bf16[64,3,16,128]{3,0,1,2:T(8,128)(2,1)} %copy.99), calls=%async_computation.5 | async-start | bytes 1572864 | tf_op jit(solution)/shard_map/all_to_all | solution.py:156
  321.8 18.8 %all-to-all-done.5 = bf16[64,3,16,128]{3,0,1,2:T(8,128)(2,1)S(1)} async-done(((bf16[64,3,16,128]{3,0,1,2:T(8,128)(2,1)}), bf16[64,3,16,128]{3,0,1,2:T(8,128)(2,1)S(1)}, u32[]{:S(2)}, u32[]{:S(2)}) %all-to-all-start.5) | async-done | bytes 786464 | tf_op jit(solution)/shard_map/all_to_all | solution.py:156
  342.5 6.3 %scatter_fusion.3 = bf16[128,2,1024]{2,1,0:T(2,128)(2,1)S(1)} fusion(bf16[128,2,1024]{2,1,0:T(2,128)(2,1)S(1)} %broadcast.224.clone.1, s32[192]{0:T(256)S(1)} %bitcast.162, bf16[192,2,1024]{2,1,0:T(2,128)(2,1)S(1)} %copy-done.6), kind=kCustom, calls=%fused_computation.7 | custom fusion | bytes 2360064 | tf_op jit(solution)/shard_map/scatter | solution.py:182
  349.1 16.2 %scatter_fusion.1 = bf16[128,2,1024]{2,1,0:T(2,128)(2,1)S(1)} fusion(bf16[128,2,1024]{2,1,0:T(2,128)(2,1)S(1)} %broadcast.224.clone, s32[192]{0:T(256)S(1)} %bitcast.163, bf16[192,2,1024]{2,1,0:T(2,128)(2,1)} %reshape.320), kind=kCustom, calls=%fused_computation.5 | custom fusion | bytes 2360064 | tf_op jit(solution)/shard_map/scatter | solution.py:177
  (112 shorter events, 55.5 us)
Async XLA Ops:
  0.6 41.4 %copy-start = (bf16[128,2,1024]{2,1,0:T(2,128)(2,1)S(1)}, bf16[128,2,1024]{2,1,0:T(2,128)(2,1)}, u32[]{:S(2)}) copy-start(bf16[128,2,1024]{2,1,0:T(2,128)(2,1)} %param.12) | copy-start | bytes 1572868
  41.0 6.6 %copy-start.15 = (pred[64,3]{0,1:T(4,128)(4,1)}, pred[64,3]{0,1:T(4,128)(4,1)S(1)}, u32[]{:S(2)}) copy-start(pred[64,3]{0,1:T(4,128)(4,1)S(1)} %fusion.45) | copy-start | bytes 580
  54.1 31.6 %all-to-all-start.2 = ((bf16[8,2,24576]{2,1,0:T(2,128)(2,1)}), bf16[8,2,24576]{2,1,0:T(2,128)(2,1)S(1)}, u32[]{:S(2)}, u32[]{:S(2)}) async-start(bf16[8,2,24576]{2,1,0:T(2,128)(2,1)} %reshape.324), calls=%async_computation.2 | async-start | bytes 1572864 | tf_op jit(solution)/shard_map/all_to_all | solution.py:91
  85.7 0.9 copy-start.5
  86.7 27.1 %all-to-all-start = ((bf16[8,2,24576]{2,1,0:T(2,128)(2,1)}), bf16[8,2,24576]{2,1,0:T(2,128)(2,1)S(1)}, u32[]{:S(2)}, u32[]{:S(2)}) async-start(bf16[8,2,24576]{2,1,0:T(2,128)(2,1)} %reshape.322), calls=%async_computation | async-start | bytes 1572864 | tf_op jit(solution)/shard_map/all_to_all | solution.py:84
  113.8 30.1 %all-to-all-start.3 = ((bf16[64,3,16,128]{3,2,1,0:T(8,128)(2,1)}), bf16[64,3,16,128]{3,2,1,0:T(8,128)(2,1)}, u32[]{:S(2)}, u32[]{:S(2)}) async-start(bf16[64,3,16,128]{3,2,1,0:T(8,128)(2,1)} %copy.96), calls=%async_computation.3 | async-start | bytes 1572864 | tf_op jit(solution)/shard_map/all_to_all | solution.py:90
  121.0 29.2 %copy-start.19 = (s32[8]{0:T(128)S(1)}, s32[8]{0:T(128)}, u32[]{:S(2)}) copy-start(s32[8]{0:T(128)} %param.17) | copy-start | bytes 100
  121.0 29.2 %copy-start.20 = (s32[128]{0:T(128)S(1)}, s32[128]{0:T(128)}, u32[]{:S(2)}) copy-start(s32[128]{0:T(128)} %param.15) | copy-start | bytes 1540
  121.0 29.2 %copy-start.18 = (s32[128]{0:T(128)S(1)}, s32[128]{0:T(128)}, u32[]{:S(2)}) copy-start(s32[128]{0:T(128)} %param.16) | copy-start | bytes 1540
  122.0 31.2 %copy-start.8 = (bf16[128,1024]{1,0:T(8,128)(2,1)S(1)}, bf16[128,1024]{1,0:T(8,128)(2,1)}, u32[]{:S(2)}) copy-start(bf16[128,1024]{1,0:T(8,128)(2,1)} %param.10) | copy-start | bytes 786436
  122.1 32.0 %copy-start.9 = (bf16[128,1024]{1,0:T(8,128)(2,1)S(1)}, bf16[128,1024]{1,0:T(8,128)(2,1)}, u32[]{:S(2)}) copy-start(bf16[128,1024]{1,0:T(8,128)(2,1)} %param.13) | copy-start | bytes 786436
  122.1 32.0 %copy-start.17 = (s32[128]{0:T(128)S(1)}, s32[128]{0:T(128)}, u32[]{:S(2)}) copy-start(s32[128]{0:T(128)} %param.14) | copy-start | bytes 1540
  143.9 29.2 %all-to-all-start.1 = ((bf16[64,3,16,128]{3,2,1,0:T(8,128)(2,1)}), bf16[64,3,16,128]{3,2,1,0:T(8,128)(2,1)S(1)}, u32[]{:S(2)}, u32[]{:S(2)}) async-start(bf16[64,3,16,128]{3,2,1,0:T(8,128)(2,1)} %copy.92), calls=%async_computation.1 | async-start | bytes 1572864 | tf_op jit(solution)/shard_map/all_to_all | solution.py:83
  180.2 3.7 %copy-start.1 = (f32[64,8,2048]{2,1,0:T(8,128)S(1)}, f32[64,8,2048]{2,1,0:T(8,128)}, u32[]{:S(2)}) copy-start(f32[64,8,2048]{2,1,0:T(8,128)} %get-tuple-element.222) | copy-start | bytes 12582916 | tf_op jit(solution)/shard_map/while
  186.0 3.6 copy-start.2
  186.0 3.6 copy-start.10
  191.4 0.7 copy-start.11
  199.7 3.7 %copy-start.1 = (f32[64,8,2048]{2,1,0:T(8,128)S(1)}, f32[64,8,2048]{2,1,0:T(8,128)}, u32[]{:S(2)}) copy-start(f32[64,8,2048]{2,1,0:T(8,128)} %get-tuple-element.222) | copy-start | bytes 12582916 | tf_op jit(solution)/shard_map/while
  205.5 3.9 %copy-start.2 = (bf16[64,8,2048]{2,1,0:T(8,128)(2,1)S(1)}, bf16[64,8,2048]{2,1,0:T(8,128)(2,1)}, u32[]{:S(2)}) copy-start(bf16[64,8,2048]{2,1,0:T(8,128)(2,1)} %multiply_convert_fusion.2) | copy-start | bytes 6291460 | tf_op jit(solution)/shard_map/while
  205.5 3.9 %copy-start.10 = (bf16[2,64,8,128]{3,2,1,0:T(8,128)(2,1)S(1)}, bf16[2,64,8,128]{3,2,1,0:T(8,128)(2,1)}, u32[]{:S(2)}) copy-start(bf16[2,64,8,128]{3,2,1,0:T(8,128)(2,1)} %get-tuple-element.238) | copy-start | bytes 786436 | tf_op jit(solution)/shard_map/while
  211.3 0.7 copy-start.11
  215.1 21.0 %copy-start.7 = (f32[2048,128]{1,0:T(8,128)S(1)}, f32[2048,128]{1,0:T(8,128)}, u32[]{:S(2)}) copy-start(f32[2048,128]{1,0:T(8,128)} %get-tuple-element.53) | copy-start | bytes 3145732
  229.9 29.2 %all-to-all-start.6 = ((bf16[64,3,16,128]{3,2,1,0:T(8,128)(2,1)}), bf16[64,3,16,128]{3,2,1,0:T(8,128)(2,1)S(1)}, u32[]{:S(2)}, u32[]{:S(2)}) async-start(bf16[64,3,16,128]{3,2,1,0:T(8,128)(2,1)} %bitcast.24), calls=%async_computation.6 | async-start | bytes 1572864 | tf_op jit(solution)/shard_map/all_to_all | solution.py:164
  249.6 69.6 %copy-start.14 = (s32[64,3]{0,1:T(4,128)S(1)}, s32[64,3]{0,1:T(4,128)}, u32[]{:S(2)}) copy-start(s32[64,3]{0,1:T(4,128)} %copy-done.13) | copy-start | bytes 2308
  249.6 69.6 %copy-start.16 = (pred[64,3]{0,1:T(4,128)(4,1)S(1)}, pred[64,3]{0,1:T(4,128)(4,1)}, u32[]{:S(2)}) copy-start(pred[64,3]{0,1:T(4,128)(4,1)} %copy-done.15) | copy-start | bytes 580
  249.6 69.9 %copy-start.12 = (bf16[2,64,8,128]{3,2,1,0:T(8,128)(2,1)S(1)}, bf16[2,64,8,128]{3,2,1,0:T(8,128)(2,1)}, u32[]{:S(2)}) copy-start(bf16[2,64,8,128]{3,2,1,0:T(8,128)(2,1)} %get-tuple-element.52) | copy-start | bytes 786436
  259.1 29.2 %all-to-all-start.4 = ((bf16[64,3,16,128]{3,2,1,0:T(8,128)(2,1)}), bf16[64,3,16,128]{3,2,1,0:T(8,128)(2,1)S(1)}, u32[]{:S(2)}, u32[]{:S(2)}) async-start(bf16[64,3,16,128]{3,2,1,0:T(8,128)(2,1)} %bitcast.19), calls=%async_computation.4 | async-start | bytes 1572864 | tf_op jit(solution)/shard_map/all_to_all | solution.py:157
  288.3 27.1 %all-to-all-start.7 = ((bf16[64,3,16,128]{3,0,1,2:T(8,128)(2,1)}), bf16[64,3,16,128]{3,0,1,2:T(8,128)(2,1)S(1)}, u32[]{:S(2)}, u32[]{:S(2)}) async-start(bf16[64,3,16,128]{3,0,1,2:T(8,128)(2,1)} %copy.103), calls=%async_computation.7 | async-start | bytes 1572864 | tf_op jit(solution)/shard_map/all_to_all | solution.py:163
  315.4 25.2 %all-to-all-start.5 = ((bf16[64,3,16,128]{3,0,1,2:T(8,128)(2,1)}), bf16[64,3,16,128]{3,0,1,2:T(8,128)(2,1)S(1)}, u32[]{:S(2)}, u32[]{:S(2)}) async-start(bf16[64,3,16,128]{3,0,1,2:T(8,128)(2,1)} %copy.99), calls=%async_computation.5 | async-start | bytes 1572864 | tf_op jit(solution)/shard_map/all_to_all | solution.py:156
  321.8 20.6 %copy-start.6 = (bf16[192,2,1024]{2,1,0:T(2,128)(2,1)S(1)}, bf16[192,2,1024]{2,1,0:T(2,128)(2,1)}, u32[]{:S(2)}) copy-start(bf16[192,2,1024]{2,1,0:T(2,128)(2,1)} %reshape.321) | copy-start | bytes 2359300
  348.9 16.5 %copy-start.4 = (bf16[128,2,1024]{2,1,0:T(2,128)(2,1)}, bf16[128,2,1024]{2,1,0:T(2,128)(2,1)S(1)}, u32[]{:S(2)}) copy-start(bf16[128,2,1024]{2,1,0:T(2,128)(2,1)S(1)} %scatter_fusion.3) | copy-start | bytes 1572868
  365.3 0.8 copy-start.3
  (1 other events, 0.6 us)
where the time goes:
time: 368 us; the launch traced here: 366 us
  waiting for transfers between devices  141 us (38%)
  local copies, waits for them, and re-layouts  97.6 us (27%)
  starting transfers between devices  44.6 us (12%)
  blocking collectives  39.8 us (11%)
  matrix products  31.4 us (9%)
  other arithmetic  10.6 us (3%)
    all_gather x1, blocking collectives, per_device(): lax.all_gather(req_tiles, 'dp', axis=0, tiled=True).reshape(dp_count, slots)  39.8 us
    all_to_all x1, waiting for transfers between devices, per_device(): lax.all_to_all(lax.all_to_all(back_values, 'dp', split_axis=0, concat_axi...  22.5 us
    all_to_all x1, waiting for transfers between devices, per_device(): lax.all_to_all(back_keys, 'dp', split_axis=0, concat_axis=0, tiled=True)  21.9 us
    all_to_all x1, waiting for transfers between devices, per_device(): lax.all_to_all(lax.all_to_all(back_keys, 'dp', split_axis=0, concat_axis=...  18.8 us
    all_to_all x1, waiting for transfers between devices, per_device(): lax.all_to_all(lax.all_to_all(send_values, 'tensor', split_axis=3, concat...  18.4 us
    all_to_all x1, waiting for transfers between devices, per_device(): lax.all_to_all(send_values, 'tensor', split_axis=3, concat_axis=2, tiled=...  17.4 us
    all_to_all x1, waiting for transfers between devices, per_device(): lax.all_to_all(lax.all_to_all(send_keys, 'tensor', split_axis=3, concat_a...  16.9 us
    scatter x1, local copies, waits for them, and re-layouts, per_device(): grad_keys = jnp.zeros(keys_in.shape, jnp.bfloat16).at[target].set(home_ke...  16.2 us
  transfers between devices with their start and end apart: 8, of which 8 were waited for; matrix products, arithmetic and copies ran while one was open for 12% of the time, Pallas kernels for 0%

commit v1 on v0

v1 whole, which is shorter than its diff:
```python
import math

import jax
import jax.numpy as jnp
from jax import lax
from jax.experimental import pallas as pl
from jax.experimental.pallas import tpu as pltpu
from jax.sharding import PartitionSpec as P

HD = 128
BF16 = jnp.bfloat16
F32 = jnp.float32
HIDDEN = -1e30
VMEM_LIMIT = 48 * 1024 * 1024


def pick_tiles(wanted_ref, keys_ref, values_ref, send_ref):
    readers, _, capacity = wanted_ref.shape
    heads = keys_ref.shape[2] // HD

    def one_reader(reader, carry):
        for rank in range(capacity):
            tile = jnp.maximum(wanted_ref[reader, 0, rank], 0)
            for head in range(heads):
                cols = slice(head * HD, (head + 1) * HD)
                send_ref[reader * heads + head, rank] = keys_ref[tile, :, cols]
                send_ref[reader * heads + head, capacity + rank] = values_ref[tile, :, cols]
        return carry

    lax.fori_loop(0, readers, one_reader, 0)


def place_tiles(wanted_ref, home_ref, grad_keys_ref, grad_values_ref):
    readers, _, capacity = wanted_ref.shape
    heads = grad_keys_ref.shape[2] // HD

    def one_reader(reader, carry):
        for rank in range(capacity):
            tile = wanted_ref[reader, 0, rank]

            @pl.when(tile >= 0)
            def _():
                for head in range(heads):
                    cols = slice(head * HD, (head + 1) * HD)
                    grad_keys_ref[tile, :, cols] = home_ref[reader * heads + head, rank]
                    grad_values_ref[tile, :, cols] = home_ref[
                        reader * heads + head, capacity + rank
                    ]

        return carry

    lax.fori_loop(0, readers, one_reader, 0)


def attend_backward(
    holder_ref,
    rank_ref,
    bias_ref,
    recv_ref,
    queries_ref,
    dout_ref,
    back_ref,
    grad_queries_ref,
    key_scr,
    value_scr,
    bias_scr,
    query_scr,
    dout_scr,
    score_scr,
    dprob_scr,
    low_scr,
    dscore_scr,
):
    scale = 1.0 / math.sqrt(HD)
    slots, rows = bias_ref.shape
    capacity = recv_ref.shape[1] // 2
    tile_len = key_scr.shape[0] // slots
    pieces = tile_len // recv_ref.shape[2]
    group = queries_ref.shape[1] // HD
    key_count = slots * tile_len
    chunk = 256
    chunks = key_count // chunk
    pair = 2 * rows
    contract_last = (((1,), (1,)), ((), ()))
    contract_first = (((0,), (0,)), ((), ()))

    def gather_slot(slot, carry):
        source = pl.ds(holder_ref[slot] * pieces, pieces)
        rank = rank_ref[slot]
        target = pl.ds(pl.multiple_of(slot * tile_len, tile_len), tile_len)
        key_scr[target, :] = recv_ref[source, rank].reshape(tile_len, HD)
        value_scr[target, :] = recv_ref[source, capacity + rank].reshape(tile_len, HD)
        bias_scr[target, :] = jnp.broadcast_to(bias_ref[pl.ds(slot, 1), :], (tile_len, rows))
        return carry

    lax.fori_loop(0, slots, gather_slot, 0)

    for head in range(group):
        cols = slice(head * HD, (head + 1) * HD)
        query_scr[head * rows : (head + 1) * rows, :] = queries_ref[:, cols]
        dout_scr[head * rows : (head + 1) * rows, :] = dout_ref[:, cols]

    def one_pair(index, carry):
        start = pl.multiple_of(index * pair, pair)
        query_pair = query_scr[pl.ds(start, pair), :]
        dout_pair = dout_scr[pl.ds(start, pair), :]

        def keys_of(step):
            return pl.ds(pl.multiple_of(step * chunk, chunk), chunk)

        def score_step(step, top):
            where = keys_of(step)
            bias = bias_scr[where, :]
            score = (
                lax.dot_general(
                    key_scr[where, :], query_pair, contract_last, preferred_element_type=F32
                )
                * scale
            )
            score = score + jnp.concatenate([bias, bias], axis=1)
            score_scr[where, :] = score
            return jnp.maximum(top, jnp.max(score, axis=0, keepdims=True))

        top = lax.fori_loop(0, chunks, score_step, jnp.full((1, pair), HIDDEN, F32))

        def exp_step(step, total):
            where = keys_of(step)
            expo = jnp.exp(score_scr[where, :] - top)
            score_scr[where, :] = expo
            return total + jnp.sum(expo, axis=0, keepdims=True)

        total = lax.fori_loop(0, chunks, exp_step, jnp.zeros((1, pair), F32))
        inverse = 1.0 / total

        def prob_step(step, delta):
            where = keys_of(step)
            prob = score_scr[where, :] * inverse
            low = prob.astype(BF16)
            dprob = lax.dot_general(
                value_scr[where, :], dout_pair, contract_last, preferred_element_type=F32
            )
            score_scr[where, :] = prob
            dprob_scr[where, :] = dprob
            low_scr[where, pl.ds(start, pair)] = low
            return delta + jnp.sum(low.astype(F32) * dprob, axis=0, keepdims=True)

        delta = lax.fori_loop(0, chunks, prob_step, jnp.zeros((1, pair), F32))

        def dscore_step(step, grad):
            where = keys_of(step)
            dscore = (score_scr[where, :] * (dprob_scr[where, :] - delta)).astype(BF16)
            dscore_scr[where, pl.ds(start, pair)] = dscore
            return grad + lax.dot_general(
                dscore, key_scr[where, :], contract_first, preferred_element_type=F32
            )

        grad = lax.fori_loop(0, chunks, dscore_step, jnp.zeros((pair, HD), F32)) * scale
        query_scr_out = grad.astype(BF16)
        grad_queries_ref[:, pl.ds(pl.multiple_of(index * 2 * HD, 2 * HD), HD)] = query_scr_out[
            :rows
        ]
        grad_queries_ref[:, pl.ds(pl.multiple_of(index * 2 * HD + HD, HD), HD)] = query_scr_out[
            rows:
        ]
        return carry

    lax.fori_loop(0, group // 2, one_pair, 0)

    def key_step(step, carry):
        where = pl.ds(pl.multiple_of(step * chunk, chunk), chunk)
        grad_value = lax.dot_general(
            low_scr[where, :], dout_scr[...], (((1,), (0,)), ((), ())), preferred_element_type=F32
        ).astype(BF16)
        grad_key = (
            lax.dot_general(
                dscore_scr[where, :],
                query_scr[...],
                (((1,), (0,)), ((), ())),
                preferred_element_type=F32,
            )
            * scale
        ).astype(BF16)
        per_chunk = chunk // tile_len
        for k in range(per_chunk):
            slot = step * per_chunk + k
            source = pl.ds(holder_ref[slot] * pieces, pieces)
            rank = rank_ref[slot]
            part = slice(k * tile_len, (k + 1) * tile_len)
            back_ref[source, rank] = grad_key[part].reshape(pieces, tile_len // pieces, HD)
            back_ref[source, capacity + rank] = grad_value[part].reshape(
                pieces, tile_len // pieces, HD
            )
        return carry

    lax.fori_loop(0, chunks, key_step, 0)


def per_device(queries, keys_in, values_in, dout, req_tiles, tile_docs, tile_rows, doc_ends):
    dp_count = lax.axis_size("dp")
    heads = lax.axis_size("tensor")
    slots = req_tiles.shape[0]
    capacity = slots // dp_count + 1
    row_part = keys_in.shape[1]
    rows = queries.shape[0]
    smem = pl.BlockSpec(memory_space=pltpu.SMEM)
    vmem = pl.BlockSpec(memory_space=pltpu.VMEM)
    params = pltpu.CompilerParams(vmem_limit_bytes=VMEM_LIMIT)

    holder = req_tiles // slots
    slot_index = jnp.arange(slots, dtype=jnp.int32)
    same_before = (holder[:, None] == holder[None, :]) & (slot_index[None, :] < slot_index[:, None])
    rank = jnp.sum(same_before.astype(jnp.int32), axis=1)
    place = holder * HD + rank
    lanes = jnp.arange(dp_count * HD, dtype=jnp.int32).reshape(dp_count, HD)
    asked = jnp.sum(
        jnp.where(place[None, None, :] == lanes[:, :capacity, None], (req_tiles % slots + 1)[None, None, :], 0),
        axis=-1,
    )
    asked = jnp.pad(asked - 1, ((0, 0), (0, HD - capacity)))[:, None, :]
    wanted = lax.all_to_all(asked, "dp", split_axis=0, concat_axis=0, tiled=True)[:, :, :capacity]

    send = pl.pallas_call(
        pick_tiles,
        out_shape=jax.ShapeDtypeStruct((dp_count * heads, 2 * capacity, row_part, HD), BF16),
        in_specs=[smem, vmem, vmem],
        out_specs=vmem,
        compiler_params=params,
        name="pick_tiles",
    )(wanted, keys_in, values_in)
    recv = lax.all_to_all(send, ("dp", "tensor"), split_axis=0, concat_axis=0, tiled=True)

    doc_count = doc_ends.shape[0]
    slot_ends = jnp.sum(
        jnp.where(
            tile_docs[:, None] == jnp.arange(doc_count, dtype=jnp.int32)[None, :],
            doc_ends[None, :],
            0,
        ),
        axis=1,
    )
    text_row = jnp.arange(rows, dtype=jnp.int32)[None, :]
    seen = (text_row >= tile_rows[:, None]) & (text_row < slot_ends[:, None])
    bias = jnp.where(seen, 0.0, HIDDEN).astype(F32)

    key_count = slots * row_part * heads
    group = queries.shape[1] // HD
    back, grad_queries = pl.pallas_call(
        attend_backward,
        out_shape=(
            jax.ShapeDtypeStruct(recv.shape, BF16),
            jax.ShapeDtypeStruct(queries.shape, BF16),
        ),
        in_specs=[smem, smem, vmem, vmem, vmem, vmem],
        out_specs=(vmem, vmem),
        scratch_shapes=[
            pltpu.VMEM((key_count, HD), BF16),
            pltpu.VMEM((key_count, HD), BF16),
            pltpu.VMEM((key_count, rows), F32),
            pltpu.VMEM((group * rows, HD), BF16),
            pltpu.VMEM((group * rows, HD), BF16),
            pltpu.VMEM((key_count, 2 * rows), F32),
            pltpu.VMEM((key_count, 2 * rows), F32),
            pltpu.VMEM((key_count, group * rows), BF16),
            pltpu.VMEM((key_count, group * rows), BF16),
        ],
        compiler_params=params,
        name="attend_backward",
    )(holder, rank, bias, recv, queries, dout)

    home = lax.all_to_all(back, ("dp", "tensor"), split_axis=0, concat_axis=0, tiled=True)
    grad_keys, grad_values = pl.pallas_call(
        place_tiles,
        out_shape=(
            jax.ShapeDtypeStruct(keys_in.shape, BF16),
            jax.ShapeDtypeStruct(values_in.shape, BF16),
        ),
        in_specs=[smem, vmem],
        out_specs=(vmem, vmem),
        compiler_params=params,
        name="place_tiles",
    )(wanted, home)
    return (grad_queries, grad_keys, grad_values)


def solution(mesh):
    return jax.shard_map(
        per_device,
        mesh=mesh,
        in_specs=(
            P("dp", "tensor"),
            P("dp", "tensor", None),
            P("dp", "tensor", None),
            P("dp", "tensor"),
            P("dp"),
            P("dp"),
            P("dp"),
            P("dp"),
        ),
        out_specs=(P("dp", "tensor"), P("dp", "tensor", None), P("dp", "tensor", None)),
        check_vma=False,
    )
```

time: 368 us -> 175 us (0.48)
  waiting for transfers between devices: 141 us -> 44.3 us
  local copies, waits for them, and re-layouts: 97.6 us -> 2.21 us
  Pallas kernels: 0 us -> 37.8 us
  blocking collectives: 39.8 us -> 74.3 us
  matrix products: 31.4 us -> 0 us
  starting transfers between devices: 44.6 us -> 14.6 us
  other arithmetic: 10.6 us -> 1.26 us
    all_to_all x8 -> x1, waiting for transfers between devices: 141 us -> 44.3 us  [per_device(): lax.all_to_all(send, ('dp', 'tensor'), split_axis=0, concat_axis=0, tiled...]
    all_to_all x0 -> x2, blocking collectives: none -> 74.3 us  [the longest x1 53.5 us: per_device(): lax.all_to_all(back, ('dp', 'tensor'), split_axis=0, concat_axis=0, tiled...]
    scatter x4 -> x0, local copies, waits for them, and re-layouts: 47.3 us -> none  [the longest x1 16.2 us: per_device(): grad_keys = jnp.zeros(keys_in.shape, jnp.bfloat16).at[target].set(home_ke...]
    all_gather x1 -> x0, blocking collectives: 39.8 us -> none  [per_device(): lax.all_gather(req_tiles, 'dp', axis=0, tiled=True).reshape(dp_count, slots)]
    pallas_call x0 -> x3, Pallas kernels: none -> 37.8 us  [the longest x1 29.2 us: per_device(): pl.pallas_call(attend_backward, out_shape=(jax.ShapeDtypeStruct(recv.shap...]
    all_to_all x8 -> x1, starting transfers between devices: 44.6 us -> 14.6 us  [per_device(): lax.all_to_all(send, ('dp', 'tensor'), split_axis=0, concat_axis=0, tiled...]
    dot_general x10 -> x0, matrix products: 22 us -> none  [the longest x2 7.58 us: one_step(): jnp.einsum('rgk,rgd->kd', dscores, query_part, preferred_element_type=jnp...]
    all_to_all x6 -> x0, local copies, waits for them, and re-layouts: 11.4 us -> none  [the longest x2 5.76 us: per_device(): lax.all_to_all(send_values, 'tensor', split_axis=3, concat_axis=2, tiled=...]
  transfers between devices with their start and end apart: 8 -> 1, of which waited for: 8 -> 1; matrix products, arithmetic and copies ran while one was open for 12% -> 0% of each run, Pallas kernels for 0% -> 0%
where the time goes in v1:
time: 175 us
  blocking collectives  74.3 us (42%)
  waiting for transfers between devices  44.3 us (25%)
  Pallas kernels  37.8 us (22%)
  starting transfers between devices  14.6 us (8%)
  local copies, waits for them, and re-layouts  2.21 us (1%)
    all_to_all x1, blocking collectives, per_device(): lax.all_to_all(back, ('dp', 'tensor'), split_axis=0, concat_axis=0, tiled...  53.5 us
    all_to_all x1, waiting for transfers between devices, per_device(): lax.all_to_all(send, ('dp', 'tensor'), split_axis=0, concat_axis=0, tiled...  44.3 us
    pallas_call x1, Pallas kernels, per_device(): pl.pallas_call(attend_backward, out_shape=(jax.ShapeDtypeStruct(recv.shap...  29.2 us
    all_to_all x1, blocking collectives, per_device(): lax.all_to_all(asked, 'dp', split_axis=0, concat_axis=0, tiled=True)  20.7 us
    all_to_all x1, starting transfers between devices, per_device(): lax.all_to_all(send, ('dp', 'tensor'), split_axis=0, concat_axis=0, tiled...  14.6 us
    pallas_call x1, Pallas kernels, per_device(): pl.pallas_call(place_tiles, out_shape=(jax.ShapeDtypeStruct(keys_in.shape...  4.53 us
    pallas_call x1, Pallas kernels, per_device(): pl.pallas_call(pick_tiles, out_shape=jax.ShapeDtypeStruct((dp_count * hea...  4.05 us
  transfers between devices with their start and end apart: 1, of which 1 were waited for; matrix products, arithmetic and copies ran while one was open for 0% of the time, Pallas kernels for 0%

profile of v1, /device:TPU:1, one launch (start us, length us, event | category | flops | bytes accessed | tf_op | source)
XLA Modules:
  0.0 175.1 jit_solution(15623871773357516802)
XLA Ops:
  0.6 0.7 fusion.3
  1.3 0.2 convert_reduce_fusion.rank_ref
  1.5 0.2 select_reduce_fusion
  1.7 0.1 copy.12
  1.8 20.7 %all_to_all.15 = s32[64,1,128]{2,1,0:T(1,128)S(1)} all-to-all(s32[64,1,128]{2,1,0:T(1,128)S(1)} %bitcast.4), channel_id=1, replica_groups=mesh['dp'=64,'tensor'=8] {'dp'}, dimensions={0} | all-to-all | bytes 65536 | tf_op jit(solution)/shard_map/all_to_all | solution.py:220
  22.6 0.0 copy-start
  22.6 1.0 copy-done
  23.6 0.0 copy-start.1
  23.6 1.0 copy-done.1
  24.6 4.1 %pick_tiles.1 = bf16[512,6,2,128]{3,2,1,0:T(2,128)(2,1)} custom-call(s32[64,1,3]{2,1,0:T(1,128)S(1)} %bitcast.2, bf16[128,2,1024]{2,1,0:T(2,128)(2,1)S(1)} %copy-done, bf16[128,2,1024]{2,1,0:T(2,128)(2,1)S(1)} %copy-done.1), custom_call_target="tpu_custom_call" | custom-call | tf_op jit(solution)/shard_map/pick_tiles/pallas_call | solution.py:222
  28.7 0.0 copy-start.5
  28.7 0.0 copy-start.6
  28.7 0.0 copy-start.4
  28.7 0.0 copy-start.2
  28.7 0.0 copy-start.3
  28.7 14.6 %all-to-all-start.1 = ((bf16[512,6,2,128]{3,2,1,0:T(2,128)(2,1)}), bf16[512,6,2,128]{3,2,1,0:T(2,128)(2,1)S(1)}, u32[]{:S(2)}, u32[]{:S(2)}) async-start(bf16[512,6,2,128]{3,2,1,0:T(2,128)(2,1)} %pick_tiles.1), calls=%async_computation.1 | async-start | bytes 3145728 | tf_op jit(solution)/shard_map/all_to_all | solution.py:230
  43.3 0.0 copy-done.5
  43.3 0.0 copy-done.6
  43.3 0.1 select_reduce_fusion.1
  43.4 0.0 copy-done.4
  43.4 0.1 fusion.2.bias_ref
  43.5 44.3 %all-to-all-done.1.recv_ref = bf16[512,6,2,128]{3,2,1,0:T(2,128)(2,1)S(1)} async-done(((bf16[512,6,2,128]{3,2,1,0:T(2,128)(2,1)}), bf16[512,6,2,128]{3,2,1,0:T(2,128)(2,1)S(1)}, u32[]{:S(2)}, u32[]{:S(2)}) %all-to-all-start.1) | async-done | bytes 1572896 | tf_op jit(solution)/shard_map/all_to_all | solution.py:230
  87.8 0.0 copy-done.2
  87.8 0.0 copy-done.3
  87.8 29.2 %attend_backward.1 = (bf16[512,6,2,128]{3,2,1,0:T(2,128)(2,1)S(1)}, bf16[128,1024]{1,0:T(8,128)(2,1)}) custom-call(s32[128]{0:T(128)S(1)} %get-tuple-element.12.holder_ref, s32[128]{0:T(128)S(1)} %convert_reduce_fusion.rank_ref, f32[128,128]{1,0:T(8,128)S(1)} %fusion.2.bias_ref, bf16[512,6,2,128]{3,2,1,0:T(2,128)(2,1)S(1)} %all-to-all-done.1.recv_ref, ...), custom_call_target="tpu_custom_call" | custom-call | tf_op jit(solution)/shard_map/attend_backward/pallas_call | solution.py:247
  117.0 53.5 %all_to_all.16.home_ref = bf16[512,6,2,128]{3,2,1,0:T(2,128)(2,1)S(1)} all-to-all(bf16[512,6,2,128]{3,2,1,0:T(2,128)(2,1)S(1)} %get-tuple-element.8), channel_id=1, replica_groups=mesh['dp'=64,'tensor'=8] {'dp','tensor'}, dimensions={0} | all-to-all | bytes 3145728 | tf_op jit(solution)/shard_map/all_to_all | solution.py:270
  170.6 4.5 %place_tiles.1 = (bf16[128,2,1024]{2,1,0:T(2,128)(2,1)}, bf16[128,2,1024]{2,1,0:T(2,128)(2,1)}) custom-call(s32[64,1,3]{2,1,0:T(1,128)S(1)} %bitcast.3, bf16[512,6,2,128]{3,2,1,0:T(2,128)(2,1)S(1)} %all_to_all.16.home_ref), custom_call_target="tpu_custom_call" | custom-call | tf_op jit(solution)/shard_map/place_tiles/pallas_call | solution.py:271
  (4 shorter events, 0.0 us)
Async XLA Ops:
  22.6 1.0 copy-start
  23.6 1.0 copy-start.1
  28.7 14.6 %copy-start.5 = (s32[8]{0:T(128)S(1)}, s32[8]{0:T(128)}, u32[]{:S(2)}) copy-start(s32[8]{0:T(128)} %param.15) | copy-start | bytes 100
  28.7 14.6 %copy-start.6 = (s32[128]{0:T(128)S(1)}, s32[128]{0:T(128)}, u32[]{:S(2)}) copy-start(s32[128]{0:T(128)} %param.13) | copy-start | bytes 1540
  28.7 14.7 %copy-start.4 = (s32[128]{0:T(128)S(1)}, s32[128]{0:T(128)}, u32[]{:S(2)}) copy-start(s32[128]{0:T(128)} %param.14) | copy-start | bytes 1540
  28.7 59.1 %copy-start.2 = (bf16[128,1024]{1,0:T(8,128)(2,1)S(1)}, bf16[128,1024]{1,0:T(8,128)(2,1)}, u32[]{:S(2)}) copy-start(bf16[128,1024]{1,0:T(8,128)(2,1)} %queries_ref.1) | copy-start | bytes 786436
  28.7 59.1 %copy-start.3 = (bf16[128,1024]{1,0:T(8,128)(2,1)S(1)}, bf16[128,1024]{1,0:T(8,128)(2,1)}, u32[]{:S(2)}) copy-start(bf16[128,1024]{1,0:T(8,128)(2,1)} %dout_ref.1) | copy-start | bytes 786436
  28.7 59.1 %all-to-all-start.1 = ((bf16[512,6,2,128]{3,2,1,0:T(2,128)(2,1)}), bf16[512,6,2,128]{3,2,1,0:T(2,128)(2,1)S(1)}, u32[]{:S(2)}, u32[]{:S(2)}) async-start(bf16[512,6,2,128]{3,2,1,0:T(2,128)(2,1)} %pick_tiles.1), calls=%async_computation.1 | async-start | bytes 3145728 | tf_op jit(solution)/shard_map/all_to_all | solution.py:230

commit v2 on v1

v2 whole, which is shorter than its diff:
```python
import math

import jax
import jax.numpy as jnp
from jax import lax
from jax.experimental import pallas as pl
from jax.experimental.pallas import tpu as pltpu
from jax.sharding import PartitionSpec as P

HD = 128
TILE = 16
BF16 = jnp.bfloat16
F32 = jnp.float32
HIDDEN = -1e30
CHUNK = 512
BLOCK = 256
VMEM_LIMIT = 48 * 1024 * 1024


def pick_tiles(wanted_ref, keys_ref, values_ref, send_ref):
    readers, _, capacity = wanted_ref.shape
    heads = keys_ref.shape[2] // HD

    def one_reader(reader, carry):
        for rank in range(capacity):
            tile = jnp.maximum(wanted_ref[reader, 0, rank], 0)
            for head in range(heads):
                cols = slice(head * HD, (head + 1) * HD)
                send_ref[reader * heads + head, rank] = keys_ref[tile, :, cols]
                send_ref[reader * heads + head, capacity + rank] = values_ref[tile, :, cols]
        return carry

    lax.fori_loop(0, readers, one_reader, 0)


def place_tiles(wanted_ref, home_ref, grad_keys_ref, grad_values_ref):
    readers, _, capacity = wanted_ref.shape
    heads = grad_keys_ref.shape[2] // HD

    def one_reader(reader, carry):
        for rank in range(capacity):
            tile = wanted_ref[reader, 0, rank]

            @pl.when(tile >= 0)
            def _():
                for head in range(heads):
                    cols = slice(head * HD, (head + 1) * HD)
                    grad_keys_ref[tile, :, cols] = home_ref[reader * heads + head, rank]
                    grad_values_ref[tile, :, cols] = home_ref[
                        reader * heads + head, capacity + rank
                    ]

        return carry

    lax.fori_loop(0, readers, one_reader, 0)


def attend_backward(
    holder_ref,
    rank_ref,
    first_ref,
    last_ref,
    bias_ref,
    recv_ref,
    queries_ref,
    dout_ref,
    back_ref,
    grad_queries_ref,
    key_scr,
    value_scr,
    expo_scr,
    dprob_scr,
    top_scr,
    grad_key_scr,
    grad_value_scr,
):
    scale = 1.0 / math.sqrt(HD)
    slots = bias_ref.shape[0]
    capacity = recv_ref.shape[1] // 2
    tile_len = key_scr.shape[0] // slots
    pieces = tile_len // recv_ref.shape[2]
    chunk, block = expo_scr.shape[1:]
    blocks = queries_ref.shape[0] // block
    contract_last = (((1,), (1,)), ((), ()))
    contract_inner = (((1,), (0,)), ((), ()))
    contract_first = (((0,), (0,)), ((), ()))

    def gather_slot(slot, carry):
        source = pl.ds(holder_ref[slot] * pieces, pieces)
        rank = rank_ref[slot]
        target = pl.ds(pl.multiple_of(slot * tile_len, tile_len), tile_len)
        key_scr[target, :HD] = recv_ref[source, rank].reshape(tile_len, HD)
        key_scr[target, HD:] = jnp.broadcast_to(bias_ref[pl.ds(slot, 1), :], (tile_len, HD)).astype(
            BF16
        )
        value_scr[target, :] = recv_ref[source, capacity + rank].reshape(tile_len, HD)
        return carry

    lax.fori_loop(0, slots, gather_slot, 0, unroll=8)
    grad_key_scr[...] = jnp.zeros_like(grad_key_scr)
    grad_value_scr[...] = jnp.zeros_like(grad_value_scr)

    def one_block(index, carry):
        rows = pl.ds(pl.multiple_of(index * block, block), block)
        first, last = first_ref[index], last_ref[index]

        def keys_of(step):
            return pl.ds(pl.multiple_of(step * chunk, chunk), chunk)

        def forward(step, carry):
            top, total, delta = carry
            where = keys_of(step)
            score = lax.dot_general(
                key_scr[where, :], queries_ref[rows, :], contract_last, preferred_element_type=F32
            )
            dprob = lax.dot_general(
                value_scr[where, :], dout_ref[rows, :], contract_last, preferred_element_type=F32
            )
            new_top = jnp.maximum(top, jnp.max(score, axis=0, keepdims=True))
            shrink = jnp.exp((top - new_top) * scale)
            expo = jnp.exp((score - new_top) * scale)
            expo_scr[step] = expo
            dprob_scr[step] = dprob
            top_scr[pl.ds(step, 1), :] = new_top
            return (
                new_top,
                total * shrink + jnp.sum(expo, axis=0, keepdims=True),
                delta * shrink + jnp.sum(expo * dprob, axis=0, keepdims=True),
            )

        zero = jnp.zeros((1, block), F32)
        top, total, delta = lax.fori_loop(
            first, last, forward, (jnp.full((1, block), 2 * HIDDEN, F32), zero, zero)
        )
        inverse = 1.0 / total
        delta = delta * inverse

        def backward(step, grad_query):
            where = keys_of(step)
            factor = jnp.exp((top_scr[pl.ds(step, 1), :] - top) * scale) * inverse
            prob = expo_scr[step] * factor
            dscore = (prob * (dprob_scr[step] - delta)).astype(BF16)
            grad_value_scr[where, :] += lax.dot_general(
                prob.astype(BF16), dout_ref[rows, :], contract_inner, preferred_element_type=F32
            )
            grad_key_scr[where, :] += lax.dot_general(
                dscore, queries_ref[rows, :HD], contract_inner, preferred_element_type=F32
            )
            return grad_query + lax.dot_general(
                dscore, key_scr[where, :HD], contract_first, preferred_element_type=F32
            )

        grad_query = lax.fori_loop(first, last, backward, jnp.zeros((block, HD), F32))
        grad_queries_ref[rows, :] = (grad_query * scale).astype(BF16)
        return carry

    lax.fori_loop(0, blocks, one_block, 0)

    def return_slot(slot, carry):
        source = pl.ds(holder_ref[slot] * pieces, pieces)
        rank = rank_ref[slot]
        where = pl.ds(pl.multiple_of(slot * tile_len, tile_len), tile_len)
        shape = (pieces, tile_len // pieces, HD)
        back_ref[source, rank] = (grad_key_scr[where, :] * scale).astype(BF16).reshape(shape)
        back_ref[source, capacity + rank] = grad_value_scr[where, :].astype(BF16).reshape(shape)
        return carry

    lax.fori_loop(0, slots, return_slot, 0, unroll=8)


def attention(recv, queries, dout, holder, rank, tile_docs, tile_rows, doc_ends):
    slots, rows = holder.shape[0], queries.shape[0]
    smem = pl.BlockSpec(memory_space=pltpu.SMEM)
    vmem = pl.BlockSpec(memory_space=pltpu.VMEM)
    group = queries.shape[1] // HD
    docs = tile_docs[:, None] == jnp.arange(doc_ends.shape[0], dtype=jnp.int32)[None, :]
    slot_ends = jnp.sum(jnp.where(docs, doc_ends[None, :], 0), axis=1)
    slot_begins = jnp.sum(jnp.where(docs[:, 1:], doc_ends[None, :-1], 0), axis=1)
    text_row = jnp.arange(rows, dtype=jnp.int32)
    seen = (text_row[None, :] >= tile_rows[:, None]) & (text_row[None, :] < slot_ends[:, None])
    bias = jnp.where(seen, 0.0, HIDDEN).astype(F32)
    tile_len = TILE
    chunk_slots = CHUNK // tile_len
    block_begin = jnp.arange(rows * group // BLOCK, dtype=jnp.int32) * (BLOCK // group)
    before = jnp.sum((slot_ends[None, :] <= block_begin[:, None]).astype(jnp.int32), axis=1)
    until = jnp.sum(
        (slot_begins[None, :] < block_begin[:, None] + BLOCK // group).astype(jnp.int32), axis=1
    )
    first = before // chunk_slots
    last = (until + chunk_slots - 1) // chunk_slots

    flat = rows * group
    query_rows = queries.reshape(flat, HD)
    dout_rows = dout.reshape(flat, HD)
    own_row = (jnp.arange(flat, dtype=jnp.int32) // group)[:, None] == text_row[None, :]
    query_rows = jnp.concatenate([query_rows, own_row.astype(BF16)], axis=1)

    key_count = slots * tile_len
    return pl.pallas_call(
        attend_backward,
        out_shape=(
            jax.ShapeDtypeStruct(recv.shape, BF16),
            jax.ShapeDtypeStruct((flat, HD), BF16),
        ),
        in_specs=[smem] * 4 + [vmem] * 4,
        out_specs=(vmem, vmem),
        scratch_shapes=[
            pltpu.VMEM((key_count, 2 * HD), BF16),
            pltpu.VMEM((key_count, HD), BF16),
            pltpu.VMEM((key_count // CHUNK, CHUNK, BLOCK), F32),
            pltpu.VMEM((key_count // CHUNK, CHUNK, BLOCK), F32),
            pltpu.VMEM((key_count // CHUNK, BLOCK), F32),
            pltpu.VMEM((key_count, HD), F32),
            pltpu.VMEM((key_count, HD), F32),
        ],
        compiler_params=pltpu.CompilerParams(vmem_limit_bytes=VMEM_LIMIT),
        name="attend_backward",
    )(holder, rank, first, last, bias, recv, query_rows, dout_rows)


def per_device(queries, keys_in, values_in, dout, req_tiles, tile_docs, tile_rows, doc_ends):
    dp_count = lax.axis_size("dp")
    heads = lax.axis_size("tensor")
    slots = req_tiles.shape[0]
    capacity = slots // dp_count + 1
    row_part = keys_in.shape[1]
    rows = queries.shape[0]
    smem = pl.BlockSpec(memory_space=pltpu.SMEM)
    vmem = pl.BlockSpec(memory_space=pltpu.VMEM)
    params = pltpu.CompilerParams(vmem_limit_bytes=VMEM_LIMIT)

    holder = req_tiles // slots
    slot_index = jnp.arange(slots, dtype=jnp.int32)
    same_before = (holder[:, None] == holder[None, :]) & (slot_index[None, :] < slot_index[:, None])
    rank = jnp.sum(same_before.astype(jnp.int32), axis=1)
    place = holder * HD + rank
    lanes = jnp.arange(dp_count * HD, dtype=jnp.int32).reshape(dp_count, HD)
    asked = jnp.sum(
        jnp.where(place[None, None, :] == lanes[:, :capacity, None], (req_tiles % slots + 1)[None, None, :], 0),
        axis=-1,
    )
    asked = jnp.pad(asked - 1, ((0, 0), (0, HD - capacity)))[:, None, :]
    wanted = lax.all_to_all(asked, "dp", split_axis=0, concat_axis=0, tiled=True)[:, :, :capacity]

    send = pl.pallas_call(
        pick_tiles,
        out_shape=jax.ShapeDtypeStruct((dp_count * heads, 2 * capacity, row_part, HD), BF16),
        in_specs=[smem, vmem, vmem],
        out_specs=vmem,
        compiler_params=params,
        name="pick_tiles",
    )(wanted, keys_in, values_in)
    recv = lax.all_to_all(send, ("dp", "tensor"), split_axis=0, concat_axis=0, tiled=True)

    back, grad_queries = attention(
        recv, queries, dout, holder, rank, tile_docs, tile_rows, doc_ends
    )

    home = lax.all_to_all(back, ("dp", "tensor"), split_axis=0, concat_axis=0, tiled=True)
    grad_keys, grad_values = pl.pallas_call(
        place_tiles,
        out_shape=(
            jax.ShapeDtypeStruct(keys_in.shape, BF16),
            jax.ShapeDtypeStruct(values_in.shape, BF16),
        ),
        in_specs=[smem, vmem],
        out_specs=(vmem, vmem),
        compiler_params=params,
        name="place_tiles",
    )(wanted, home)
    return (grad_queries.reshape(queries.shape), grad_keys, grad_values)


def solution(mesh):
    return jax.shard_map(
        per_device,
        mesh=mesh,
        in_specs=(
            P("dp", "tensor"),
            P("dp", "tensor", None),
            P("dp", "tensor", None),
            P("dp", "tensor"),
            P("dp"),
            P("dp"),
            P("dp"),
            P("dp"),
        ),
        out_specs=(P("dp", "tensor"), P("dp", "tensor", None), P("dp", "tensor", None)),
        check_vma=False,
    )
```

time: 175 us -> 157 us (0.90)
  blocking collectives: 74.3 us -> 20.7 us
  waiting for transfers between devices: 44.3 us -> 86.8 us
  Pallas kernels: 37.8 us -> 19.1 us
  starting transfers between devices: 14.6 us -> 23.1 us
  local copies, waits for them, and re-layouts: 2.21 us -> 4.4 us
    all_to_all x1 -> x0, blocking collectives: 53.5 us -> none  [per_device(): lax.all_to_all(back, ('dp', 'tensor'), split_axis=0, concat_axis=0, tiled...]
    all_to_all x0 -> x1, waiting for transfers between devices: none -> 43.7 us  [per_device(): lax.all_to_all(back, ('dp', 'tensor'), split_axis=0, concat_axis=0, tiled...]
    pallas_call x1, Pallas kernels: 29.2 us -> 10.5 us  [attention(): pl.pallas_call(attend_backward, out_shape=(jax.ShapeDtypeStruct(recv.shap...]
    all_to_all x0 -> x1, starting transfers between devices: none -> 8.51 us  [per_device(): lax.all_to_all(back, ('dp', 'tensor'), split_axis=0, concat_axis=0, tiled...]
  transfers between devices with their start and end apart: 1 -> 2, of which waited for: 1 -> 2; matrix products, arithmetic and copies ran while one was open for 0% -> 1% of each run, Pallas kernels for 0% -> 0%
where the time goes in v2:
time: 157 us
  waiting for transfers between devices  86.8 us (55%)
  starting transfers between devices  23.1 us (15%)
  blocking collectives  20.7 us (13%)
  Pallas kernels  19.1 us (12%)
  local copies, waits for them, and re-layouts  4.4 us (3%)
  other arithmetic  2.03 us (1%)
    all_to_all x1, waiting for transfers between devices, per_device(): lax.all_to_all(back, ('dp', 'tensor'), split_axis=0, concat_axis=0, tiled...  43.7 us
    all_to_all x1, waiting for transfers between devices, per_device(): lax.all_to_all(send, ('dp', 'tensor'), split_axis=0, concat_axis=0, tiled...  43.2 us
    all_to_all x1, blocking collectives, per_device(): lax.all_to_all(asked, 'dp', split_axis=0, concat_axis=0, tiled=True)  20.7 us
    all_to_all x1, starting transfers between devices, per_device(): lax.all_to_all(send, ('dp', 'tensor'), split_axis=0, concat_axis=0, tiled...  14.6 us
    pallas_call x1, Pallas kernels, attention(): pl.pallas_call(attend_backward, out_shape=(jax.ShapeDtypeStruct(recv.shap...  10.5 us
    all_to_all x1, starting transfers between devices, per_device(): lax.all_to_all(back, ('dp', 'tensor'), split_axis=0, concat_axis=0, tiled...  8.51 us
    pallas_call x1, Pallas kernels, per_device(): pl.pallas_call(place_tiles, out_shape=(jax.ShapeDtypeStruct(keys_in.shape...  4.53 us
    pallas_call x1, Pallas kernels, per_device(): pl.pallas_call(pick_tiles, out_shape=jax.ShapeDtypeStruct((dp_count * hea...  4.04 us
  transfers between devices with their start and end apart: 2, of which 2 were waited for; matrix products, arithmetic and copies ran while one was open for 1% of the time, Pallas kernels for 0%

profile of v2, /device:TPU:1, one launch (start us, length us, event | category | flops | bytes accessed | tf_op | source)
XLA Modules:
  0.0 157.0 jit_solution(13605566574379214962)
XLA Ops:
  0.6 0.7 fusion.7
  1.3 0.2 convert_reduce_fusion.rank_ref
  1.5 0.2 select_reduce_fusion
  1.7 0.1 copy.12
  1.8 20.7 %all_to_all.15 = s32[64,1,128]{2,1,0:T(1,128)S(1)} all-to-all(s32[64,1,128]{2,1,0:T(1,128)S(1)} %bitcast.5), channel_id=1, replica_groups=mesh['dp'=64,'tensor'=8] {'dp'}, dimensions={0} | all-to-all | bytes 65536 | tf_op jit(solution)/shard_map/all_to_all | solution.py:243
  22.6 1.0 copy-done.1
  23.6 1.0 copy-done.2
  24.6 4.0 %pick_tiles.1 = bf16[512,6,2,128]{3,2,1,0:T(2,128)(2,1)} custom-call(s32[64,1,3]{2,1,0:T(1,128)S(1)} %bitcast.3, bf16[128,2,1024]{2,1,0:T(2,128)(2,1)S(1)} %copy-done.1, bf16[128,2,1024]{2,1,0:T(2,128)(2,1)S(1)} %copy-done.2), custom_call_target="tpu_custom_call" | custom-call | tf_op jit(solution)/shard_map/pick_tiles/pallas_call | solution.py:245
  28.7 14.6 %all-to-all-start.1 = ((bf16[512,6,2,128]{3,2,1,0:T(2,128)(2,1)}), bf16[512,6,2,128]{3,2,1,0:T(2,128)(2,1)S(1)}, u32[]{:S(2)}, u32[]{:S(2)}) async-start(bf16[512,6,2,128]{3,2,1,0:T(2,128)(2,1)} %pick_tiles.1), calls=%async_computation.1 | async-start | bytes 3145728 | tf_op jit(solution)/shard_map/all_to_all | solution.py:253
  43.3 0.0 copy-done.3
  43.3 0.0 copy-start.5
  43.3 0.1 reshape.58
  43.4 0.0 copy-done.4
  43.4 0.1 reshape.59.dout_ref
  43.6 0.0 copy-done.6
  43.6 0.0 copy-done.7
  43.6 0.1 select_reduce_fusion.2
  43.7 0.2 convert_reduce_fusion.2
  43.9 0.1 select_reduce_fusion.1
  44.0 0.2 convert_reduce_fusion.1
  44.2 0.2 fusion
  44.4 0.1 pad_maximum_fusion.queries_ref
  44.5 0.0 copy-done.5
  44.5 0.1 fusion.3.bias_ref
  44.6 43.2 %all-to-all-done.1.recv_ref = bf16[512,6,2,128]{3,2,1,0:T(2,128)(2,1)S(1)} async-done(((bf16[512,6,2,128]{3,2,1,0:T(2,128)(2,1)}), bf16[512,6,2,128]{3,2,1,0:T(2,128)(2,1)S(1)}, u32[]{:S(2)}, u32[]{:S(2)}) %all-to-all-start.1) | async-done | bytes 1572896 | tf_op jit(solution)/shard_map/all_to_all | solution.py:253
  87.8 10.5 %attend_backward.1 = (bf16[512,6,2,128]{3,2,1,0:T(2,128)(2,1)S(1)}, bf16[1024,128]{1,0:T(8,128)(2,1)S(1)}) custom-call(s32[128]{0:T(128)S(1)} %get-tuple-element.12.holder_ref, s32[128]{0:T(128)S(1)} %convert_reduce_fusion.rank_ref, s32[4]{0:T(128)S(1)} %get-tuple-element.14.first_ref, s32[4]{0:T(128)S(1)} %get-tuple-element.13.last_ref, ...), custom_call_target="tpu_custom_call" | custom-call | tf_op jit(solution)/shard_map/attend_backward/pallas_call | solution.py:199
  98.3 0.0 copy-start
  98.3 1.1 copy-done
  99.5 8.5 %all-to-all-start.2 = ((bf16[512,6,2,128]{3,2,1,0:T(2,128)(2,1)}), bf16[512,6,2,128]{3,2,1,0:T(2,128)(2,1)S(1)}, u32[]{:S(2)}, u32[]{:S(2)}) async-start(bf16[512,6,2,128]{3,2,1,0:T(2,128)(2,1)} %copy-done), calls=%async_computation.2 | async-start | bytes 3145728 | tf_op jit(solution)/shard_map/all_to_all | solution.py:259
  108.0 0.8 reshape.60
  108.8 43.7 %all-to-all-done.2.home_ref = bf16[512,6,2,128]{3,2,1,0:T(2,128)(2,1)S(1)} async-done(((bf16[512,6,2,128]{3,2,1,0:T(2,128)(2,1)}), bf16[512,6,2,128]{3,2,1,0:T(2,128)(2,1)S(1)}, u32[]{:S(2)}, u32[]{:S(2)}) %all-to-all-start.2) | async-done | bytes 1572896 | tf_op jit(solution)/shard_map/all_to_all | solution.py:259
  152.5 4.5 %place_tiles.1 = (bf16[128,2,1024]{2,1,0:T(2,128)(2,1)}, bf16[128,2,1024]{2,1,0:T(2,128)(2,1)}) custom-call(s32[64,1,3]{2,1,0:T(1,128)S(1)} %bitcast.4, bf16[512,6,2,128]{3,2,1,0:T(2,128)(2,1)S(1)} %all-to-all-done.2.home_ref), custom_call_target="tpu_custom_call" | custom-call | tf_op jit(solution)/shard_map/place_tiles/pallas_call | solution.py:260
  (15 shorter events, 0.1 us)
Async XLA Ops:
  22.6 1.0 copy-start.1
  23.6 1.0 copy-start.2
  28.7 14.6 %copy-start.3 = (bf16[128,1024]{1,0:T(8,128)(2,1)S(1)}, bf16[128,1024]{1,0:T(8,128)(2,1)}, u32[]{:S(2)}) copy-start(bf16[128,1024]{1,0:T(8,128)(2,1)} %param.8) | copy-start | bytes 786436
  28.7 14.7 %copy-start.4 = (bf16[128,1024]{1,0:T(8,128)(2,1)S(1)}, bf16[128,1024]{1,0:T(8,128)(2,1)}, u32[]{:S(2)}) copy-start(bf16[128,1024]{1,0:T(8,128)(2,1)} %param.11) | copy-start | bytes 786436
  28.7 14.9 %copy-start.6 = (s32[8]{0:T(128)S(1)}, s32[8]{0:T(128)}, u32[]{:S(2)}) copy-start(s32[8]{0:T(128)} %param.15) | copy-start | bytes 100
  28.7 14.9 %copy-start.7 = (s32[128]{0:T(128)S(1)}, s32[128]{0:T(128)}, u32[]{:S(2)}) copy-start(s32[128]{0:T(128)} %param.13) | copy-start | bytes 1540
  28.7 59.1 %all-to-all-start.1 = ((bf16[512,6,2,128]{3,2,1,0:T(2,128)(2,1)}), bf16[512,6,2,128]{3,2,1,0:T(2,128)(2,1)S(1)}, u32[]{:S(2)}, u32[]{:S(2)}) async-start(bf16[512,6,2,128]{3,2,1,0:T(2,128)(2,1)} %pick_tiles.1), calls=%async_computation.1 | async-start | bytes 3145728 | tf_op jit(solution)/shard_map/all_to_all | solution.py:253
  43.3 1.2 copy-start.5
  98.3 1.2 copy-start
  99.5 53.0 %all-to-all-start.2 = ((bf16[512,6,2,128]{3,2,1,0:T(2,128)(2,1)}), bf16[512,6,2,128]{3,2,1,0:T(2,128)(2,1)S(1)}, u32[]{:S(2)}, u32[]{:S(2)}) async-start(bf16[512,6,2,128]{3,2,1,0:T(2,128)(2,1)} %copy-done), calls=%async_computation.2 | async-start | bytes 3145728 | tf_op jit(solution)/shard_map/all_to_all | solution.py:259

commit v3 on v2

v3 whole, which is shorter than its diff:
```python
import math

import jax
import jax.numpy as jnp
from jax import lax
from jax.experimental import pallas as pl
from jax.experimental.pallas import tpu as pltpu
from jax.sharding import PartitionSpec as P

HD = 128
TILE = 16
BF16 = jnp.bfloat16
F32 = jnp.float32
HIDDEN = -1e30
CHUNK = 512
BLOCK = 256
PARTS = 4
VMEM_LIMIT = 48 * 1024 * 1024


def pick_tiles(
    wanted_ref, keys_hbm, values_hbm, send_hbm, keys_ref, values_ref, send_ref, in_sem, out_sem
):
    readers, _, capacity = wanted_ref.shape
    heads = keys_ref.shape[2] // HD
    loads = [
        pltpu.make_async_copy(keys_hbm, keys_ref, in_sem.at[0]),
        pltpu.make_async_copy(values_hbm, values_ref, in_sem.at[1]),
    ]
    for load in loads:
        load.start()
    for load in loads:
        load.wait()

    part = readers // PARTS
    stores = []
    for step in range(PARTS):

        def one_reader(offset, carry):
            reader = step * part + offset

            def one_tile(rank):
                tile = jnp.maximum(wanted_ref[reader, 0, rank], 0)
                for head in range(heads):
                    cols = slice(head * HD, (head + 1) * HD)
                    send_ref[reader * heads + head, rank] = keys_ref[tile, :, cols]
                    send_ref[reader * heads + head, capacity + rank] = values_ref[tile, :, cols]

            for rank in range(capacity):
                one_tile(rank)
            return carry

        lax.fori_loop(0, part, one_reader, 0, unroll=4)
        rows = pl.ds(step * part * heads, part * heads)
        stores.append(pltpu.make_async_copy(send_ref.at[rows], send_hbm.at[rows], out_sem.at[step]))
        stores[-1].start()
    for store in stores:
        store.wait()


def place_tiles(
    source_ref, home_ref, grad_keys_hbm, grad_values_hbm, grad_keys_ref, grad_values_ref, out_sem
):
    chunks, lines = home_ref.shape[:2]
    capacity = lines // 2
    heads = grad_keys_ref.shape[2] // HD
    flat_ref = home_ref.reshape(chunks * lines, *home_ref.shape[2:])
    part = grad_keys_ref.shape[0] // PARTS
    stores = []
    for step in range(PARTS):

        def one_tile(offset, carry):
            tile = step * part + offset
            source = source_ref[tile]
            for head in range(heads):
                cols = slice(head * HD, (head + 1) * HD)
                grad_keys_ref[tile, :, cols] = flat_ref[source + lines * head]
                grad_values_ref[tile, :, cols] = flat_ref[source + lines * head + capacity]
            return carry

        lax.fori_loop(0, part, one_tile, 0, unroll=4)
        rows = pl.ds(step * part, part)
        for kind, (ref, hbm) in enumerate(
            ((grad_keys_ref, grad_keys_hbm), (grad_values_ref, grad_values_hbm))
        ):
            stores.append(
                pltpu.make_async_copy(ref.at[rows], hbm.at[rows], out_sem.at[kind, step])
            )
            stores[-1].start()
    for store in stores:
        store.wait()


def attend_backward(
    holder_ref,
    rank_ref,
    slot_ref,
    first_ref,
    steps_ref,
    bias_ref,
    recv_ref,
    queries_ref,
    dout_ref,
    back_hbm,
    grad_queries_ref,
    key_scr,
    value_scr,
    expo_scr,
    dprob_scr,
    top_scr,
    grad_key_scr,
    grad_value_scr,
    back_ref,
    out_sem,
):
    scale = 1.0 / math.sqrt(HD)
    rate = scale * math.log2(math.e)
    slots = bias_ref.shape[0]
    capacity = recv_ref.shape[1] // 2
    tile_len = TILE
    pieces = tile_len // recv_ref.shape[2]
    chunk, block = expo_scr.shape[1:]
    blocks = queries_ref.shape[0] // block
    key_count = slots * tile_len
    tail = pl.ds(key_count, key_scr.shape[0] - key_count)
    contract_last = (((1,), (1,)), ((), ()))
    contract_inner = (((1,), (0,)), ((), ()))
    contract_first = (((0,), (0,)), ((), ()))

    def gather_slot(slot, carry):
        source = pl.ds(holder_ref[slot] * pieces, pieces)
        rank = rank_ref[slot]
        target = pl.ds(pl.multiple_of(slot * tile_len, tile_len), tile_len)
        key_scr[target, :HD] = recv_ref[source, rank].reshape(tile_len, HD)
        key_scr[target, HD:] = jnp.broadcast_to(bias_ref[pl.ds(slot, 1), :], (tile_len, HD)).astype(
            BF16
        )
        value_scr[target, :] = recv_ref[source, capacity + rank].reshape(tile_len, HD)
        return carry

    lax.fori_loop(0, slots, gather_slot, 0, unroll=8)
    key_scr[tail, :HD] = jnp.zeros((tail.size, HD), BF16)
    key_scr[tail, HD:] = jnp.full((tail.size, HD), HIDDEN, BF16)
    value_scr[tail, :] = jnp.zeros((tail.size, HD), BF16)
    grad_key_scr[...] = jnp.zeros_like(grad_key_scr)
    grad_value_scr[...] = jnp.zeros_like(grad_value_scr)

    def one_block(index, carry):
        rows = pl.ds(pl.multiple_of(index * block, block), block)
        first, steps = first_ref[index], steps_ref[index]

        def keys_of(step):
            return pl.ds(pl.multiple_of(first * tile_len + step * chunk, tile_len), chunk)

        def forward(step, carry):
            top, total, delta = carry
            where = keys_of(step)
            score = lax.dot_general(
                key_scr[where, :], queries_ref[rows, :], contract_last, preferred_element_type=F32
            )
            dprob = lax.dot_general(
                value_scr[where, :], dout_ref[rows, :], contract_last, preferred_element_type=F32
            )
            new_top = jnp.maximum(top, jnp.max(score, axis=0, keepdims=True))
            shrink = jnp.exp2((top - new_top) * rate)
            expo = jnp.exp2((score - new_top) * rate)
            expo_scr[step] = expo
            dprob_scr[step] = dprob
            top_scr[pl.ds(step, 1), :] = new_top
            return (
                new_top,
                total * shrink + jnp.sum(expo, axis=0, keepdims=True),
                delta * shrink + jnp.sum(expo * dprob, axis=0, keepdims=True),
            )

        zero = jnp.zeros((1, block), F32)
        top, total, delta = lax.fori_loop(
            0, steps, forward, (jnp.full((1, block), 2 * HIDDEN, F32), zero, zero)
        )
        inverse = 1.0 / total
        delta = delta * inverse

        def backward(step, grad_query):
            where = keys_of(step)
            factor = jnp.exp2((top_scr[pl.ds(step, 1), :] - top) * rate) * inverse
            prob = expo_scr[step] * factor
            dscore = (prob * (dprob_scr[step] - delta)).astype(BF16)
            grad_value_scr[where, :] += lax.dot_general(
                prob.astype(BF16), dout_ref[rows, :], contract_inner, preferred_element_type=F32
            )
            grad_key_scr[where, :] += lax.dot_general(
                dscore, queries_ref[rows, :HD], contract_inner, preferred_element_type=F32
            )
            return grad_query + lax.dot_general(
                dscore, key_scr[where, :HD], contract_first, preferred_element_type=F32
            )

        grad_query = lax.fori_loop(0, steps, backward, jnp.zeros((block, HD), F32))
        grad_queries_ref[rows, :] = (grad_query * scale).astype(BF16)
        return carry

    lax.fori_loop(0, blocks, one_block, 0)

    part = slot_ref.shape[0] // PARTS
    stores = []
    for step in range(PARTS):

        def return_tiles(offset, carry):
            holder = step * part + offset

            def one_tile(rank):
                slot = jnp.maximum(slot_ref[holder, rank], 0)
                where = pl.ds(pl.multiple_of(slot * tile_len, tile_len), tile_len)
                chunks = pl.ds(holder * pieces, pieces)
                shape = (pieces, tile_len // pieces, HD)
                grad_key = (grad_key_scr[where, :] * scale).astype(BF16)
                back_ref[chunks, rank] = grad_key.reshape(shape)
                grad_value = grad_value_scr[where, :].astype(BF16)
                back_ref[chunks, capacity + rank] = grad_value.reshape(shape)

            for rank in range(capacity):
                one_tile(rank)
            return carry

        lax.fori_loop(0, part, return_tiles, 0, unroll=4)
        chunks = pl.ds(step * part * pieces, part * pieces)
        stores.append(
            pltpu.make_async_copy(back_ref.at[chunks], back_hbm.at[chunks], out_sem.at[step])
        )
        stores[-1].start()
    for store in stores:
        store.wait()


def attention(recv, queries, dout, holder, rank, slot_of, tile_docs, tile_rows, doc_ends):
    slots, rows = holder.shape[0], queries.shape[0]
    smem = pl.BlockSpec(memory_space=pltpu.SMEM)
    vmem = pl.BlockSpec(memory_space=pltpu.VMEM)
    group = queries.shape[1] // HD
    docs = tile_docs[:, None] == jnp.arange(doc_ends.shape[0], dtype=jnp.int32)[None, :]
    slot_ends = jnp.sum(jnp.where(docs, doc_ends[None, :], 0), axis=1)
    slot_begins = jnp.sum(jnp.where(docs[:, 1:], doc_ends[None, :-1], 0), axis=1)
    text_row = jnp.arange(rows, dtype=jnp.int32)
    seen = (text_row[None, :] >= tile_rows[:, None]) & (text_row[None, :] < slot_ends[:, None])
    bias = jnp.where(seen, 0.0, HIDDEN).astype(F32)
    tile_len = TILE
    chunk_slots = CHUNK // tile_len
    block_begin = jnp.arange(rows * group // BLOCK, dtype=jnp.int32) * (BLOCK // group)
    first = jnp.sum((slot_ends[None, :] <= block_begin[:, None]).astype(jnp.int32), axis=1)
    until = jnp.sum(
        (slot_begins[None, :] < block_begin[:, None] + BLOCK // group).astype(jnp.int32), axis=1
    )
    steps = (until - first + chunk_slots - 1) // chunk_slots

    flat = rows * group
    query_rows = queries.reshape(flat, HD)
    dout_rows = dout.reshape(flat, HD)
    own_row = (jnp.arange(flat, dtype=jnp.int32) // group)[:, None] == text_row[None, :]
    query_rows = jnp.concatenate([query_rows, own_row.astype(BF16)], axis=1)

    key_count = slots * tile_len
    return pl.pallas_call(
        attend_backward,
        out_shape=(
            jax.ShapeDtypeStruct(recv.shape, BF16),
            jax.ShapeDtypeStruct((flat, HD), BF16),
        ),
        in_specs=[smem] * 5 + [vmem] * 4,
        out_specs=(pl.BlockSpec(memory_space=pl.ANY), vmem),
        scratch_shapes=[
            pltpu.VMEM((key_count + CHUNK, 2 * HD), BF16),
            pltpu.VMEM((key_count + CHUNK, HD), BF16),
            pltpu.VMEM((key_count // CHUNK, CHUNK, BLOCK), F32),
            pltpu.VMEM((key_count // CHUNK, CHUNK, BLOCK), F32),
            pltpu.VMEM((key_count // CHUNK, BLOCK), F32),
            pltpu.VMEM((key_count + CHUNK, HD), F32),
            pltpu.VMEM((key_count + CHUNK, HD), F32),
            pltpu.VMEM(recv.shape, BF16),
            pltpu.SemaphoreType.DMA((PARTS,)),
        ],
        compiler_params=pltpu.CompilerParams(vmem_limit_bytes=VMEM_LIMIT),
        name="attend_backward",
    )(holder, rank, slot_of, first, steps, bias, recv, query_rows, dout_rows)


def per_device(queries, keys_in, values_in, dout, req_tiles, tile_docs, tile_rows, doc_ends):
    dp_count = lax.axis_size("dp")
    heads = lax.axis_size("tensor")
    slots = req_tiles.shape[0]
    capacity = slots // dp_count + 1
    row_part = keys_in.shape[1]
    rows = queries.shape[0]
    smem = pl.BlockSpec(memory_space=pltpu.SMEM)
    vmem = pl.BlockSpec(memory_space=pltpu.VMEM)
    hbm = pl.BlockSpec(memory_space=pl.ANY)
    params = pltpu.CompilerParams(vmem_limit_bytes=VMEM_LIMIT)

    holder = req_tiles // slots
    slot_index = jnp.arange(slots, dtype=jnp.int32)
    same_before = (holder[:, None] == holder[None, :]) & (slot_index[None, :] < slot_index[:, None])
    rank = jnp.sum(same_before.astype(jnp.int32), axis=1)
    places = jnp.arange(dp_count, dtype=jnp.int32)[:, None, None]
    ranks = jnp.arange(capacity, dtype=jnp.int32)[None, :, None]
    there = (holder[None, None, :] == places) & (rank[None, None, :] == ranks)
    asked = jnp.sum(jnp.where(there, (req_tiles % slots + 1)[None, None, :], 0), axis=-1) - 1
    slot_of = jnp.sum(jnp.where(there, (slot_index + 1)[None, None, :], 0), axis=-1) - 1
    asked = jnp.pad(asked, ((0, 0), (0, HD - capacity)))[:, None, :]
    wanted = lax.all_to_all(asked, "dp", split_axis=0, concat_axis=0, tiled=True)[:, :, :capacity]

    send = pl.pallas_call(
        pick_tiles,
        out_shape=jax.ShapeDtypeStruct((dp_count * heads, 2 * capacity, row_part, HD), BF16),
        in_specs=[smem, hbm, hbm],
        out_specs=hbm,
        scratch_shapes=[
            pltpu.VMEM(keys_in.shape, BF16),
            pltpu.VMEM(values_in.shape, BF16),
            pltpu.VMEM((dp_count * heads, 2 * capacity, row_part, HD), BF16),
            pltpu.SemaphoreType.DMA((2,)),
            pltpu.SemaphoreType.DMA((PARTS,)),
        ],
        compiler_params=params,
        name="pick_tiles",
    )(wanted, keys_in, values_in)
    recv = lax.all_to_all(send, ("dp", "tensor"), split_axis=0, concat_axis=0, tiled=True)

    back, grad_queries = attention(
        recv, queries, dout, holder, rank, slot_of, tile_docs, tile_rows, doc_ends
    )

    home = lax.all_to_all(back, ("dp", "tensor"), split_axis=0, concat_axis=0, tiled=True)
    tile_index = jnp.arange(slots, dtype=jnp.int32)[:, None, None]
    lines = jnp.arange(dp_count, dtype=jnp.int32)[:, None] * (heads * 2 * capacity) + ranks[:, :, 0]
    source = jnp.sum(jnp.where(wanted[:, 0][None] == tile_index, lines[None], 0), axis=(1, 2))
    grad_keys, grad_values = pl.pallas_call(
        place_tiles,
        out_shape=(
            jax.ShapeDtypeStruct(keys_in.shape, BF16),
            jax.ShapeDtypeStruct(values_in.shape, BF16),
        ),
        in_specs=[smem, vmem],
        out_specs=(hbm, hbm),
        scratch_shapes=[
            pltpu.VMEM(keys_in.shape, BF16),
            pltpu.VMEM(values_in.shape, BF16),
            pltpu.SemaphoreType.DMA((2, PARTS)),
        ],
        compiler_params=params,
        name="place_tiles",
    )(source, home)
    return (grad_queries.reshape(queries.shape), grad_keys, grad_values)


def solution(mesh):
    return jax.shard_map(
        per_device,
        mesh=mesh,
        in_specs=(
            P("dp", "tensor"),
            P("dp", "tensor", None),
            P("dp", "tensor", None),
            P("dp", "tensor"),
            P("dp"),
            P("dp"),
            P("dp"),
            P("dp"),
        ),
        out_specs=(P("dp", "tensor"), P("dp", "tensor", None), P("dp", "tensor", None)),
        check_vma=False,
    )
```

time: 157 us -> 156 us (level)
  Pallas kernels: 19.1 us -> 16.2 us
    pallas_call x1, Pallas kernels: 4.53 us -> 2.3 us  [per_device(): pl.pallas_call(place_tiles, out_shape=(jax.ShapeDtypeStruct(keys_in.shape...]
where the time goes in v3:
time: 156 us; the launch traced here: 155 us
  waiting for transfers between devices  86.8 us (56%)
  starting transfers between devices  24.1 us (15%)
  blocking collectives  20.7 us (13%)
  Pallas kernels  16.2 us (10%)
  local copies, waits for them, and re-layouts  4.55 us (3%)
  other arithmetic  2.01 us (1%)
    all_to_all x1, waiting for transfers between devices, per_device(): lax.all_to_all(back, ('dp', 'tensor'), split_axis=0, concat_axis=0, tiled...  43.6 us
    all_to_all x1, waiting for transfers between devices, per_device(): lax.all_to_all(send, ('dp', 'tensor'), split_axis=0, concat_axis=0, tiled...  43.2 us
    all_to_all x1, blocking collectives, per_device(): lax.all_to_all(asked, 'dp', split_axis=0, concat_axis=0, tiled=True)  20.7 us
    all_to_all x1, starting transfers between devices, per_device(): lax.all_to_all(send, ('dp', 'tensor'), split_axis=0, concat_axis=0, tiled...  14.6 us
    pallas_call x1, Pallas kernels, attention(): pl.pallas_call(attend_backward, out_shape=(jax.ShapeDtypeStruct(recv.shap...  10.5 us
    all_to_all x1, starting transfers between devices, per_device(): lax.all_to_all(back, ('dp', 'tensor'), split_axis=0, concat_axis=0, tiled...  9.5 us
    pallas_call x1, Pallas kernels, per_device(): pl.pallas_call(pick_tiles, out_shape=jax.ShapeDtypeStruct((dp_count * hea...  3.38 us
    unnamed x16, local copies, waits for them, and re-layouts  3.26 us
  transfers between devices with their start and end apart: 2, of which 2 were waited for; matrix products, arithmetic and copies ran while one was open for 1% of the time, Pallas kernels for 0%

profile of v3, /device:TPU:1, one launch (start us, length us, event | category | flops | bytes accessed | tf_op | source)
XLA Modules:
  0.0 155.2 jit_solution(9354544985753571707)
XLA Ops:
  0.6 0.7 fusion.9
  1.3 0.2 convert_reduce_fusion.rank_ref
  1.5 0.2 fusion.2
  1.7 0.1 copy.19
  1.8 20.7 %all_to_all.15 = s32[64,1,128]{2,1,0:T(1,128)S(1)} all-to-all(s32[64,1,128]{2,1,0:T(1,128)S(1)} %copy.19), channel_id=1, replica_groups=mesh['dp'=64,'tensor'=8] {'dp'}, dimensions={0} | all-to-all | bytes 65536 | tf_op jit(solution)/shard_map/all_to_all | solution.py:308
  22.5 1.0 copy-done.1
  23.5 1.0 copy-done.2
  24.6 3.4 %pick_tiles.1 = bf16[512,6,2,128]{3,2,1,0:T(2,128)(2,1)} custom-call(s32[64,1,3]{2,1,0:T(1,128)S(1)} %bitcast.5, bf16[128,2,1024]{2,1,0:T(2,128)(2,1)S(1)} %copy-done.1, bf16[128,2,1024]{2,1,0:T(2,128)(2,1)S(1)} %copy-done.2), custom_call_target="tpu_custom_call" | custom-call | tf_op jit(solution)/shard_map/pick_tiles/pallas_call | solution.py:310
  28.0 0.0 copy-start.3
  28.0 0.0 copy-start.4
  28.0 0.0 copy-start.6
  28.0 0.0 copy-start.7
  28.0 14.6 %all-to-all-start.1 = ((bf16[512,6,2,128]{3,2,1,0:T(2,128)(2,1)}), bf16[512,6,2,128]{3,2,1,0:T(2,128)(2,1)S(1)}, u32[]{:S(2)}, u32[]{:S(2)}) async-start(bf16[512,6,2,128]{3,2,1,0:T(2,128)(2,1)} %pick_tiles.1), calls=%async_computation.1 | async-start | bytes 3145728 | tf_op jit(solution)/shard_map/all_to_all | solution.py:325
  42.6 0.0 copy-start.5
  42.6 0.1 copy.17
  42.7 0.1 reshape.121
  42.9 0.1 reshape.122.dout_ref
  43.0 0.1 select_reduce_fusion.2
  43.1 0.1 select_reduce_fusion.1
  43.2 0.2 convert_reduce_fusion.1
  43.4 0.2 fusion
  43.6 0.1 pad_maximum_fusion.queries_ref
  43.8 0.1 fusion.5.bias_ref
  43.9 43.2 %all-to-all-done.1.recv_ref = bf16[512,6,2,128]{3,2,1,0:T(2,128)(2,1)S(1)} async-done(((bf16[512,6,2,128]{3,2,1,0:T(2,128)(2,1)}), bf16[512,6,2,128]{3,2,1,0:T(2,128)(2,1)S(1)}, u32[]{:S(2)}, u32[]{:S(2)}) %all-to-all-start.1) | async-done | bytes 1572896 | tf_op jit(solution)/shard_map/all_to_all | solution.py:325
  87.1 10.5 %attend_backward.1 = (bf16[512,6,2,128]{3,2,1,0:T(2,128)(2,1)S(1)}, bf16[1024,128]{1,0:T(8,128)(2,1)S(1)}) custom-call(s32[128]{0:T(128)S(1)} %get-tuple-element.14.holder_ref, s32[128]{0:T(128)S(1)} %convert_reduce_fusion.rank_ref, s32[64,3]{1,0:T(8,128)S(1)} %broadcast_add_fusion.slot_ref, s32[4]{0:T(128)S(1)} %get-tuple-element.17.first_ref, ...), custom_call_target="tpu_custom_call" | custom-call | tf_op jit(solution)/shard_map/attend_backward/pallas_call | solution.py:262
  97.6 1.1 copy-done
  98.8 9.5 %all-to-all-start.2 = ((bf16[512,6,2,128]{3,2,1,0:T(2,128)(2,1)}), bf16[512,6,2,128]{3,2,1,0:T(2,128)(2,1)S(1)}, u32[]{:S(2)}, u32[]{:S(2)}) async-start(bf16[512,6,2,128]{3,2,1,0:T(2,128)(2,1)} %copy-done), calls=%async_computation.2 | async-start | bytes 3145728 | tf_op jit(solution)/shard_map/all_to_all | solution.py:331
  108.3 0.1 copy.20
  108.4 0.1 select_reduce_fusion.source_ref
  108.5 0.8 reshape.123
  109.3 43.6 %all-to-all-done.2.home_ref = bf16[512,6,2,128]{3,2,1,0:T(2,128)(2,1)S(1)} async-done(((bf16[512,6,2,128]{3,2,1,0:T(2,128)(2,1)}), bf16[512,6,2,128]{3,2,1,0:T(2,128)(2,1)S(1)}, u32[]{:S(2)}, u32[]{:S(2)}) %all-to-all-start.2) | async-done | bytes 1572896 | tf_op jit(solution)/shard_map/all_to_all | solution.py:331
  152.9 2.3 %place_tiles.1 = (bf16[128,2,1024]{2,1,0:T(2,128)(2,1)}, bf16[128,2,1024]{2,1,0:T(2,128)(2,1)}) custom-call(s32[128]{0:T(128)S(1)} %select_reduce_fusion.source_ref, bf16[512,6,2,128]{3,2,1,0:T(2,128)(2,1)S(1)} %all-to-all-done.2.home_ref), custom_call_target="tpu_custom_call" | custom-call | tf_op jit(solution)/shard_map/place_tiles/pallas_call | solution.py:335
  (20 shorter events, 0.1 us)
Async XLA Ops:
  22.5 1.0 copy-start.1
  23.5 1.0 copy-start.2
  28.0 14.7 %copy-start.3 = (bf16[128,1024]{1,0:T(8,128)(2,1)S(1)}, bf16[128,1024]{1,0:T(8,128)(2,1)}, u32[]{:S(2)}) copy-start(bf16[128,1024]{1,0:T(8,128)(2,1)} %param.8) | copy-start | bytes 786436
  28.0 14.9 %copy-start.4 = (bf16[128,1024]{1,0:T(8,128)(2,1)S(1)}, bf16[128,1024]{1,0:T(8,128)(2,1)}, u32[]{:S(2)}) copy-start(bf16[128,1024]{1,0:T(8,128)(2,1)} %param.11) | copy-start | bytes 786436
  28.0 15.0 %copy-start.6 = (s32[8]{0:T(128)S(1)}, s32[8]{0:T(128)}, u32[]{:S(2)}) copy-start(s32[8]{0:T(128)} %param.15) | copy-start | bytes 100
  28.0 15.0 %copy-start.7 = (s32[128]{0:T(128)S(1)}, s32[128]{0:T(128)}, u32[]{:S(2)}) copy-start(s32[128]{0:T(128)} %param.13) | copy-start | bytes 1540
  28.0 59.1 %all-to-all-start.1 = ((bf16[512,6,2,128]{3,2,1,0:T(2,128)(2,1)}), bf16[512,6,2,128]{3,2,1,0:T(2,128)(2,1)S(1)}, u32[]{:S(2)}, u32[]{:S(2)}) async-start(bf16[512,6,2,128]{3,2,1,0:T(2,128)(2,1)} %pick_tiles.1), calls=%async_computation.1 | async-start | bytes 3145728 | tf_op jit(solution)/shard_map/all_to_all | solution.py:325
  42.6 1.1 copy-start.5
  97.6 1.2 copy-start
  98.8 54.1 %all-to-all-start.2 = ((bf16[512,6,2,128]{3,2,1,0:T(2,128)(2,1)}), bf16[512,6,2,128]{3,2,1,0:T(2,128)(2,1)S(1)}, u32[]{:S(2)}, u32[]{:S(2)}) async-start(bf16[512,6,2,128]{3,2,1,0:T(2,128)(2,1)} %copy-done), calls=%async_computation.2 | async-start | bytes 3145728 | tf_op jit(solution)/shard_map/all_to_all | solution.py:331

commit v4 on v3

--- a/solution.py
+++ b/solution.py
@@ -110,6 +110,7 @@
     top_scr,
     grad_key_scr,
     grad_value_scr,
+    grad_query_scr,
     back_ref,
     out_sem,
 ):
@@ -121,6 +122,7 @@
     pieces = tile_len // recv_ref.shape[2]
     chunk, block = expo_scr.shape[1:]
     blocks = queries_ref.shape[0] // block
+    group = grad_queries_ref.shape[1] // HD
     key_count = slots * tile_len
     tail = pl.ds(key_count, key_scr.shape[0] - key_count)
     contract_last = (((1,), (1,)), ((), ()))
@@ -196,7 +198,11 @@
             )
 
         grad_query = lax.fori_loop(0, steps, backward, jnp.zeros((block, HD), F32))
-        grad_queries_ref[rows, :] = (grad_query * scale).astype(BF16)
+        grad_query_scr[...] = grad_query * scale
+        text_rows = pl.ds(pl.multiple_of(index * (block // group), block // group), block // group)
+        for head in range(group):
+            mine = grad_query_scr[pl.ds(head, block // group, stride=group), :]
+            grad_queries_ref[text_rows, head * HD : (head + 1) * HD] = mine.astype(BF16)
         return carry
 
     lax.fori_loop(0, blocks, one_block, 0)
@@ -232,10 +238,8 @@
         store.wait()
 
 
-def attention(recv, queries, dout, holder, rank, slot_of, tile_docs, tile_rows, doc_ends):
-    slots, rows = holder.shape[0], queries.shape[0]
-    smem = pl.BlockSpec(memory_space=pltpu.SMEM)
-    vmem = pl.BlockSpec(memory_space=pltpu.VMEM)
+def prepare(queries, dout, tile_docs, tile_rows, doc_ends):
+    rows = queries.shape[0]
     group = queries.shape[1] // HD
     docs = tile_docs[:, None] == jnp.arange(doc_ends.shape[0], dtype=jnp.int32)[None, :]
     slot_ends = jnp.sum(jnp.where(docs, doc_ends[None, :], 0), axis=1)
@@ -258,12 +262,20 @@
     own_row = (jnp.arange(flat, dtype=jnp.int32) // group)[:, None] == text_row[None, :]
     query_rows = jnp.concatenate([query_rows, own_row.astype(BF16)], axis=1)
 
-    key_count = slots * tile_len
+    return first, steps, bias, query_rows, dout_rows
+
+
+def attention(recv, holder, rank, slot_of, first, steps, bias, query_rows, dout_rows):
+    smem = pl.BlockSpec(memory_space=pltpu.SMEM)
+    vmem = pl.BlockSpec(memory_space=pltpu.VMEM)
+    slots, rows = bias.shape
+    group = query_rows.shape[0] // rows
+    key_count = slots * TILE
     return pl.pallas_call(
         attend_backward,
         out_shape=(
             jax.ShapeDtypeStruct(recv.shape, BF16),
-            jax.ShapeDtypeStruct((flat, HD), BF16),
+            jax.ShapeDtypeStruct((rows, group * HD), BF16),
         ),
         in_specs=[smem] * 5 + [vmem] * 4,
         out_specs=(pl.BlockSpec(memory_space=pl.ANY), vmem),
@@ -275,6 +287,7 @@
             pltpu.VMEM((key_count // CHUNK, BLOCK), F32),
             pltpu.VMEM((key_count + CHUNK, HD), F32),
             pltpu.VMEM((key_count + CHUNK, HD), F32),
+            pltpu.VMEM((BLOCK, HD), F32),
             pltpu.VMEM(recv.shape, BF16),
             pltpu.SemaphoreType.DMA((PARTS,)),
         ],
@@ -306,6 +319,9 @@
     slot_of = jnp.sum(jnp.where(there, (slot_index + 1)[None, None, :], 0), axis=-1) - 1
     asked = jnp.pad(asked, ((0, 0), (0, HD - capacity)))[:, None, :]
     wanted = lax.all_to_all(asked, "dp", split_axis=0, concat_axis=0, tiled=True)[:, :, :capacity]
+
+    prepared = prepare(queries, dout, tile_docs, tile_rows, doc_ends)
+    wanted, prepared = lax.optimization_barrier((wanted, prepared))
 
     send = pl.pallas_call(
         pick_tiles,
@@ -324,14 +340,13 @@
     )(wanted, keys_in, values_in)
     recv = lax.all_to_all(send, ("dp", "tensor"), split_axis=0, concat_axis=0, tiled=True)
 
-    back, grad_queries = attention(
-        recv, queries, dout, holder, rank, slot_of, tile_docs, tile_rows, doc_ends
-    )
-
-    home = lax.all_to_all(back, ("dp", "tensor"), split_axis=0, concat_axis=0, tiled=True)
     tile_index = jnp.arange(slots, dtype=jnp.int32)[:, None, None]
     lines = jnp.arange(dp_count, dtype=jnp.int32)[:, None] * (heads * 2 * capacity) + ranks[:, :, 0]
     source = jnp.sum(jnp.where(wanted[:, 0][None] == tile_index, lines[None], 0), axis=(1, 2))
+    recv, source = lax.optimization_barrier((recv, source))
+    back, grad_queries = attention(recv, holder, rank, slot_of, *prepared)
+
+    home = lax.all_to_all(back, ("dp", "tensor"), split_axis=0, concat_axis=0, tiled=True)
     grad_keys, grad_values = pl.pallas_call(
         place_tiles,
         out_shape=(
@@ -348,7 +363,7 @@
         compiler_params=params,
         name="place_tiles",
     )(source, home)
-    return (grad_queries.reshape(queries.shape), grad_keys, grad_values)
+    return (grad_queries, grad_keys, grad_values)
 
 
 def solution(mesh):

time: 156 us -> 156 us (level)
  waiting for transfers between devices: 86.8 us -> 49.1 us
  blocking collectives: 20.7 us -> 53.5 us
  starting transfers between devices: 24.1 us -> 27.6 us
  Pallas kernels: 16.2 us -> 17.8 us
    all_to_all x1, waiting for transfers between devices: 43.6 us -> 4.91 us  [per_device(): lax.all_to_all(asked, 'dp', split_axis=0, concat_axis=0, tiled=True)]
    all_to_all x1, blocking collectives: 20.7 us -> 53.5 us  [per_device(): lax.all_to_all(back, ('dp', 'tensor'), split_axis=0, concat_axis=0, tiled...]
    unnamed x16 -> x8, local copies, waits for them, and re-layouts: 3.26 us -> 0.02 us
    all_to_all x1, starting transfers between devices: 9.5 us -> 11.6 us  [per_device(): lax.all_to_all(asked, 'dp', split_axis=0, concat_axis=0, tiled=True)]
    pallas_call x1, Pallas kernels: 10.5 us -> 12.1 us  [attention(): pl.pallas_call(attend_backward, out_shape=(jax.ShapeDtypeStruct(recv.shap...]
  transfers between devices with their start and end apart: 2 -> 2, of which waited for: 2 -> 2; matrix products, arithmetic and copies ran while one was open for 1% -> 3% of each run, Pallas kernels for 0% -> 0%
where the time goes in v4:
time: 156 us; the launch traced here: 155 us
  blocking collectives  53.5 us (34%)
  waiting for transfers between devices  49.1 us (31%)
  starting transfers between devices  27.6 us (18%)
  Pallas kernels  17.8 us (11%)
  other arithmetic  3.39 us (2%)
  local copies, waits for them, and re-layouts  3.02 us (2%)
    all_to_all x1, blocking collectives, per_device(): lax.all_to_all(back, ('dp', 'tensor'), split_axis=0, concat_axis=0, tiled...  53.5 us
    all_to_all x1, waiting for transfers between devices, per_device(): lax.all_to_all(send, ('dp', 'tensor'), split_axis=0, concat_axis=0, tiled...  44.1 us
    all_to_all x1, starting transfers between devices, per_device(): lax.all_to_all(send, ('dp', 'tensor'), split_axis=0, concat_axis=0, tiled...  16 us
    pallas_call x1, Pallas kernels, attention(): pl.pallas_call(attend_backward, out_shape=(jax.ShapeDtypeStruct(recv.shap...  12.1 us
    all_to_all x1, starting transfers between devices, per_device(): lax.all_to_all(asked, 'dp', split_axis=0, concat_axis=0, tiled=True)  11.6 us
    all_to_all x1, waiting for transfers between devices, per_device(): lax.all_to_all(asked, 'dp', split_axis=0, concat_axis=0, tiled=True)  4.91 us
    pallas_call x1, Pallas kernels, per_device(): pl.pallas_call(pick_tiles, out_shape=jax.ShapeDtypeStruct((dp_count * hea...  3.38 us
  transfers between devices with their start and end apart: 2, of which 2 were waited for; matrix products, arithmetic and copies ran while one was open for 3% of the time, Pallas kernels for 0%

profile of v4, /device:TPU:1, one launch (start us, length us, event | category | flops | bytes accessed | tf_op | source)
XLA Modules:
  0.0 155.2 jit_solution(3523622284833333504)
XLA Ops:
  0.6 0.0 copy-start.3
  0.6 0.0 copy-start.2
  0.7 0.0 copy-start.1
  0.7 0.0 copy-start
  0.7 0.8 fusion.9
  1.4 0.2 convert_reduce_fusion.rank_ref
  1.6 0.2 fusion.2
  1.9 0.7 copy.19
  2.6 11.6 %all-to-all-start = ((s32[64,1,128]{2,1,0:T(1,128)}), s32[64,1,128]{2,1,0:T(1,128)S(1)}, u32[]{:S(2)}, u32[]{:S(2)}) async-start(s32[64,1,128]{2,1,0:T(1,128)} %copy.19), calls=%async_computation | async-start | bytes 65536 | tf_op jit(solution)/shard_map/all_to_all | solution.py:321
  14.2 0.7 iota_compare_fusion.6
  14.9 0.8 select_reduce_fusion.2
  15.6 0.2 fusion
  15.8 1.1 reshape.118
  16.9 1.1 reshape.119.dout_ref
  18.0 0.0 copy-done.3
  18.0 0.1 select_reduce_fusion.1
  18.1 0.0 copy-done.2
  18.1 0.1 fusion.5.bias_ref
  18.2 0.2 convert_reduce_fusion.1
  18.4 0.1 pad_maximum_fusion.queries_ref
  18.5 4.9 %all-to-all-done = s32[64,1,128]{2,1,0:T(1,128)S(1)} async-done(((s32[64,1,128]{2,1,0:T(1,128)}), s32[64,1,128]{2,1,0:T(1,128)S(1)}, u32[]{:S(2)}, u32[]{:S(2)}) %all-to-all-start) | async-done | bytes 32800 | tf_op jit(solution)/shard_map/all_to_all | solution.py:321
  23.4 0.0 copy-done.1
  23.4 0.0 copy-done
  23.4 3.4 %pick_tiles.1 = bf16[512,6,2,128]{3,2,1,0:T(2,128)(2,1)} custom-call(s32[64,1,3]{2,1,0:T(1,128)S(1)} %bitcast.5, bf16[128,2,1024]{2,1,0:T(2,128)(2,1)S(1)} %copy-done, bf16[128,2,1024]{2,1,0:T(2,128)(2,1)S(1)} %copy-done.1), custom_call_target="tpu_custom_call" | custom-call | tf_op jit(solution)/shard_map/pick_tiles/pallas_call | solution.py:326
  26.8 16.0 %all-to-all-start.1 = ((bf16[512,6,2,128]{3,2,1,0:T(2,128)(2,1)}), bf16[512,6,2,128]{3,2,1,0:T(2,128)(2,1)S(1)}, u32[]{:S(2)}, u32[]{:S(2)}) async-start(bf16[512,6,2,128]{3,2,1,0:T(2,128)(2,1)} %pick_tiles.1), calls=%async_computation.1 | async-start | bytes 3145728 | tf_op jit(solution)/shard_map/all_to_all | solution.py:341
  42.8 0.1 copy.17
  42.9 0.1 copy.20
  43.0 0.1 select_reduce_fusion.source_ref
  43.1 44.1 %all-to-all-done.1.recv_ref = bf16[512,6,2,128]{3,2,1,0:T(2,128)(2,1)S(1)} async-done(((bf16[512,6,2,128]{3,2,1,0:T(2,128)(2,1)}), bf16[512,6,2,128]{3,2,1,0:T(2,128)(2,1)S(1)}, u32[]{:S(2)}, u32[]{:S(2)}) %all-to-all-start.1) | async-done | bytes 1572896 | tf_op jit(solution)/shard_map/all_to_all | solution.py:341
  87.3 12.1 %attend_backward.1 = (bf16[512,6,2,128]{3,2,1,0:T(2,128)(2,1)S(1)}, bf16[128,1024]{1,0:T(8,128)(2,1)}) custom-call(s32[128]{0:T(128)S(1)} %get-tuple-element.30.holder_ref, s32[128]{0:T(128)S(1)} %convert_reduce_fusion.rank_ref, s32[64,3]{1,0:T(8,128)S(1)} %broadcast_add_fusion.slot_ref, s32[4]{0:T(128)S(1)} %get-tuple-element.15.first_ref, ...), custom_call_target="tpu_custom_call" | custom-call | tf_op jit(solution)/shard_map/attend_backward/pallas_call | solution.py:274
  99.4 53.5 %all_to_all.15.home_ref = bf16[512,6,2,128]{3,2,1,0:T(2,128)(2,1)S(1)} all-to-all(bf16[512,6,2,128]{3,2,1,0:T(2,128)(2,1)S(1)} %get-tuple-element.24), channel_id=1, replica_groups=mesh['dp'=64,'tensor'=8] {'dp','tensor'}, dimensions={0} | all-to-all | bytes 3145728 | tf_op jit(solution)/shard_map/all_to_all | solution.py:349
  152.9 2.3 %place_tiles.1 = (bf16[128,2,1024]{2,1,0:T(2,128)(2,1)}, bf16[128,2,1024]{2,1,0:T(2,128)(2,1)}) custom-call(s32[128]{0:T(128)S(1)} %select_reduce_fusion.source_ref, bf16[512,6,2,128]{3,2,1,0:T(2,128)(2,1)S(1)} %all_to_all.15.home_ref), custom_call_target="tpu_custom_call" | custom-call | tf_op jit(solution)/shard_map/place_tiles/pallas_call | solution.py:350
  (11 shorter events, 0.1 us)
Async XLA Ops:
  0.6 17.3 %copy-start.3 = (s32[8]{0:T(128)S(1)}, s32[8]{0:T(128)}, u32[]{:S(2)}) copy-start(s32[8]{0:T(128)} %param.15) | copy-start | bytes 100
  0.6 17.4 %copy-start.2 = (s32[128]{0:T(128)S(1)}, s32[128]{0:T(128)}, u32[]{:S(2)}) copy-start(s32[128]{0:T(128)} %param.14) | copy-start | bytes 1540
  0.7 22.7 %copy-start.1 = (bf16[128,2,1024]{2,1,0:T(2,128)(2,1)S(1)}, bf16[128,2,1024]{2,1,0:T(2,128)(2,1)}, u32[]{:S(2)}) copy-start(bf16[128,2,1024]{2,1,0:T(2,128)(2,1)} %values_hbm.1) | copy-start | bytes 1572868
  0.7 22.7 %copy-start = (bf16[128,2,1024]{2,1,0:T(2,128)(2,1)S(1)}, bf16[128,2,1024]{2,1,0:T(2,128)(2,1)}, u32[]{:S(2)}) copy-start(bf16[128,2,1024]{2,1,0:T(2,128)(2,1)} %keys_hbm.1) | copy-start | bytes 1572868
  2.6 20.8 %all-to-all-start = ((s32[64,1,128]{2,1,0:T(1,128)}), s32[64,1,128]{2,1,0:T(1,128)S(1)}, u32[]{:S(2)}, u32[]{:S(2)}) async-start(s32[64,1,128]{2,1,0:T(1,128)} %copy.19), calls=%async_computation | async-start | bytes 65536 | tf_op jit(solution)/shard_map/all_to_all | solution.py:321
  26.8 60.5 %all-to-all-start.1 = ((bf16[512,6,2,128]{3,2,1,0:T(2,128)(2,1)}), bf16[512,6,2,128]{3,2,1,0:T(2,128)(2,1)S(1)}, u32[]{:S(2)}, u32[]{:S(2)}) async-start(bf16[512,6,2,128]{3,2,1,0:T(2,128)(2,1)} %pick_tiles.1), calls=%async_computation.1 | async-start | bytes 3145728 | tf_op jit(solution)/shard_map/all_to_all | solution.py:341

commit v5 on v4

--- a/solution.py
+++ b/solution.py
@@ -101,7 +101,7 @@
     recv_ref,
     queries_ref,
     dout_ref,
-    back_hbm,
+    back_ref,
     grad_queries_ref,
     key_scr,
     value_scr,
@@ -110,9 +110,6 @@
     top_scr,
     grad_key_scr,
     grad_value_scr,
-    grad_query_scr,
-    back_ref,
-    out_sem,
 ):
     scale = 1.0 / math.sqrt(HD)
     rate = scale * math.log2(math.e)
@@ -123,6 +120,7 @@
     chunk, block = expo_scr.shape[1:]
     blocks = queries_ref.shape[0] // block
     group = grad_queries_ref.shape[1] // HD
+    span = block // group
     key_count = slots * tile_len
     tail = pl.ds(key_count, key_scr.shape[0] - key_count)
     contract_last = (((1,), (1,)), ((), ()))
@@ -198,44 +196,32 @@
             )
 
         grad_query = lax.fori_loop(0, steps, backward, jnp.zeros((block, HD), F32))
-        grad_query_scr[...] = grad_query * scale
-        text_rows = pl.ds(pl.multiple_of(index * (block // group), block // group), block // group)
+        grad_query = (grad_query * scale).astype(BF16)
+        text_rows = pl.ds(pl.multiple_of(index * span, span), span)
         for head in range(group):
-            mine = grad_query_scr[pl.ds(head, block // group, stride=group), :]
-            grad_queries_ref[text_rows, head * HD : (head + 1) * HD] = mine.astype(BF16)
+            mine = grad_query[head * span : (head + 1) * span]
+            grad_queries_ref[text_rows, head * HD : (head + 1) * HD] = mine
         return carry
 
     lax.fori_loop(0, blocks, one_block, 0)
 
-    part = slot_ref.shape[0] // PARTS
-    stores = []
-    for step in range(PARTS):
-
-        def return_tiles(offset, carry):
-            holder = step * part + offset
-
-            def one_tile(rank):
-                slot = jnp.maximum(slot_ref[holder, rank], 0)
-                where = pl.ds(pl.multiple_of(slot * tile_len, tile_len), tile_len)
-                chunks = pl.ds(holder * pieces, pieces)
-                shape = (pieces, tile_len // pieces, HD)
-                grad_key = (grad_key_scr[where, :] * scale).astype(BF16)
-                back_ref[chunks, rank] = grad_key.reshape(shape)
-                grad_value = grad_value_scr[where, :].astype(BF16)
-                back_ref[chunks, capacity + rank] = grad_value.reshape(shape)
-
-            for rank in range(capacity):
-                one_tile(rank)
-            return carry
-
-        lax.fori_loop(0, part, return_tiles, 0, unroll=4)
-        chunks = pl.ds(step * part * pieces, part * pieces)
-        stores.append(
-            pltpu.make_async_copy(back_ref.at[chunks], back_hbm.at[chunks], out_sem.at[step])
-        )
-        stores[-1].start()
-    for store in stores:
-        store.wait()
+    def return_tiles(holder, carry):
+        chunks = pl.ds(holder * pieces, pieces)
+        shape = (pieces, tile_len // pieces, HD)
+        for rank in range(capacity):
+            slot = jnp.maximum(slot_ref[holder, rank], 0)
+            where = pl.ds(pl.multiple_of(slot * tile_len, tile_len), tile_len)
+            grad_key = (grad_key_scr[where, :] * scale).astype(BF16)
+            back_ref[chunks, rank] = grad_key.reshape(shape)
+            back_ref[chunks, capacity + rank] = grad_value_scr[where, :].astype(BF16).reshape(shape)
+        return carry
+
+    lax.fori_loop(0, slot_ref.shape[0], return_tiles, 0, unroll=4)
+
+
+def by_block(rows, span):
+    blocks = rows.reshape(rows.shape[0] // span, span, rows.shape[1] // HD, HD)
+    return blocks.transpose(0, 2, 1, 3).reshape(-1, HD)
 
 
 def prepare(queries, dout, tile_docs, tile_rows, doc_ends):
@@ -257,9 +243,12 @@
     steps = (until - first + chunk_slots - 1) // chunk_slots
 
     flat = rows * group
-    query_rows = queries.reshape(flat, HD)
-    dout_rows = dout.reshape(flat, HD)
-    own_row = (jnp.arange(flat, dtype=jnp.int32) // group)[:, None] == text_row[None, :]
+    span = BLOCK // group
+    query_rows = by_block(queries, span)
+    dout_rows = by_block(dout, span)
+    position = jnp.arange(flat, dtype=jnp.int32)
+    own = position // BLOCK * span + position % span
+    own_row = own[:, None] == text_row[None, :]
     query_rows = jnp.concatenate([query_rows, own_row.astype(BF16)], axis=1)
 
     return first, steps, bias, query_rows, dout_rows
@@ -278,7 +267,7 @@
             jax.ShapeDtypeStruct((rows, group * HD), BF16),
         ),
         in_specs=[smem] * 5 + [vmem] * 4,
-        out_specs=(pl.BlockSpec(memory_space=pl.ANY), vmem),
+        out_specs=(vmem, vmem),
         scratch_shapes=[
             pltpu.VMEM((key_count + CHUNK, 2 * HD), BF16),
             pltpu.VMEM((key_count + CHUNK, HD), BF16),
@@ -287,9 +276,6 @@
             pltpu.VMEM((key_count // CHUNK, BLOCK), F32),
             pltpu.VMEM((key_count + CHUNK, HD), F32),
             pltpu.VMEM((key_count + CHUNK, HD), F32),
-            pltpu.VMEM((BLOCK, HD), F32),
-            pltpu.VMEM(recv.shape, BF16),
-            pltpu.SemaphoreType.DMA((PARTS,)),
         ],
         compiler_params=pltpu.CompilerParams(vmem_limit_bytes=VMEM_LIMIT),
         name="attend_backward",

time: 156 us -> 154 us (0.987)
    reshape x2, local copies, waits for them, and re-layouts: 2.13 us -> 0.09 us  [by_block(): blocks = rows.reshape(rows.shape[0] // span, span, rows.shape[1] // HD, HD)]
  transfers between devices with their start and end apart: 2 -> 2, of which waited for: 2 -> 2; matrix products, arithmetic and copies ran while one was open for 3% -> 2% of each run, Pallas kernels for 0% -> 0%
where the time goes in v5:
time: 154 us; the launch traced here: 153 us
  blocking collectives  53.5 us (35%)
  waiting for transfers between devices  49.9 us (32%)
  starting transfers between devices  26.7 us (17%)
  Pallas kernels  16.9 us (11%)
  other arithmetic  3.35 us (2%)
  local copies, waits for them, and re-layouts  2.11 us (1%)
    all_to_all x1, blocking collectives, per_device(): lax.all_to_all(back, ('dp', 'tensor'), split_axis=0, concat_axis=0, tiled...  53.5 us
    all_to_all x1, waiting for transfers between devices, per_device(): lax.all_to_all(send, ('dp', 'tensor'), split_axis=0, concat_axis=0, tiled...  44.1 us
    all_to_all x1, starting transfers between devices, per_device(): lax.all_to_all(send, ('dp', 'tensor'), split_axis=0, concat_axis=0, tiled...  15.1 us
    all_to_all x1, starting transfers between devices, per_device(): lax.all_to_all(asked, 'dp', split_axis=0, concat_axis=0, tiled=True)  11.6 us
    pallas_call x1, Pallas kernels, attention(): pl.pallas_call(attend_backward, out_shape=(jax.ShapeDtypeStruct(recv.shap...  11.2 us
    all_to_all x1, waiting for transfers between devices, per_device(): lax.all_to_all(asked, 'dp', split_axis=0, concat_axis=0, tiled=True)  5.77 us
    pallas_call x1, Pallas kernels, per_device(): pl.pallas_call(pick_tiles, out_shape=jax.ShapeDtypeStruct((dp_count * hea...  3.38 us
  transfers between devices with their start and end apart: 2, of which 2 were waited for; matrix products, arithmetic and copies ran while one was open for 2% of the time, Pallas kernels for 0%

profile of v5, /device:TPU:1, one launch (start us, length us, event | category | flops | bytes accessed | tf_op | source)
XLA Modules:
  0.0 153.4 jit_solution(1975173605019243924)
XLA Ops:
  0.6 0.0 copy-start.4
  0.6 0.0 copy-start.2
  0.7 0.0 copy-start.3
  0.7 0.7 fusion.16
  1.4 0.2 convert_reduce_fusion.rank_ref
  1.6 0.2 fusion.2
  1.8 0.7 copy.25
  2.5 11.6 %all-to-all-start = ((s32[64,1,128]{2,1,0:T(1,128)}), s32[64,1,128]{2,1,0:T(1,128)S(1)}, u32[]{:S(2)}, u32[]{:S(2)}) async-start(s32[64,1,128]{2,1,0:T(1,128)} %copy.25), calls=%async_computation | async-start | bytes 65536 | tf_op jit(solution)/shard_map/all_to_all | solution.py:307
  14.2 0.7 iota_compare_fusion.6
  14.8 0.8 select_reduce_fusion.2
  15.6 0.2 fusion
  15.8 0.0 copy-start
  15.8 0.0 copy-start.1
  15.8 1.1 copy.29
  16.9 0.0 copy-done.2
  17.1 0.0 copy-done.4
  17.1 0.1 select_reduce_fusion.1
  17.2 0.0 copy-done.3
  17.2 0.1 fusion.5.bias_ref
  17.3 0.2 convert_reduce_fusion.1
  17.5 0.1 pad_maximum_fusion.queries_ref
  17.6 5.8 %all-to-all-done = s32[64,1,128]{2,1,0:T(1,128)S(1)} async-done(((s32[64,1,128]{2,1,0:T(1,128)}), s32[64,1,128]{2,1,0:T(1,128)S(1)}, u32[]{:S(2)}, u32[]{:S(2)}) %all-to-all-start) | async-done | bytes 32800 | tf_op jit(solution)/shard_map/all_to_all | solution.py:307
  23.3 0.0 copy-done
  23.3 3.4 %pick_tiles.1 = bf16[512,6,2,128]{3,2,1,0:T(2,128)(2,1)} custom-call(s32[64,1,3]{2,1,0:T(1,128)S(1)} %bitcast.18, bf16[128,2,1024]{2,1,0:T(2,128)(2,1)S(1)} %copy-done, bf16[128,2,1024]{2,1,0:T(2,128)(2,1)S(1)} %copy-done.1), custom_call_target="tpu_custom_call" | custom-call | tf_op jit(solution)/shard_map/pick_tiles/pallas_call | solution.py:312
  26.7 15.1 %all-to-all-start.1 = ((bf16[512,6,2,128]{3,2,1,0:T(2,128)(2,1)}), bf16[512,6,2,128]{3,2,1,0:T(2,128)(2,1)S(1)}, u32[]{:S(2)}, u32[]{:S(2)}) async-start(bf16[512,6,2,128]{3,2,1,0:T(2,128)(2,1)} %pick_tiles.1), calls=%async_computation.1 | async-start | bytes 3145728 | tf_op jit(solution)/shard_map/all_to_all | solution.py:327
  41.9 0.1 copy.23
  42.0 0.1 copy.28
  42.1 0.1 select_reduce_fusion.source_ref
  42.2 44.1 %all-to-all-done.1.recv_ref = bf16[512,6,2,128]{3,2,1,0:T(2,128)(2,1)S(1)} async-done(((bf16[512,6,2,128]{3,2,1,0:T(2,128)(2,1)}), bf16[512,6,2,128]{3,2,1,0:T(2,128)(2,1)S(1)}, u32[]{:S(2)}, u32[]{:S(2)}) %all-to-all-start.1) | async-done | bytes 1572896 | tf_op jit(solution)/shard_map/all_to_all | solution.py:327
  86.3 11.2 %attend_backward.1 = (bf16[512,6,2,128]{3,2,1,0:T(2,128)(2,1)S(1)}, bf16[128,1024]{1,0:T(8,128)(2,1)}) custom-call(s32[128]{0:T(128)S(1)} %get-tuple-element.30.holder_ref, s32[128]{0:T(128)S(1)} %convert_reduce_fusion.rank_ref, s32[64,3]{1,0:T(8,128)S(1)} %broadcast_add_fusion.slot_ref, s32[4]{0:T(128)S(1)} %get-tuple-element.15.first_ref, ...), custom_call_target="tpu_custom_call" | custom-call | tf_op jit(solution)/shard_map/attend_backward/pallas_call | solution.py:263
  97.5 53.5 %all_to_all.15.home_ref = bf16[512,6,2,128]{3,2,1,0:T(2,128)(2,1)S(1)} all-to-all(bf16[512,6,2,128]{3,2,1,0:T(2,128)(2,1)S(1)} %get-tuple-element.24), channel_id=1, replica_groups=mesh['dp'=64,'tensor'=8] {'dp','tensor'}, dimensions={0} | all-to-all | bytes 3145728 | tf_op jit(solution)/shard_map/all_to_all | solution.py:335
  151.1 2.3 %place_tiles.1 = (bf16[128,2,1024]{2,1,0:T(2,128)(2,1)}, bf16[128,2,1024]{2,1,0:T(2,128)(2,1)}) custom-call(s32[128]{0:T(128)S(1)} %select_reduce_fusion.source_ref, bf16[512,6,2,128]{3,2,1,0:T(2,128)(2,1)S(1)} %all_to_all.15.home_ref), custom_call_target="tpu_custom_call" | custom-call | tf_op jit(solution)/shard_map/place_tiles/pallas_call | solution.py:336
  (15 shorter events, 0.2 us)
Async XLA Ops:
  0.6 16.4 %copy-start.4 = (s32[8]{0:T(128)S(1)}, s32[8]{0:T(128)}, u32[]{:S(2)}) copy-start(s32[8]{0:T(128)} %param.15) | copy-start | bytes 100
  0.6 16.3 %copy-start.2 = (bf16[128,1024]{1,0:T(8,128)(2,1)S(1)}, bf16[128,1024]{1,0:T(8,128)(2,1)}, u32[]{:S(2)}) copy-start(bf16[128,1024]{1,0:T(8,128)(2,1)} %param.11) | copy-start | bytes 786436
  0.7 16.5 %copy-start.3 = (s32[128]{0:T(128)S(1)}, s32[128]{0:T(128)}, u32[]{:S(2)}) copy-start(s32[128]{0:T(128)} %param.14) | copy-start | bytes 1540
  2.5 20.8 %all-to-all-start = ((s32[64,1,128]{2,1,0:T(1,128)}), s32[64,1,128]{2,1,0:T(1,128)S(1)}, u32[]{:S(2)}, u32[]{:S(2)}) async-start(s32[64,1,128]{2,1,0:T(1,128)} %copy.25), calls=%async_computation | async-start | bytes 65536 | tf_op jit(solution)/shard_map/all_to_all | solution.py:307
  15.8 7.6 %copy-start = (bf16[128,2,1024]{2,1,0:T(2,128)(2,1)S(1)}, bf16[128,2,1024]{2,1,0:T(2,128)(2,1)}, u32[]{:S(2)}) copy-start(bf16[128,2,1024]{2,1,0:T(2,128)(2,1)} %keys_hbm.1) | copy-start | bytes 1572868
  15.8 7.5 %copy-start.1 = (bf16[128,2,1024]{2,1,0:T(2,128)(2,1)S(1)}, bf16[128,2,1024]{2,1,0:T(2,128)(2,1)}, u32[]{:S(2)}) copy-start(bf16[128,2,1024]{2,1,0:T(2,128)(2,1)} %values_hbm.1) | copy-start | bytes 1572868
  26.7 59.6 %all-to-all-start.1 = ((bf16[512,6,2,128]{3,2,1,0:T(2,128)(2,1)}), bf16[512,6,2,128]{3,2,1,0:T(2,128)(2,1)S(1)}, u32[]{:S(2)}, u32[]{:S(2)}) async-start(bf16[512,6,2,128]{3,2,1,0:T(2,128)(2,1)} %pick_tiles.1), calls=%async_computation.1 | async-start | bytes 3145728 | tf_op jit(solution)/shard_map/all_to_all | solution.py:327

commit v6 on v5

--- a/solution.py
+++ b/solution.py
@@ -1,3 +1,4 @@
+import functools
 import math
 
 import jax
@@ -16,6 +17,26 @@
 BLOCK = 256
 PARTS = 4
 VMEM_LIMIT = 48 * 1024 * 1024
+
+
+def ask(capacity, list_ref, asked_ref, rank_ref):
+    holders, lanes = asked_ref.shape
+    slots = list_ref.shape[1]
+    tiles = list_ref[...]
+    across = jnp.broadcast_to(tiles // slots, (slots, slots))
+    slot_here = lax.broadcasted_iota(jnp.int32, (slots, slots), 1)
+    slot_before = lax.broadcasted_iota(jnp.int32, (slots, slots), 0)
+    before = (across.T == across) & (slot_before < slot_here)
+    rank = jnp.sum(before.astype(jnp.int32), axis=0, keepdims=True)
+    rank_ref[...] = rank
+    holder = lax.broadcasted_iota(jnp.int32, (holders, slots), 0)
+    lane = lax.broadcasted_iota(jnp.int32, (holders, lanes), 1)
+    asked = jnp.full((holders, lanes), -1, jnp.int32)
+    for step in range(capacity):
+        mine = (across[:holders] == holder) & (rank == step)
+        tile = jnp.sum(jnp.where(mine, tiles % slots + 1, 0), axis=1, keepdims=True) - 1
+        asked = jnp.where(lane == step, tile, asked)
+    asked_ref[...] = asked
 
 
 def pick_tiles(
@@ -94,7 +115,6 @@
 def attend_backward(
     holder_ref,
     rank_ref,
-    slot_ref,
     first_ref,
     steps_ref,
     bias_ref,
@@ -102,7 +122,7 @@
     queries_ref,
     dout_ref,
     back_ref,
-    grad_queries_ref,
+    grad_queries_hbm,
     key_scr,
     value_scr,
     expo_scr,
@@ -110,6 +130,8 @@
     top_scr,
     grad_key_scr,
     grad_value_scr,
+    grad_queries_ref,
+    out_sem,
 ):
     scale = 1.0 / math.sqrt(HD)
     rate = scale * math.log2(math.e)
@@ -145,6 +167,12 @@
     grad_key_scr[...] = jnp.zeros_like(grad_key_scr)
     grad_value_scr[...] = jnp.zeros_like(grad_value_scr)
 
+    def store_queries(index):
+        text_rows = pl.ds(pl.multiple_of(index * span, span), span)
+        return pltpu.make_async_copy(
+            grad_queries_ref.at[text_rows], grad_queries_hbm.at[text_rows], out_sem.at[index]
+        )
+
     def one_block(index, carry):
         rows = pl.ds(pl.multiple_of(index * block, block), block)
         first, steps = first_ref[index], steps_ref[index]
@@ -201,22 +229,23 @@
         for head in range(group):
             mine = grad_query[head * span : (head + 1) * span]
             grad_queries_ref[text_rows, head * HD : (head + 1) * HD] = mine
+        store_queries(index).start()
         return carry
 
     lax.fori_loop(0, blocks, one_block, 0)
 
-    def return_tiles(holder, carry):
-        chunks = pl.ds(holder * pieces, pieces)
+    def return_slot(slot, carry):
+        source = pl.ds(holder_ref[slot] * pieces, pieces)
+        rank = rank_ref[slot]
+        where = pl.ds(pl.multiple_of(slot * tile_len, tile_len), tile_len)
         shape = (pieces, tile_len // pieces, HD)
-        for rank in range(capacity):
-            slot = jnp.maximum(slot_ref[holder, rank], 0)
-            where = pl.ds(pl.multiple_of(slot * tile_len, tile_len), tile_len)
-            grad_key = (grad_key_scr[where, :] * scale).astype(BF16)
-            back_ref[chunks, rank] = grad_key.reshape(shape)
-            back_ref[chunks, capacity + rank] = grad_value_scr[where, :].astype(BF16).reshape(shape)
+        back_ref[source, rank] = (grad_key_scr[where, :] * scale).astype(BF16).reshape(shape)
+        back_ref[source, capacity + rank] = grad_value_scr[where, :].astype(BF16).reshape(shape)
         return carry
 
-    lax.fori_loop(0, slot_ref.shape[0], return_tiles, 0, unroll=4)
+    lax.fori_loop(0, slots, return_slot, 0, unroll=8)
+    for index in range(blocks):
+        store_queries(index).wait()
 
 
 def by_block(rows, span):
@@ -254,7 +283,7 @@
     return first, steps, bias, query_rows, dout_rows
 
 
-def attention(recv, holder, rank, slot_of, first, steps, bias, query_rows, dout_rows):
+def attention(recv, holder, rank, first, steps, bias, query_rows, dout_rows):
     smem = pl.BlockSpec(memory_space=pltpu.SMEM)
     vmem = pl.BlockSpec(memory_space=pltpu.VMEM)
     slots, rows = bias.shape
@@ -266,20 +295,22 @@
             jax.ShapeDtypeStruct(recv.shape, BF16),
             jax.ShapeDtypeStruct((rows, group * HD), BF16),
         ),
-        in_specs=[smem] * 5 + [vmem] * 4,
-        out_specs=(vmem, vmem),
+        in_specs=[smem] * 4 + [vmem] * 4,
+        out_specs=(vmem, pl.BlockSpec(memory_space=pl.ANY)),
         scratch_shapes=[
             pltpu.VMEM((key_count + CHUNK, 2 * HD), BF16),
             pltpu.VMEM((key_count + CHUNK, HD), BF16),
-            pltpu.VMEM((key_count // CHUNK, CHUNK, BLOCK), F32),
-            pltpu.VMEM((key_count // CHUNK, CHUNK, BLOCK), F32),
-            pltpu.VMEM((key_count // CHUNK, BLOCK), F32),
+            pltpu.VMEM((-(-key_count // CHUNK), CHUNK, BLOCK), F32),
+            pltpu.VMEM((-(-key_count // CHUNK), CHUNK, BLOCK), F32),
+            pltpu.VMEM((-(-key_count // CHUNK), BLOCK), F32),
             pltpu.VMEM((key_count + CHUNK, HD), F32),
             pltpu.VMEM((key_count + CHUNK, HD), F32),
+            pltpu.VMEM((rows, group * HD), BF16),
+            pltpu.SemaphoreType.DMA((rows * group // BLOCK,)),
         ],
         compiler_params=pltpu.CompilerParams(vmem_limit_bytes=VMEM_LIMIT),
         name="attend_backward",
-    )(holder, rank, slot_of, first, steps, bias, recv, query_rows, dout_rows)
+    )(holder, rank, first, steps, bias, recv, query_rows, dout_rows)
 
 
 def per_device(queries, keys_in, values_in, dout, req_tiles, tile_docs, tile_rows, doc_ends):
@@ -294,16 +325,19 @@
     hbm = pl.BlockSpec(memory_space=pl.ANY)
     params = pltpu.CompilerParams(vmem_limit_bytes=VMEM_LIMIT)
 
-    holder = req_tiles // slots
-    slot_index = jnp.arange(slots, dtype=jnp.int32)
-    same_before = (holder[:, None] == holder[None, :]) & (slot_index[None, :] < slot_index[:, None])
-    rank = jnp.sum(same_before.astype(jnp.int32), axis=1)
-    places = jnp.arange(dp_count, dtype=jnp.int32)[:, None, None]
+    asked, rank = pl.pallas_call(
+        functools.partial(ask, capacity),
+        out_shape=(
+            jax.ShapeDtypeStruct((dp_count, HD), jnp.int32),
+            jax.ShapeDtypeStruct((1, slots), jnp.int32),
+        ),
+        in_specs=[vmem],
+        out_specs=(vmem, vmem),
+        name="ask",
+    )(req_tiles.reshape(1, slots))
+    holder, rank = req_tiles // slots, rank.reshape(slots)
+    asked = asked[:, None, :]
     ranks = jnp.arange(capacity, dtype=jnp.int32)[None, :, None]
-    there = (holder[None, None, :] == places) & (rank[None, None, :] == ranks)
-    asked = jnp.sum(jnp.where(there, (req_tiles % slots + 1)[None, None, :], 0), axis=-1) - 1
-    slot_of = jnp.sum(jnp.where(there, (slot_index + 1)[None, None, :], 0), axis=-1) - 1
-    asked = jnp.pad(asked, ((0, 0), (0, HD - capacity)))[:, None, :]
     wanted = lax.all_to_all(asked, "dp", split_axis=0, concat_axis=0, tiled=True)[:, :, :capacity]
 
     prepared = prepare(queries, dout, tile_docs, tile_rows, doc_ends)
@@ -330,7 +364,7 @@
     lines = jnp.arange(dp_count, dtype=jnp.int32)[:, None] * (heads * 2 * capacity) + ranks[:, :, 0]
     source = jnp.sum(jnp.where(wanted[:, 0][None] == tile_index, lines[None], 0), axis=(1, 2))
     recv, source = lax.optimization_barrier((recv, source))
-    back, grad_queries = attention(recv, holder, rank, slot_of, *prepared)
+    back, grad_queries = attention(recv, holder, rank, *prepared)
 
     home = lax.all_to_all(back, ("dp", "tensor"), split_axis=0, concat_axis=0, tiled=True)
     grad_keys, grad_values = pl.pallas_call(

time: 154 us -> 152 us (0.987)
    pallas_call x0 -> x1, Pallas kernels: none -> 1.59 us  [per_device(): pl.pallas_call(functools.partial(ask, capacity), out_shape=(jax.ShapeDtyp...]
where the time goes in v6:
time: 152 us
  blocking collectives  53.6 us (35%)
  waiting for transfers between devices  50 us (33%)
  starting transfers between devices  26.7 us (18%)
  Pallas kernels  17.1 us (11%)
  other arithmetic  2.26 us (1%)
    all_to_all x1, blocking collectives, per_device(): lax.all_to_all(back, ('dp', 'tensor'), split_axis=0, concat_axis=0, tiled...  53.6 us
    all_to_all x1, waiting for transfers between devices, per_device(): lax.all_to_all(send, ('dp', 'tensor'), split_axis=0, concat_axis=0, tiled...  44.2 us
    all_to_all x1, starting transfers between devices, per_device(): lax.all_to_all(send, ('dp', 'tensor'), split_axis=0, concat_axis=0, tiled...  15.1 us
    all_to_all x1, starting transfers between devices, per_device(): lax.all_to_all(asked, 'dp', split_axis=0, concat_axis=0, tiled=True)  11.6 us
    pallas_call x1, Pallas kernels, attention(): pl.pallas_call(attend_backward, out_shape=(jax.ShapeDtypeStruct(recv.shap...  9.88 us
    all_to_all x1, waiting for transfers between devices, per_device(): lax.all_to_all(asked, 'dp', split_axis=0, concat_axis=0, tiled=True)  5.77 us
    pallas_call x1, Pallas kernels, per_device(): pl.pallas_call(pick_tiles, out_shape=jax.ShapeDtypeStruct((dp_count * hea...  3.38 us
  transfers between devices with their start and end apart: 2, of which 2 were waited for; matrix products, arithmetic and copies ran while one was open for 2% of the time, Pallas kernels for 0%

profile of v6, /device:TPU:1, one launch (start us, length us, event | category | flops | bytes accessed | tf_op | source)
XLA Modules:
  0.0 151.9 jit_solution(7671719866057779861)
XLA Ops:
  0.6 0.0 copy-start.5
  0.6 0.0 copy-start.3
  0.7 0.0 copy-start.4
  0.7 1.6 %ask.1 = (s32[64,128]{1,0:T(8,128)}, s32[1,128]{1,0:T(1,128)}) custom-call(s32[1,128]{1,0:T(1,128)} %bitcast.29), custom_call_target="tpu_custom_call" | custom-call | tf_op jit(solution)/shard_map/ask/pallas_call | solution.py:328
  2.3 11.6 %all-to-all-start = ((s32[64,1,128]{2,1,0:T(1,128)}), s32[64,1,128]{2,1,0:T(1,128)S(1)}, u32[]{:S(2)}, u32[]{:S(2)}) async-start(s32[64,1,128]{2,1,0:T(1,128)} %bitcast.27), calls=%async_computation | async-start | bytes 65536 | tf_op jit(solution)/shard_map/all_to_all | solution.py:341
  13.9 0.7 iota_compare_fusion.4
  14.6 0.8 select_reduce_fusion.2
  15.3 0.2 fusion
  15.5 0.0 copy-start
  15.6 0.0 copy-start.1
  15.6 1.1 copy.16
  16.7 0.0 copy-done.3
  16.8 0.0 copy-done.5
  16.8 0.1 select_reduce_fusion.1
  16.9 0.0 copy-done.4
  16.9 0.1 fusion.2.bias_ref
  17.0 0.2 convert_reduce_fusion
  17.3 0.1 pad_maximum_fusion.queries_ref
  17.3 5.8 %all-to-all-done = s32[64,1,128]{2,1,0:T(1,128)S(1)} async-done(((s32[64,1,128]{2,1,0:T(1,128)}), s32[64,1,128]{2,1,0:T(1,128)S(1)}, u32[]{:S(2)}, u32[]{:S(2)}) %all-to-all-start) | async-done | bytes 32800 | tf_op jit(solution)/shard_map/all_to_all | solution.py:341
  23.1 0.0 copy-done
  23.1 0.0 copy-done.1
  23.1 3.4 %pick_tiles.1 = bf16[512,6,2,128]{3,2,1,0:T(2,128)(2,1)} custom-call(s32[64,1,3]{2,1,0:T(1,128)S(1)} %bitcast.19, bf16[128,2,1024]{2,1,0:T(2,128)(2,1)S(1)} %copy-done, bf16[128,2,1024]{2,1,0:T(2,128)(2,1)S(1)} %copy-done.1), custom_call_target="tpu_custom_call" | custom-call | tf_op jit(solution)/shard_map/pick_tiles/pallas_call | solution.py:346
  26.5 0.0 copy-start.6
  26.5 0.0 copy-start.2
  26.5 15.1 %all-to-all-start.1 = ((bf16[512,6,2,128]{3,2,1,0:T(2,128)(2,1)}), bf16[512,6,2,128]{3,2,1,0:T(2,128)(2,1)S(1)}, u32[]{:S(2)}, u32[]{:S(2)}) async-start(bf16[512,6,2,128]{3,2,1,0:T(2,128)(2,1)} %pick_tiles.1), calls=%async_computation.1 | async-start | bytes 3145728 | tf_op jit(solution)/shard_map/all_to_all | solution.py:361
  41.7 0.0 copy-done.6
  41.7 0.1 copy.15
  41.8 0.1 select_reduce_fusion.source_ref
  41.9 44.2 %all-to-all-done.1.recv_ref = bf16[512,6,2,128]{3,2,1,0:T(2,128)(2,1)S(1)} async-done(((bf16[512,6,2,128]{3,2,1,0:T(2,128)(2,1)}), bf16[512,6,2,128]{3,2,1,0:T(2,128)(2,1)S(1)}, u32[]{:S(2)}, u32[]{:S(2)}) %all-to-all-start.1) | async-done | bytes 1572896 | tf_op jit(solution)/shard_map/all_to_all | solution.py:361
  86.1 9.9 %attend_backward.1 = (bf16[512,6,2,128]{3,2,1,0:T(2,128)(2,1)S(1)}, bf16[128,1024]{1,0:T(8,128)(2,1)}) custom-call(s32[128]{0:T(128)S(1)} %and_select_fusion.1.holder_ref, s32[128]{0:T(128)S(1)} %bitcast.21, s32[4]{0:T(128)S(1)} %get-tuple-element.19.first_ref, s32[4]{0:T(128)S(1)} %and_select_fusion.steps_ref, f32[128,128]{1,0:T(8,128)S(1)} %fusion.2.bias_ref, ...), custom_call_target="tpu_custom_call" | custom-call | tf_op jit(solution)/shard_map/attend_backward/pallas_call | solution.py:292
  96.0 53.6 %all_to_all.15.home_ref = bf16[512,6,2,128]{3,2,1,0:T(2,128)(2,1)S(1)} all-to-all(bf16[512,6,2,128]{3,2,1,0:T(2,128)(2,1)S(1)} %get-tuple-element.28), channel_id=1, replica_groups=mesh['dp'=64,'tensor'=8] {'dp','tensor'}, dimensions={0} | all-to-all | bytes 3145728 | tf_op jit(solution)/shard_map/all_to_all | solution.py:369
  149.6 2.3 %place_tiles.1 = (bf16[128,2,1024]{2,1,0:T(2,128)(2,1)}, bf16[128,2,1024]{2,1,0:T(2,128)(2,1)}) custom-call(s32[128]{0:T(128)S(1)} %select_reduce_fusion.source_ref, bf16[512,6,2,128]{3,2,1,0:T(2,128)(2,1)S(1)} %all_to_all.15.home_ref), custom_call_target="tpu_custom_call" | custom-call | tf_op jit(solution)/shard_map/place_tiles/pallas_call | solution.py:370
  (11 shorter events, 0.2 us)
Async XLA Ops:
  0.6 16.2 %copy-start.5 = (s32[8]{0:T(128)S(1)}, s32[8]{0:T(128)}, u32[]{:S(2)}) copy-start(s32[8]{0:T(128)} %param.15) | copy-start | bytes 100
  0.6 16.1 %copy-start.3 = (bf16[128,1024]{1,0:T(8,128)(2,1)S(1)}, bf16[128,1024]{1,0:T(8,128)(2,1)}, u32[]{:S(2)}) copy-start(bf16[128,1024]{1,0:T(8,128)(2,1)} %param.11) | copy-start | bytes 786436
  0.7 16.3 %copy-start.4 = (s32[128]{0:T(128)S(1)}, s32[128]{0:T(128)}, u32[]{:S(2)}) copy-start(s32[128]{0:T(128)} %param.14) | copy-start | bytes 1540
  2.3 20.8 %all-to-all-start = ((s32[64,1,128]{2,1,0:T(1,128)}), s32[64,1,128]{2,1,0:T(1,128)S(1)}, u32[]{:S(2)}, u32[]{:S(2)}) async-start(s32[64,1,128]{2,1,0:T(1,128)} %bitcast.27), calls=%async_computation | async-start | bytes 65536 | tf_op jit(solution)/shard_map/all_to_all | solution.py:341
  15.5 7.6 %copy-start = (bf16[128,2,1024]{2,1,0:T(2,128)(2,1)S(1)}, bf16[128,2,1024]{2,1,0:T(2,128)(2,1)}, u32[]{:S(2)}) copy-start(bf16[128,2,1024]{2,1,0:T(2,128)(2,1)} %keys_hbm.1) | copy-start | bytes 1572868
  15.6 7.5 %copy-start.1 = (bf16[128,2,1024]{2,1,0:T(2,128)(2,1)S(1)}, bf16[128,2,1024]{2,1,0:T(2,128)(2,1)}, u32[]{:S(2)}) copy-start(bf16[128,2,1024]{2,1,0:T(2,128)(2,1)} %values_hbm.1) | copy-start | bytes 1572868
  26.5 15.2 %copy-start.6 = (s32[128]{0:T(128)S(1)}, s32[128]{0:T(128)}, u32[]{:S(2)}) copy-start(s32[128]{0:T(128)} %param.12) | copy-start | bytes 1540
  26.5 59.6 %copy-start.2 = (s32[1,128]{1,0:T(1,128)S(1)}, s32[1,128]{1,0:T(1,128)}, u32[]{:S(2)}) copy-start(s32[1,128]{1,0:T(1,128)} %get-tuple-element.17) | copy-start | bytes 1540
  26.5 59.6 %all-to-all-start.1 = ((bf16[512,6,2,128]{3,2,1,0:T(2,128)(2,1)}), bf16[512,6,2,128]{3,2,1,0:T(2,128)(2,1)S(1)}, u32[]{:S(2)}, u32[]{:S(2)}) async-start(bf16[512,6,2,128]{3,2,1,0:T(2,128)(2,1)} %pick_tiles.1), calls=%async_computation.1 | async-start | bytes 3145728 | tf_op jit(solution)/shard_map/all_to_all | solution.py:361

commit v7 on v6

--- a/solution.py
+++ b/solution.py
@@ -13,9 +13,9 @@
 BF16 = jnp.bfloat16
 F32 = jnp.float32
 HIDDEN = -1e30
-CHUNK = 512
+CHUNK = 768
 BLOCK = 256
-PARTS = 4
+PARTS = 8
 VMEM_LIMIT = 48 * 1024 * 1024
 
 
@@ -40,19 +40,10 @@
 
 
 def pick_tiles(
-    wanted_ref, keys_hbm, values_hbm, send_hbm, keys_ref, values_ref, send_ref, in_sem, out_sem
+    wanted_ref, keys_ref, values_ref, send_hbm, send_ref, out_sem
 ):
     readers, _, capacity = wanted_ref.shape
     heads = keys_ref.shape[2] // HD
-    loads = [
-        pltpu.make_async_copy(keys_hbm, keys_ref, in_sem.at[0]),
-        pltpu.make_async_copy(values_hbm, values_ref, in_sem.at[1]),
-    ]
-    for load in loads:
-        load.start()
-    for load in loads:
-        load.wait()
-
     part = readers // PARTS
     stores = []
     for step in range(PARTS):
@@ -158,14 +149,16 @@
             BF16
         )
         value_scr[target, :] = recv_ref[source, capacity + rank].reshape(tile_len, HD)
+        grad_key_scr[target, :] = jnp.zeros((tile_len, HD), F32)
+        grad_value_scr[target, :] = jnp.zeros((tile_len, HD), F32)
         return carry
 
     lax.fori_loop(0, slots, gather_slot, 0, unroll=8)
     key_scr[tail, :HD] = jnp.zeros((tail.size, HD), BF16)
     key_scr[tail, HD:] = jnp.full((tail.size, HD), HIDDEN, BF16)
     value_scr[tail, :] = jnp.zeros((tail.size, HD), BF16)
-    grad_key_scr[...] = jnp.zeros_like(grad_key_scr)
-    grad_value_scr[...] = jnp.zeros_like(grad_value_scr)
+    grad_key_scr[tail, :] = jnp.zeros((tail.size, HD), F32)
+    grad_value_scr[tail, :] = jnp.zeros((tail.size, HD), F32)
 
     def store_queries(index):
         text_rows = pl.ds(pl.multiple_of(index * span, span), span)
@@ -346,13 +339,10 @@
     send = pl.pallas_call(
         pick_tiles,
         out_shape=jax.ShapeDtypeStruct((dp_count * heads, 2 * capacity, row_part, HD), BF16),
-        in_specs=[smem, hbm, hbm],
+        in_specs=[smem, vmem, vmem],
         out_specs=hbm,
         scratch_shapes=[
-            pltpu.VMEM(keys_in.shape, BF16),
-            pltpu.VMEM(values_in.shape, BF16),
             pltpu.VMEM((dp_count * heads, 2 * capacity, row_part, HD), BF16),
-            pltpu.SemaphoreType.DMA((2,)),
             pltpu.SemaphoreType.DMA((PARTS,)),
         ],
         compiler_params=params,

time: 152 us -> 152 us (level)
  no operation moved by 1% of the time
where the time goes in v7:
time: 152 us
  blocking collectives  53.4 us (35%)
  waiting for transfers between devices  50 us (33%)
  starting transfers between devices  26.7 us (18%)
  Pallas kernels  17 us (11%)
  other arithmetic  2.26 us (1%)
    all_to_all x1, blocking collectives, per_device(): lax.all_to_all(back, ('dp', 'tensor'), split_axis=0, concat_axis=0, tiled...  53.4 us
    all_to_all x1, waiting for transfers between devices, per_device(): lax.all_to_all(send, ('dp', 'tensor'), split_axis=0, concat_axis=0, tiled...  44.2 us
    all_to_all x1, starting transfers between devices, per_device(): lax.all_to_all(send, ('dp', 'tensor'), split_axis=0, concat_axis=0, tiled...  15.1 us
    all_to_all x1, starting transfers between devices, per_device(): lax.all_to_all(asked, 'dp', split_axis=0, concat_axis=0, tiled=True)  11.6 us
    pallas_call x1, Pallas kernels, attention(): pl.pallas_call(attend_backward, out_shape=(jax.ShapeDtypeStruct(recv.shap...  9.81 us
    all_to_all x1, waiting for transfers between devices, per_device(): lax.all_to_all(asked, 'dp', split_axis=0, concat_axis=0, tiled=True)  5.76 us
    pallas_call x1, Pallas kernels, per_device(): pl.pallas_call(pick_tiles, out_shape=jax.ShapeDtypeStruct((dp_count * hea...  3.29 us
  transfers between devices with their start and end apart: 2, of which 2 were waited for; matrix products, arithmetic and copies ran while one was open for 2% of the time, Pallas kernels for 0%

profile of v7, /device:TPU:1, one launch (start us, length us, event | category | flops | bytes accessed | tf_op | source)
XLA Modules:
  0.0 151.6 jit_solution(5153753123688195266)
XLA Ops:
  0.6 0.0 copy-start.5
  0.6 0.0 copy-start.3
  0.7 0.0 copy-start.4
  0.7 1.6 %ask.1 = (s32[64,128]{1,0:T(8,128)}, s32[1,128]{1,0:T(1,128)}) custom-call(s32[1,128]{1,0:T(1,128)} %bitcast.29), custom_call_target="tpu_custom_call" | custom-call | tf_op jit(solution)/shard_map/ask/pallas_call | solution.py:321
  2.3 11.6 %all-to-all-start = ((s32[64,1,128]{2,1,0:T(1,128)}), s32[64,1,128]{2,1,0:T(1,128)S(1)}, u32[]{:S(2)}, u32[]{:S(2)}) async-start(s32[64,1,128]{2,1,0:T(1,128)} %bitcast.27), calls=%async_computation | async-start | bytes 65536 | tf_op jit(solution)/shard_map/all_to_all | solution.py:334
  13.9 0.7 iota_compare_fusion.4
  14.6 0.8 select_reduce_fusion.2
  15.3 0.2 fusion
  15.5 0.0 copy-start
  15.6 0.0 copy-start.1
  15.6 1.1 copy.16
  16.7 0.0 copy-done.3
  16.8 0.0 copy-done.5
  16.8 0.1 select_reduce_fusion.1
  16.9 0.0 copy-done.4
  16.9 0.1 fusion.2.bias_ref
  17.0 0.2 convert_reduce_fusion
  17.3 0.1 pad_maximum_fusion.queries_ref
  17.3 5.8 %all-to-all-done = s32[64,1,128]{2,1,0:T(1,128)S(1)} async-done(((s32[64,1,128]{2,1,0:T(1,128)}), s32[64,1,128]{2,1,0:T(1,128)S(1)}, u32[]{:S(2)}, u32[]{:S(2)}) %all-to-all-start) | async-done | bytes 32800 | tf_op jit(solution)/shard_map/all_to_all | solution.py:334
  23.1 0.0 copy-done
  23.1 0.0 copy-done.1
  23.1 3.3 %pick_tiles.1 = bf16[512,6,2,128]{3,2,1,0:T(2,128)(2,1)} custom-call(s32[64,1,3]{2,1,0:T(1,128)S(1)} %bitcast.19, bf16[128,2,1024]{2,1,0:T(2,128)(2,1)S(1)} %copy-done, bf16[128,2,1024]{2,1,0:T(2,128)(2,1)S(1)} %copy-done.1), custom_call_target="tpu_custom_call" | custom-call | tf_op jit(solution)/shard_map/pick_tiles/pallas_call | solution.py:339
  26.4 0.0 copy-start.6
  26.4 0.0 copy-start.2
  26.4 15.1 %all-to-all-start.1 = ((bf16[512,6,2,128]{3,2,1,0:T(2,128)(2,1)}), bf16[512,6,2,128]{3,2,1,0:T(2,128)(2,1)S(1)}, u32[]{:S(2)}, u32[]{:S(2)}) async-start(bf16[512,6,2,128]{3,2,1,0:T(2,128)(2,1)} %pick_tiles.1), calls=%async_computation.1 | async-start | bytes 3145728 | tf_op jit(solution)/shard_map/all_to_all | solution.py:351
  41.6 0.0 copy-done.6
  41.6 0.1 copy.15
  41.7 0.1 select_reduce_fusion.source_ref
  41.8 44.2 %all-to-all-done.1.recv_ref = bf16[512,6,2,128]{3,2,1,0:T(2,128)(2,1)S(1)} async-done(((bf16[512,6,2,128]{3,2,1,0:T(2,128)(2,1)}), bf16[512,6,2,128]{3,2,1,0:T(2,128)(2,1)S(1)}, u32[]{:S(2)}, u32[]{:S(2)}) %all-to-all-start.1) | async-done | bytes 1572896 | tf_op jit(solution)/shard_map/all_to_all | solution.py:351
  86.0 9.8 %attend_backward.1 = (bf16[512,6,2,128]{3,2,1,0:T(2,128)(2,1)S(1)}, bf16[128,1024]{1,0:T(8,128)(2,1)}) custom-call(s32[128]{0:T(128)S(1)} %and_select_fusion.1.holder_ref, s32[128]{0:T(128)S(1)} %bitcast.21, s32[4]{0:T(128)S(1)} %get-tuple-element.19.first_ref, s32[4]{0:T(128)S(1)} %and_select_fusion.steps_ref, f32[128,128]{1,0:T(8,128)S(1)} %fusion.2.bias_ref, ...), custom_call_target="tpu_custom_call" | custom-call | tf_op jit(solution)/shard_map/attend_backward/pallas_call | solution.py:285
  95.9 53.4 %all_to_all.15.home_ref = bf16[512,6,2,128]{3,2,1,0:T(2,128)(2,1)S(1)} all-to-all(bf16[512,6,2,128]{3,2,1,0:T(2,128)(2,1)S(1)} %get-tuple-element.28), channel_id=1, replica_groups=mesh['dp'=64,'tensor'=8] {'dp','tensor'}, dimensions={0} | all-to-all | bytes 3145728 | tf_op jit(solution)/shard_map/all_to_all | solution.py:359
  149.3 2.3 %place_tiles.1 = (bf16[128,2,1024]{2,1,0:T(2,128)(2,1)}, bf16[128,2,1024]{2,1,0:T(2,128)(2,1)}) custom-call(s32[128]{0:T(128)S(1)} %select_reduce_fusion.source_ref, bf16[512,6,2,128]{3,2,1,0:T(2,128)(2,1)S(1)} %all_to_all.15.home_ref), custom_call_target="tpu_custom_call" | custom-call | tf_op jit(solution)/shard_map/place_tiles/pallas_call | solution.py:360
  (11 shorter events, 0.2 us)
Async XLA Ops:
  0.6 16.2 %copy-start.5 = (s32[8]{0:T(128)S(1)}, s32[8]{0:T(128)}, u32[]{:S(2)}) copy-start(s32[8]{0:T(128)} %param.15) | copy-start | bytes 100
  0.6 16.1 %copy-start.3 = (bf16[128,1024]{1,0:T(8,128)(2,1)S(1)}, bf16[128,1024]{1,0:T(8,128)(2,1)}, u32[]{:S(2)}) copy-start(bf16[128,1024]{1,0:T(8,128)(2,1)} %param.11) | copy-start | bytes 786436
  0.7 16.3 %copy-start.4 = (s32[128]{0:T(128)S(1)}, s32[128]{0:T(128)}, u32[]{:S(2)}) copy-start(s32[128]{0:T(128)} %param.14) | copy-start | bytes 1540
  2.3 20.8 %all-to-all-start = ((s32[64,1,128]{2,1,0:T(1,128)}), s32[64,1,128]{2,1,0:T(1,128)S(1)}, u32[]{:S(2)}, u32[]{:S(2)}) async-start(s32[64,1,128]{2,1,0:T(1,128)} %bitcast.27), calls=%async_computation | async-start | bytes 65536 | tf_op jit(solution)/shard_map/all_to_all | solution.py:334
  15.5 7.6 %copy-start = (bf16[128,2,1024]{2,1,0:T(2,128)(2,1)S(1)}, bf16[128,2,1024]{2,1,0:T(2,128)(2,1)}, u32[]{:S(2)}) copy-start(bf16[128,2,1024]{2,1,0:T(2,128)(2,1)} %keys_ref.1) | copy-start | bytes 1572868
  15.6 7.5 %copy-start.1 = (bf16[128,2,1024]{2,1,0:T(2,128)(2,1)S(1)}, bf16[128,2,1024]{2,1,0:T(2,128)(2,1)}, u32[]{:S(2)}) copy-start(bf16[128,2,1024]{2,1,0:T(2,128)(2,1)} %values_ref.1) | copy-start | bytes 1572868
  26.4 15.2 %copy-start.6 = (s32[128]{0:T(128)S(1)}, s32[128]{0:T(128)}, u32[]{:S(2)}) copy-start(s32[128]{0:T(128)} %param.12) | copy-start | bytes 1540
  26.4 59.6 %copy-start.2 = (s32[1,128]{1,0:T(1,128)S(1)}, s32[1,128]{1,0:T(1,128)}, u32[]{:S(2)}) copy-start(s32[1,128]{1,0:T(1,128)} %get-tuple-element.17) | copy-start | bytes 1540
  26.4 59.6 %all-to-all-start.1 = ((bf16[512,6,2,128]{3,2,1,0:T(2,128)(2,1)}), bf16[512,6,2,128]{3,2,1,0:T(2,128)(2,1)S(1)}, u32[]{:S(2)}, u32[]{:S(2)}) async-start(bf16[512,6,2,128]{3,2,1,0:T(2,128)(2,1)} %pick_tiles.1), calls=%async_computation.1 | async-start | bytes 3145728 | tf_op jit(solution)/shard_map/all_to_all | solution.py:351

commit v8 on v7

--- a/solution.py
+++ b/solution.py
@@ -19,7 +19,7 @@
 VMEM_LIMIT = 48 * 1024 * 1024
 
 
-def ask(capacity, list_ref, asked_ref, rank_ref):
+def ask(capacity, list_ref, asked_ref, rank_ref, holder_ref):
     holders, lanes = asked_ref.shape
     slots = list_ref.shape[1]
     tiles = list_ref[...]
@@ -29,6 +29,7 @@
     before = (across.T == across) & (slot_before < slot_here)
     rank = jnp.sum(before.astype(jnp.int32), axis=0, keepdims=True)
     rank_ref[...] = rank
+    holder_ref[...] = tiles // slots
     holder = lax.broadcasted_iota(jnp.int32, (holders, slots), 0)
     lane = lax.broadcasted_iota(jnp.int32, (holders, lanes), 1)
     asked = jnp.full((holders, lanes), -1, jnp.int32)
@@ -39,35 +40,19 @@
     asked_ref[...] = asked
 
 
-def pick_tiles(
-    wanted_ref, keys_ref, values_ref, send_hbm, send_ref, out_sem
-):
+def pick_tiles(wanted_ref, keys_ref, values_ref, send_ref):
     readers, _, capacity = wanted_ref.shape
     heads = keys_ref.shape[2] // HD
-    part = readers // PARTS
-    stores = []
-    for step in range(PARTS):
-
-        def one_reader(offset, carry):
-            reader = step * part + offset
-
-            def one_tile(rank):
-                tile = jnp.maximum(wanted_ref[reader, 0, rank], 0)
-                for head in range(heads):
-                    cols = slice(head * HD, (head + 1) * HD)
-                    send_ref[reader * heads + head, rank] = keys_ref[tile, :, cols]
-                    send_ref[reader * heads + head, capacity + rank] = values_ref[tile, :, cols]
-
-            for rank in range(capacity):
-                one_tile(rank)
-            return carry
-
-        lax.fori_loop(0, part, one_reader, 0, unroll=4)
-        rows = pl.ds(step * part * heads, part * heads)
-        stores.append(pltpu.make_async_copy(send_ref.at[rows], send_hbm.at[rows], out_sem.at[step]))
-        stores[-1].start()
-    for store in stores:
-        store.wait()
+    def one_reader(reader, carry):
+        for rank in range(capacity):
+            tile = jnp.maximum(wanted_ref[reader, 0, rank], 0)
+            for head in range(heads):
+                cols = slice(head * HD, (head + 1) * HD)
+                send_ref[reader * heads + head, rank] = keys_ref[tile, :, cols]
+                send_ref[reader * heads + head, capacity + rank] = values_ref[tile, :, cols]
+        return carry
+
+    lax.fori_loop(0, readers, one_reader, 0, unroll=4)
 
 
 def place_tiles(
@@ -318,42 +303,40 @@
     hbm = pl.BlockSpec(memory_space=pl.ANY)
     params = pltpu.CompilerParams(vmem_limit_bytes=VMEM_LIMIT)
 
-    asked, rank = pl.pallas_call(
+    asked, rank, holder = pl.pallas_call(
         functools.partial(ask, capacity),
         out_shape=(
             jax.ShapeDtypeStruct((dp_count, HD), jnp.int32),
             jax.ShapeDtypeStruct((1, slots), jnp.int32),
+            jax.ShapeDtypeStruct((1, slots), jnp.int32),
         ),
         in_specs=[vmem],
-        out_specs=(vmem, vmem),
+        out_specs=(vmem, vmem, vmem),
         name="ask",
     )(req_tiles.reshape(1, slots))
-    holder, rank = req_tiles // slots, rank.reshape(slots)
+    holder, rank = holder.reshape(slots), rank.reshape(slots)
     asked = asked[:, None, :]
     ranks = jnp.arange(capacity, dtype=jnp.int32)[None, :, None]
     wanted = lax.all_to_all(asked, "dp", split_axis=0, concat_axis=0, tiled=True)[:, :, :capacity]
 
     prepared = prepare(queries, dout, tile_docs, tile_rows, doc_ends)
-    wanted, prepared = lax.optimization_barrier((wanted, prepared))
+    tile_index = jnp.arange(slots, dtype=jnp.int32)[:, None, None]
+    lines = jnp.arange(dp_count, dtype=jnp.int32)[:, None] * (heads * 2 * capacity) + ranks[:, :, 0]
+    source = jnp.sum(jnp.where(wanted[:, 0][None] == tile_index, lines[None], 0), axis=(1, 2))
+    wanted, prepared, source, holder, rank = lax.optimization_barrier(
+        (wanted, prepared, source, holder, rank)
+    )
 
     send = pl.pallas_call(
         pick_tiles,
         out_shape=jax.ShapeDtypeStruct((dp_count * heads, 2 * capacity, row_part, HD), BF16),
         in_specs=[smem, vmem, vmem],
-        out_specs=hbm,
-        scratch_shapes=[
-            pltpu.VMEM((dp_count * heads, 2 * capacity, row_part, HD), BF16),
-            pltpu.SemaphoreType.DMA((PARTS,)),
-        ],
+        out_specs=vmem,
         compiler_params=params,
         name="pick_tiles",
     )(wanted, keys_in, values_in)
     recv = lax.all_to_all(send, ("dp", "tensor"), split_axis=0, concat_axis=0, tiled=True)
 
-    tile_index = jnp.arange(slots, dtype=jnp.int32)[:, None, None]
-    lines = jnp.arange(dp_count, dtype=jnp.int32)[:, None] * (heads * 2 * capacity) + ranks[:, :, 0]
-    source = jnp.sum(jnp.where(wanted[:, 0][None] == tile_index, lines[None], 0), axis=(1, 2))
-    recv, source = lax.optimization_barrier((recv, source))
     back, grad_queries = attention(recv, holder, rank, *prepared)
 
     home = lax.all_to_all(back, ("dp", "tensor"), split_axis=0, concat_axis=0, tiled=True)

time: 152 us -> 151 us (level)
  blocking collectives: 53.4 us -> 114 us
  waiting for transfers between devices: 50 us -> 5.75 us
  starting transfers between devices: 26.7 us -> 11.6 us
  Pallas kernels: 17 us -> 15.1 us
    all_to_all x0 -> x1, blocking collectives: none -> 59.4 us  [per_device(): lax.all_to_all(send, ('dp', 'tensor'), split_axis=0, concat_axis=0, tiled...]
    all_to_all x1 -> x0, waiting for transfers between devices: 44.2 us -> none  [per_device(): lax.all_to_all(send, ('dp', 'tensor'), split_axis=0, concat_axis=0, tiled...]
    all_to_all x1 -> x0, starting transfers between devices: 15.1 us -> none  [per_device(): lax.all_to_all(send, ('dp', 'tensor'), split_axis=0, concat_axis=0, tiled...]
  transfers between devices with their start and end apart: 2 -> 1, of which waited for: 2 -> 1; matrix products, arithmetic and copies ran while one was open for 2% -> 2% of each run, Pallas kernels for 0% -> 0%
where the time goes in v8:
time: 151 us
  blocking collectives  114 us (75%)
  Pallas kernels  15.1 us (10%)
  starting transfers between devices  11.6 us (8%)
  waiting for transfers between devices  5.75 us (4%)
  other arithmetic  2.25 us (1%)
    all_to_all x1, blocking collectives, per_device(): lax.all_to_all(send, ('dp', 'tensor'), split_axis=0, concat_axis=0, tiled...  59.4 us
    all_to_all x1, blocking collectives, per_device(): lax.all_to_all(back, ('dp', 'tensor'), split_axis=0, concat_axis=0, tiled...  54.3 us
    all_to_all x1, starting transfers between devices, per_device(): lax.all_to_all(asked, 'dp', split_axis=0, concat_axis=0, tiled=True)  11.6 us
    pallas_call x1, Pallas kernels, attention(): pl.pallas_call(attend_backward, out_shape=(jax.ShapeDtypeStruct(recv.shap...  8.64 us
    all_to_all x1, waiting for transfers between devices, per_device(): lax.all_to_all(asked, 'dp', split_axis=0, concat_axis=0, tiled=True)  5.75 us
  transfers between devices with their start and end apart: 1, of which 1 were waited for; matrix products, arithmetic and copies ran while one was open for 2% of the time, Pallas kernels for 0%

profile of v8, /device:TPU:1, one launch (start us, length us, event | category | flops | bytes accessed | tf_op | source)
XLA Modules:
  0.0 150.6 jit_solution(6944133044682890654)
XLA Ops:
  0.6 0.0 copy-start.6
  0.6 0.0 copy-start.4
  0.7 0.0 copy-start.5
  0.7 1.6 %ask.1 = (s32[64,128]{1,0:T(8,128)}, s32[1,128]{1,0:T(1,128)}, s32[1,128]{1,0:T(1,128)}) custom-call(s32[1,128]{1,0:T(1,128)} %bitcast.31), custom_call_target="tpu_custom_call" | custom-call | tf_op jit(solution)/shard_map/ask/pallas_call | solution.py:306
  2.3 11.6 %all-to-all-start = ((s32[64,1,128]{2,1,0:T(1,128)}), s32[64,1,128]{2,1,0:T(1,128)S(1)}, u32[]{:S(2)}, u32[]{:S(2)}) async-start(s32[64,1,128]{2,1,0:T(1,128)} %bitcast.29), calls=%async_computation | async-start | bytes 65536 | tf_op jit(solution)/shard_map/all_to_all | solution.py:320
  13.9 0.7 iota_compare_fusion.4
  14.6 0.8 select_reduce_fusion.2
  15.3 0.2 fusion
  15.6 0.0 copy-start
  15.6 0.0 copy-start.1
  15.6 1.1 copy.16
  16.7 0.0 copy-done.4
  16.8 0.0 copy-done.6
  16.8 0.1 select_reduce_fusion.1
  16.9 0.0 copy-done.5
  16.9 0.1 fusion.2.bias_ref
  17.0 0.2 convert_reduce_fusion
  17.3 0.1 pad_maximum_fusion.queries_ref
  17.3 5.7 %all-to-all-done = s32[64,1,128]{2,1,0:T(1,128)S(1)} async-done(((s32[64,1,128]{2,1,0:T(1,128)}), s32[64,1,128]{2,1,0:T(1,128)S(1)}, u32[]{:S(2)}, u32[]{:S(2)}) %all-to-all-start) | async-done | bytes 32800 | tf_op jit(solution)/shard_map/all_to_all | solution.py:320
  23.1 0.1 copy.15
  23.2 0.1 select_reduce_fusion.source_ref
  23.3 0.0 copy-done
  23.3 0.0 copy-done.1
  23.3 2.5 %pick_tiles.1 = bf16[512,6,2,128]{3,2,1,0:T(2,128)(2,1)S(1)} custom-call(s32[64,1,3]{2,1,0:T(1,128)S(1)} %bitcast.21, bf16[128,2,1024]{2,1,0:T(2,128)(2,1)S(1)} %copy-done, bf16[128,2,1024]{2,1,0:T(2,128)(2,1)S(1)} %copy-done.1), custom_call_target="tpu_custom_call" | custom-call | tf_op jit(solution)/shard_map/pick_tiles/pallas_call | solution.py:330
  25.9 0.0 copy-start.2
  25.9 0.0 copy-start.3
  25.9 59.4 %all_to_all.15.recv_ref = bf16[512,6,2,128]{3,2,1,0:T(2,128)(2,1)S(1)} all-to-all(bf16[512,6,2,128]{3,2,1,0:T(2,128)(2,1)S(1)} %pick_tiles.1), channel_id=1, replica_groups=mesh['dp'=64,'tensor'=8] {'dp','tensor'}, dimensions={0} | all-to-all | bytes 3145728 | tf_op jit(solution)/shard_map/all_to_all | solution.py:338
  85.3 0.0 copy-done.2
  85.3 0.0 copy-done.3
  85.3 8.6 %attend_backward.1 = (bf16[512,6,2,128]{3,2,1,0:T(2,128)(2,1)S(1)}, bf16[128,1024]{1,0:T(8,128)(2,1)}) custom-call(s32[128]{0:T(128)S(1)} %bitcast.23, s32[128]{0:T(128)S(1)} %bitcast.22, s32[4]{0:T(128)S(1)} %get-tuple-element.24.first_ref, s32[4]{0:T(128)S(1)} %and_select_fusion.steps_ref, f32[128,128]{1,0:T(8,128)S(1)} %fusion.2.bias_ref, ...), custom_call_target="tpu_custom_call" | custom-call | tf_op jit(solution)/shard_map/attend_backward/pallas_call | solution.py:270
  93.9 54.3 %all_to_all.16.home_ref = bf16[512,6,2,128]{3,2,1,0:T(2,128)(2,1)S(1)} all-to-all(bf16[512,6,2,128]{3,2,1,0:T(2,128)(2,1)S(1)} %get-tuple-element.32), channel_id=1, replica_groups=mesh['dp'=64,'tensor'=8] {'dp','tensor'}, dimensions={0} | all-to-all | bytes 3145728 | tf_op jit(solution)/shard_map/all_to_all | solution.py:342
  148.3 2.3 %place_tiles.1 = (bf16[128,2,1024]{2,1,0:T(2,128)(2,1)}, bf16[128,2,1024]{2,1,0:T(2,128)(2,1)}) custom-call(s32[128]{0:T(128)S(1)} %select_reduce_fusion.source_ref, bf16[512,6,2,128]{3,2,1,0:T(2,128)(2,1)S(1)} %all_to_all.16.home_ref), custom_call_target="tpu_custom_call" | custom-call | tf_op jit(solution)/shard_map/place_tiles/pallas_call | solution.py:343
  (9 shorter events, 0.2 us)
Async XLA Ops:
  0.6 16.2 %copy-start.6 = (s32[8]{0:T(128)S(1)}, s32[8]{0:T(128)}, u32[]{:S(2)}) copy-start(s32[8]{0:T(128)} %param.15) | copy-start | bytes 100
  0.6 16.1 %copy-start.4 = (bf16[128,1024]{1,0:T(8,128)(2,1)S(1)}, bf16[128,1024]{1,0:T(8,128)(2,1)}, u32[]{:S(2)}) copy-start(bf16[128,1024]{1,0:T(8,128)(2,1)} %param.11) | copy-start | bytes 786436
  0.7 16.3 %copy-start.5 = (s32[128]{0:T(128)S(1)}, s32[128]{0:T(128)}, u32[]{:S(2)}) copy-start(s32[128]{0:T(128)} %param.14) | copy-start | bytes 1540
  2.3 20.8 %all-to-all-start = ((s32[64,1,128]{2,1,0:T(1,128)}), s32[64,1,128]{2,1,0:T(1,128)S(1)}, u32[]{:S(2)}, u32[]{:S(2)}) async-start(s32[64,1,128]{2,1,0:T(1,128)} %bitcast.29), calls=%async_computation | async-start | bytes 65536 | tf_op jit(solution)/shard_map/all_to_all | solution.py:320
  15.6 7.8 %copy-start = (bf16[128,2,1024]{2,1,0:T(2,128)(2,1)S(1)}, bf16[128,2,1024]{2,1,0:T(2,128)(2,1)}, u32[]{:S(2)}) copy-start(bf16[128,2,1024]{2,1,0:T(2,128)(2,1)} %keys_ref.1) | copy-start | bytes 1572868
  15.6 7.8 %copy-start.1 = (bf16[128,2,1024]{2,1,0:T(2,128)(2,1)S(1)}, bf16[128,2,1024]{2,1,0:T(2,128)(2,1)}, u32[]{:S(2)}) copy-start(bf16[128,2,1024]{2,1,0:T(2,128)(2,1)} %values_ref.1) | copy-start | bytes 1572868
  25.9 59.4 %copy-start.2 = (s32[1,128]{1,0:T(1,128)S(1)}, s32[1,128]{1,0:T(1,128)}, u32[]{:S(2)}) copy-start(s32[1,128]{1,0:T(1,128)} %get-tuple-element.21) | copy-start | bytes 1540
  25.9 59.4 %copy-start.3 = (s32[1,128]{1,0:T(1,128)S(1)}, s32[1,128]{1,0:T(1,128)}, u32[]{:S(2)}) copy-start(s32[1,128]{1,0:T(1,128)} %get-tuple-element.20) | copy-start | bytes 1540

commit v9 on v8

--- a/solution.py
+++ b/solution.py
@@ -43,16 +43,25 @@
 def pick_tiles(wanted_ref, keys_ref, values_ref, send_ref):
     readers, _, capacity = wanted_ref.shape
     heads = keys_ref.shape[2] // HD
-    def one_reader(reader, carry):
-        for rank in range(capacity):
-            tile = jnp.maximum(wanted_ref[reader, 0, rank], 0)
-            for head in range(heads):
-                cols = slice(head * HD, (head + 1) * HD)
-                send_ref[reader * heads + head, rank] = keys_ref[tile, :, cols]
-                send_ref[reader * heads + head, capacity + rank] = values_ref[tile, :, cols]
-        return carry
-
-    lax.fori_loop(0, readers, one_reader, 0, unroll=4)
+    def copy_tile(reader, rank):
+        tile = jnp.maximum(wanted_ref[reader, 0, rank], 0)
+        for head in range(heads):
+            cols = slice(head * HD, (head + 1) * HD)
+            send_ref[reader * heads + head, rank] = keys_ref[tile, :, cols]
+            send_ref[reader * heads + head, capacity + rank] = values_ref[tile, :, cols]
+
+    def first_tiles(reader, carry):
+        for rank in range(capacity - 1):
+            copy_tile(reader, rank)
+        return carry
+
+    def last_tile(reader, carry):
+        rank = capacity - 1
+        pl.when(wanted_ref[reader, 0, rank] >= 0)(functools.partial(copy_tile, reader, rank))
+        return carry
+
+    lax.fori_loop(0, readers, first_tiles, 0, unroll=4)
+    lax.fori_loop(0, readers, last_tile, 0, unroll=8)
 
 
 def place_tiles(

time: 151 us -> 151 us (level)
  no operation moved by 1% of the time
where the time goes in v9:
time: 151 us
  blocking collectives  113 us (75%)
  Pallas kernels  16.4 us (11%)
  starting transfers between devices  11.6 us (8%)
  waiting for transfers between devices  5.75 us (4%)
  other arithmetic  2.25 us (1%)
    all_to_all x1, blocking collectives, per_device(): lax.all_to_all(send, ('dp', 'tensor'), split_axis=0, concat_axis=0, tiled...  59.4 us
    all_to_all x1, blocking collectives, per_device(): lax.all_to_all(back, ('dp', 'tensor'), split_axis=0, concat_axis=0, tiled...  53.6 us
    all_to_all x1, starting transfers between devices, per_device(): lax.all_to_all(asked, 'dp', split_axis=0, concat_axis=0, tiled=True)  11.6 us
    pallas_call x1, Pallas kernels, attention(): pl.pallas_call(attend_backward, out_shape=(jax.ShapeDtypeStruct(recv.shap...  9.77 us
    all_to_all x1, waiting for transfers between devices, per_device(): lax.all_to_all(asked, 'dp', split_axis=0, concat_axis=0, tiled=True)  5.75 us
  transfers between devices with their start and end apart: 1, of which 1 were waited for; matrix products, arithmetic and copies ran while one was open for 2% of the time, Pallas kernels for 0%

profile of v9, /device:TPU:1, one launch (start us, length us, event | category | flops | bytes accessed | tf_op | source)
XLA Modules:
  0.0 151.2 jit_solution(14466670606780694844)
XLA Ops:
  0.6 0.0 copy-start.6
  0.6 0.0 copy-start.4
  0.7 0.0 copy-start.5
  0.7 1.6 %ask.1 = (s32[64,128]{1,0:T(8,128)}, s32[1,128]{1,0:T(1,128)}, s32[1,128]{1,0:T(1,128)}) custom-call(s32[1,128]{1,0:T(1,128)} %bitcast.31), custom_call_target="tpu_custom_call" | custom-call | tf_op jit(solution)/shard_map/ask/pallas_call | solution.py:315
  2.3 11.6 %all-to-all-start = ((s32[64,1,128]{2,1,0:T(1,128)}), s32[64,1,128]{2,1,0:T(1,128)S(1)}, u32[]{:S(2)}, u32[]{:S(2)}) async-start(s32[64,1,128]{2,1,0:T(1,128)} %bitcast.29), calls=%async_computation | async-start | bytes 65536 | tf_op jit(solution)/shard_map/all_to_all | solution.py:329
  13.9 0.7 iota_compare_fusion.4
  14.6 0.8 select_reduce_fusion.2
  15.3 0.2 fusion
  15.6 0.0 copy-start
  15.6 0.0 copy-start.1
  15.6 1.1 copy.16
  16.7 0.0 copy-done.4
  16.8 0.0 copy-done.6
  16.8 0.1 select_reduce_fusion.1
  16.9 0.0 copy-done.5
  16.9 0.1 fusion.2.bias_ref
  17.0 0.2 convert_reduce_fusion
  17.3 0.1 pad_maximum_fusion.queries_ref
  17.3 5.7 %all-to-all-done = s32[64,1,128]{2,1,0:T(1,128)S(1)} async-done(((s32[64,1,128]{2,1,0:T(1,128)}), s32[64,1,128]{2,1,0:T(1,128)S(1)}, u32[]{:S(2)}, u32[]{:S(2)}) %all-to-all-start) | async-done | bytes 32800 | tf_op jit(solution)/shard_map/all_to_all | solution.py:329
  23.1 0.1 copy.15
  23.2 0.1 select_reduce_fusion.source_ref
  23.3 0.0 copy-done
  23.3 0.0 copy-done.1
  23.3 2.7 %pick_tiles.1 = bf16[512,6,2,128]{3,2,1,0:T(2,128)(2,1)S(1)} custom-call(s32[64,1,3]{2,1,0:T(1,128)S(1)} %bitcast.21, bf16[128,2,1024]{2,1,0:T(2,128)(2,1)S(1)} %copy-done, bf16[128,2,1024]{2,1,0:T(2,128)(2,1)S(1)} %copy-done.1), custom_call_target="tpu_custom_call" | custom-call | tf_op jit(solution)/shard_map/pick_tiles/pallas_call | solution.py:339
  26.0 0.0 copy-start.2
  26.1 0.0 copy-start.3
  26.1 59.4 %all_to_all.15.recv_ref = bf16[512,6,2,128]{3,2,1,0:T(2,128)(2,1)S(1)} all-to-all(bf16[512,6,2,128]{3,2,1,0:T(2,128)(2,1)S(1)} %pick_tiles.1), channel_id=1, replica_groups=mesh['dp'=64,'tensor'=8] {'dp','tensor'}, dimensions={0} | all-to-all | bytes 3145728 | tf_op jit(solution)/shard_map/all_to_all | solution.py:347
  85.5 0.0 copy-done.2
  85.5 0.0 copy-done.3
  85.5 9.8 %attend_backward.1 = (bf16[512,6,2,128]{3,2,1,0:T(2,128)(2,1)S(1)}, bf16[128,1024]{1,0:T(8,128)(2,1)}) custom-call(s32[128]{0:T(128)S(1)} %bitcast.23, s32[128]{0:T(128)S(1)} %bitcast.22, s32[4]{0:T(128)S(1)} %get-tuple-element.24.first_ref, s32[4]{0:T(128)S(1)} %and_select_fusion.steps_ref, f32[128,128]{1,0:T(8,128)S(1)} %fusion.2.bias_ref, ...), custom_call_target="tpu_custom_call" | custom-call | tf_op jit(solution)/shard_map/attend_backward/pallas_call | solution.py:279
  95.3 53.6 %all_to_all.16.home_ref = bf16[512,6,2,128]{3,2,1,0:T(2,128)(2,1)S(1)} all-to-all(bf16[512,6,2,128]{3,2,1,0:T(2,128)(2,1)S(1)} %get-tuple-element.32), channel_id=1, replica_groups=mesh['dp'=64,'tensor'=8] {'dp','tensor'}, dimensions={0} | all-to-all | bytes 3145728 | tf_op jit(solution)/shard_map/all_to_all | solution.py:351
  148.9 2.3 %place_tiles.1 = (bf16[128,2,1024]{2,1,0:T(2,128)(2,1)}, bf16[128,2,1024]{2,1,0:T(2,128)(2,1)}) custom-call(s32[128]{0:T(128)S(1)} %select_reduce_fusion.source_ref, bf16[512,6,2,128]{3,2,1,0:T(2,128)(2,1)S(1)} %all_to_all.16.home_ref), custom_call_target="tpu_custom_call" | custom-call | tf_op jit(solution)/shard_map/place_tiles/pallas_call | solution.py:352
  (9 shorter events, 0.2 us)
Async XLA Ops:
  0.6 16.2 %copy-start.6 = (s32[8]{0:T(128)S(1)}, s32[8]{0:T(128)}, u32[]{:S(2)}) copy-start(s32[8]{0:T(128)} %param.15) | copy-start | bytes 100
  0.6 16.1 %copy-start.4 = (bf16[128,1024]{1,0:T(8,128)(2,1)S(1)}, bf16[128,1024]{1,0:T(8,128)(2,1)}, u32[]{:S(2)}) copy-start(bf16[128,1024]{1,0:T(8,128)(2,1)} %param.11) | copy-start | bytes 786436
  0.7 16.3 %copy-start.5 = (s32[128]{0:T(128)S(1)}, s32[128]{0:T(128)}, u32[]{:S(2)}) copy-start(s32[128]{0:T(128)} %param.14) | copy-start | bytes 1540
  2.3 20.8 %all-to-all-start = ((s32[64,1,128]{2,1,0:T(1,128)}), s32[64,1,128]{2,1,0:T(1,128)S(1)}, u32[]{:S(2)}, u32[]{:S(2)}) async-start(s32[64,1,128]{2,1,0:T(1,128)} %bitcast.29), calls=%async_computation | async-start | bytes 65536 | tf_op jit(solution)/shard_map/all_to_all | solution.py:329
  15.6 7.8 %copy-start = (bf16[128,2,1024]{2,1,0:T(2,128)(2,1)S(1)}, bf16[128,2,1024]{2,1,0:T(2,128)(2,1)}, u32[]{:S(2)}) copy-start(bf16[128,2,1024]{2,1,0:T(2,128)(2,1)} %keys_ref.1) | copy-start | bytes 1572868
  15.6 7.8 %copy-start.1 = (bf16[128,2,1024]{2,1,0:T(2,128)(2,1)S(1)}, bf16[128,2,1024]{2,1,0:T(2,128)(2,1)}, u32[]{:S(2)}) copy-start(bf16[128,2,1024]{2,1,0:T(2,128)(2,1)} %values_ref.1) | copy-start | bytes 1572868
  26.0 59.4 %copy-start.2 = (s32[1,128]{1,0:T(1,128)S(1)}, s32[1,128]{1,0:T(1,128)}, u32[]{:S(2)}) copy-start(s32[1,128]{1,0:T(1,128)} %get-tuple-element.21) | copy-start | bytes 1540
  26.1 59.4 %copy-start.3 = (s32[1,128]{1,0:T(1,128)S(1)}, s32[1,128]{1,0:T(1,128)}, u32[]{:S(2)}) copy-start(s32[1,128]{1,0:T(1,128)} %get-tuple-element.20) | copy-start | bytes 1540

commit v10 on v8

--- a/solution.py
+++ b/solution.py
@@ -52,7 +52,7 @@
                 send_ref[reader * heads + head, capacity + rank] = values_ref[tile, :, cols]
         return carry
 
-    lax.fori_loop(0, readers, one_reader, 0, unroll=4)
+    lax.fori_loop(0, readers, one_reader, 0, unroll=8)
 
 
 def place_tiles(
@@ -138,7 +138,7 @@
         grad_value_scr[target, :] = jnp.zeros((tile_len, HD), F32)
         return carry
 
-    lax.fori_loop(0, slots, gather_slot, 0, unroll=8)
+    lax.fori_loop(0, slots, gather_slot, 0, unroll=16)
     key_scr[tail, :HD] = jnp.zeros((tail.size, HD), BF16)
     key_scr[tail, HD:] = jnp.full((tail.size, HD), HIDDEN, BF16)
     value_scr[tail, :] = jnp.zeros((tail.size, HD), BF16)
@@ -221,7 +221,7 @@
         back_ref[source, capacity + rank] = grad_value_scr[where, :].astype(BF16).reshape(shape)
         return carry
 
-    lax.fori_loop(0, slots, return_slot, 0, unroll=8)
+    lax.fori_loop(0, slots, return_slot, 0, unroll=16)
     for index in range(blocks):
         store_queries(index).wait()
 

time: 151 us -> 150 us (level)
  no operation moved by 1% of the time
where the time goes in v10:
time: 150 us
  blocking collectives  114 us (76%)
  Pallas kernels  14.8 us (10%)
  starting transfers between devices  11.6 us (8%)
  waiting for transfers between devices  5.75 us (4%)
  other arithmetic  2.25 us (2%)
    all_to_all x1, blocking collectives, per_device(): lax.all_to_all(send, ('dp', 'tensor'), split_axis=0, concat_axis=0, tiled...  59.4 us
    all_to_all x1, blocking collectives, per_device(): lax.all_to_all(back, ('dp', 'tensor'), split_axis=0, concat_axis=0, tiled...  54.1 us
    all_to_all x1, starting transfers between devices, per_device(): lax.all_to_all(asked, 'dp', split_axis=0, concat_axis=0, tiled=True)  11.6 us
    pallas_call x1, Pallas kernels, attention(): pl.pallas_call(attend_backward, out_shape=(jax.ShapeDtypeStruct(recv.shap...  8.46 us
    all_to_all x1, waiting for transfers between devices, per_device(): lax.all_to_all(asked, 'dp', split_axis=0, concat_axis=0, tiled=True)  5.75 us
  transfers between devices with their start and end apart: 1, of which 1 were waited for; matrix products, arithmetic and copies ran while one was open for 2% of the time, Pallas kernels for 0%

profile of v10, /device:TPU:1, one launch (start us, length us, event | category | flops | bytes accessed | tf_op | source)
XLA Modules:
  0.0 150.1 jit_solution(14354876658809394497)
XLA Ops:
  0.6 0.0 copy-start.6
  0.6 0.0 copy-start.4
  0.7 0.0 copy-start.5
  0.7 1.6 %ask.1 = (s32[64,128]{1,0:T(8,128)}, s32[1,128]{1,0:T(1,128)}, s32[1,128]{1,0:T(1,128)}) custom-call(s32[1,128]{1,0:T(1,128)} %bitcast.31), custom_call_target="tpu_custom_call" | custom-call | tf_op jit(solution)/shard_map/ask/pallas_call | solution.py:306
  2.3 11.6 %all-to-all-start = ((s32[64,1,128]{2,1,0:T(1,128)}), s32[64,1,128]{2,1,0:T(1,128)S(1)}, u32[]{:S(2)}, u32[]{:S(2)}) async-start(s32[64,1,128]{2,1,0:T(1,128)} %bitcast.29), calls=%async_computation | async-start | bytes 65536 | tf_op jit(solution)/shard_map/all_to_all | solution.py:320
  13.9 0.7 iota_compare_fusion.4
  14.6 0.8 select_reduce_fusion.2
  15.3 0.2 fusion
  15.6 0.0 copy-start
  15.6 0.0 copy-start.1
  15.6 1.1 copy.16
  16.7 0.0 copy-done.4
  16.8 0.0 copy-done.6
  16.8 0.1 select_reduce_fusion.1
  16.9 0.0 copy-done.5
  16.9 0.1 fusion.2.bias_ref
  17.0 0.2 convert_reduce_fusion
  17.3 0.1 pad_maximum_fusion.queries_ref
  17.3 5.7 %all-to-all-done = s32[64,1,128]{2,1,0:T(1,128)S(1)} async-done(((s32[64,1,128]{2,1,0:T(1,128)}), s32[64,1,128]{2,1,0:T(1,128)S(1)}, u32[]{:S(2)}, u32[]{:S(2)}) %all-to-all-start) | async-done | bytes 32800 | tf_op jit(solution)/shard_map/all_to_all | solution.py:320
  23.1 0.1 copy.15
  23.2 0.1 select_reduce_fusion.source_ref
  23.3 0.0 copy-done
  23.3 0.0 copy-done.1
  23.3 2.4 %pick_tiles.1 = bf16[512,6,2,128]{3,2,1,0:T(2,128)(2,1)S(1)} custom-call(s32[64,1,3]{2,1,0:T(1,128)S(1)} %bitcast.21, bf16[128,2,1024]{2,1,0:T(2,128)(2,1)S(1)} %copy-done, bf16[128,2,1024]{2,1,0:T(2,128)(2,1)S(1)} %copy-done.1), custom_call_target="tpu_custom_call" | custom-call | tf_op jit(solution)/shard_map/pick_tiles/pallas_call | solution.py:330
  25.8 0.0 copy-start.2
  25.8 0.0 copy-start.3
  25.8 59.4 %all_to_all.15.recv_ref = bf16[512,6,2,128]{3,2,1,0:T(2,128)(2,1)S(1)} all-to-all(bf16[512,6,2,128]{3,2,1,0:T(2,128)(2,1)S(1)} %pick_tiles.1), channel_id=1, replica_groups=mesh['dp'=64,'tensor'=8] {'dp','tensor'}, dimensions={0} | all-to-all | bytes 3145728 | tf_op jit(solution)/shard_map/all_to_all | solution.py:338
  85.2 0.0 copy-done.2
  85.2 0.0 copy-done.3
  85.2 8.5 %attend_backward.1 = (bf16[512,6,2,128]{3,2,1,0:T(2,128)(2,1)S(1)}, bf16[128,1024]{1,0:T(8,128)(2,1)}) custom-call(s32[128]{0:T(128)S(1)} %bitcast.23, s32[128]{0:T(128)S(1)} %bitcast.22, s32[4]{0:T(128)S(1)} %get-tuple-element.24.first_ref, s32[4]{0:T(128)S(1)} %and_select_fusion.steps_ref, f32[128,128]{1,0:T(8,128)S(1)} %fusion.2.bias_ref, ...), custom_call_target="tpu_custom_call" | custom-call | tf_op jit(solution)/shard_map/attend_backward/pallas_call | solution.py:270
  93.7 54.1 %all_to_all.16.home_ref = bf16[512,6,2,128]{3,2,1,0:T(2,128)(2,1)S(1)} all-to-all(bf16[512,6,2,128]{3,2,1,0:T(2,128)(2,1)S(1)} %get-tuple-element.32), channel_id=1, replica_groups=mesh['dp'=64,'tensor'=8] {'dp','tensor'}, dimensions={0} | all-to-all | bytes 3145728 | tf_op jit(solution)/shard_map/all_to_all | solution.py:342
  147.8 2.3 %place_tiles.1 = (bf16[128,2,1024]{2,1,0:T(2,128)(2,1)}, bf16[128,2,1024]{2,1,0:T(2,128)(2,1)}) custom-call(s32[128]{0:T(128)S(1)} %select_reduce_fusion.source_ref, bf16[512,6,2,128]{3,2,1,0:T(2,128)(2,1)S(1)} %all_to_all.16.home_ref), custom_call_target="tpu_custom_call" | custom-call | tf_op jit(solution)/shard_map/place_tiles/pallas_call | solution.py:343
  (9 shorter events, 0.2 us)
Async XLA Ops:
  0.6 16.2 %copy-start.6 = (s32[8]{0:T(128)S(1)}, s32[8]{0:T(128)}, u32[]{:S(2)}) copy-start(s32[8]{0:T(128)} %param.15) | copy-start | bytes 100
  0.6 16.1 %copy-start.4 = (bf16[128,1024]{1,0:T(8,128)(2,1)S(1)}, bf16[128,1024]{1,0:T(8,128)(2,1)}, u32[]{:S(2)}) copy-start(bf16[128,1024]{1,0:T(8,128)(2,1)} %param.11) | copy-start | bytes 786436
  0.7 16.3 %copy-start.5 = (s32[128]{0:T(128)S(1)}, s32[128]{0:T(128)}, u32[]{:S(2)}) copy-start(s32[128]{0:T(128)} %param.14) | copy-start | bytes 1540
  2.3 20.8 %all-to-all-start = ((s32[64,1,128]{2,1,0:T(1,128)}), s32[64,1,128]{2,1,0:T(1,128)S(1)}, u32[]{:S(2)}, u32[]{:S(2)}) async-start(s32[64,1,128]{2,1,0:T(1,128)} %bitcast.29), calls=%async_computation | async-start | bytes 65536 | tf_op jit(solution)/shard_map/all_to_all | solution.py:320
  15.6 7.8 %copy-start = (bf16[128,2,1024]{2,1,0:T(2,128)(2,1)S(1)}, bf16[128,2,1024]{2,1,0:T(2,128)(2,1)}, u32[]{:S(2)}) copy-start(bf16[128,2,1024]{2,1,0:T(2,128)(2,1)} %keys_ref.1) | copy-start | bytes 1572868
  15.6 7.8 %copy-start.1 = (bf16[128,2,1024]{2,1,0:T(2,128)(2,1)S(1)}, bf16[128,2,1024]{2,1,0:T(2,128)(2,1)}, u32[]{:S(2)}) copy-start(bf16[128,2,1024]{2,1,0:T(2,128)(2,1)} %values_ref.1) | copy-start | bytes 1572868
  25.8 59.4 %copy-start.2 = (s32[1,128]{1,0:T(1,128)S(1)}, s32[1,128]{1,0:T(1,128)}, u32[]{:S(2)}) copy-start(s32[1,128]{1,0:T(1,128)} %get-tuple-element.21) | copy-start | bytes 1540
  25.8 59.4 %copy-start.3 = (s32[1,128]{1,0:T(1,128)S(1)}, s32[1,128]{1,0:T(1,128)}, u32[]{:S(2)}) copy-start(s32[1,128]{1,0:T(1,128)} %get-tuple-element.20) | copy-start | bytes 1540
